TPU v7x, 128 devices: a whole 4x4x4 slice. The times are simulated.
128 devices in a mesh: var: 32 (over z, y, core), lat: 2 (over x_lo), lon: 2 (over x_hi).
Axes of the slice: x: 4 (x_hi: 2, x_lo: 2; x = x_hi * 2 + x_lo), y: 4, z: 4, core: 2. Of those that a mesh axis runs over, the one named last changes fastest.
Arguments:
- pixels: bfloat16 [32, 24, 64, 4, 384], P(None, 'lat', 'var', None, 'lon'), may hold values from -6 to 6
- var_order: int32 [64], replicated, may hold values from 0 to 63, each once
- embed_weight: bfloat16 [64, 16, 512], P('var'), may hold values from -0.1875 to 0.1875
- level_mix: float32 [64, 2], replicated, may hold values from -3 to 3
- norm_gain: float32 [512], replicated, may hold values from 0.5 to 1.5
- w_qkv: bfloat16 [512, 1536], replicated, may hold values from -4 to 4
- w_proj: bfloat16 [512, 512], replicated, may hold values from -0.25 to 0.25
- mask_ids: int32 [768, 2, 96], P(('var', 'lat'), None, 'lon'), may hold values from 0 to 2
- cotangent: bfloat16 [768, 2, 96, 512], P(('var', 'lat'), None, 'lon'), may hold values from -0.015625 to 0.015625
Outputs:
- block_out: bfloat16 [768, 2, 96, 512], P(('var', 'lat'), None, 'lon')
- grad_embed: float32 [64, 16, 512], P('var')
- grad_qkv: float32 [512, 1536], replicated
- grad_proj: float32 [512, 512], replicated
All inputs are finite; a program needn't handle non-finite values.
Results may differ from a plain program's by a relative error of at most 0.023.
Values may be sent and summed in bfloat16 or wider, within the bound.
No kernel may reach another device: no remote copies, remote signals or barrier semaphores. Data moves between devices by JAX's collectives and lax.ppermute only.
A program may use at most 128 MiB of HBM per device.

v0:
```python
import math

import jax
import jax.numpy as jnp
from jax import lax
from jax.sharding import PartitionSpec as P

D = 512
HEADS = 8
HDIM = 64
PSIDE = 4
WCOL = 6


epsilon = 1e-05


def from_behind(array, axis, by):
    count = lax.axis_size(axis)
    return lax.ppermute(array, axis, [(i, (i + by) % count) for i in range(count)])


def to_windows(tensor):
    row_count, level_count, col_count, features = tensor.shape
    window_count = col_count // WCOL
    parts = tensor.reshape(row_count, level_count, window_count, WCOL, features)
    return parts.transpose(2, 0, 1, 3, 4).reshape(
        window_count, row_count * level_count * WCOL, features
    )


def from_windows(tensor, row_count, level_count):
    window_count, token_count, features = tensor.shape
    parts = tensor.reshape(window_count, row_count, level_count, WCOL, features)
    return parts.transpose(1, 2, 0, 3, 4).reshape(
        row_count, level_count, window_count * WCOL, features
    )


def split_heads(windows):
    window_count, token_count = windows.shape[:2]
    parts = windows.reshape(window_count, token_count, 3, HEADS, HDIM)
    return (parts[:, :, 0], parts[:, :, 1], parts[:, :, 2])


def window_probs(query_rows, key_rows, region_ids):
    scores = jnp.einsum("wqhe,wkhe->whqk", query_rows, key_rows, preferred_element_type=jnp.float32)
    scores = scores * (1.0 / math.sqrt(HDIM))
    same_region = region_ids[:, None, :, None] == region_ids[:, None, None, :]
    scores = jnp.where(same_region, scores, -1e30)
    row_max = jnp.max(scores, axis=-1, keepdims=True)
    exponent = jnp.exp(scores - row_max)
    return exponent / jnp.sum(exponent, axis=-1, keepdims=True)


def layer_norm(tensor, gain):
    values = tensor.astype(jnp.float32)
    average = jnp.mean(values, axis=-1, keepdims=True)
    centred = values - average
    inverse_std = lax.rsqrt(jnp.mean(centred * centred, axis=-1, keepdims=True) + epsilon)
    unit_values = centred * inverse_std
    return ((unit_values * gain).astype(jnp.bfloat16), unit_values, inverse_std)


def norm_back(grad_normed, unit_values, inverse_std, gain):
    scaled = grad_normed * gain
    return inverse_std * (
        scaled
        - jnp.mean(scaled, axis=-1, keepdims=True)
        - unit_values * jnp.mean(scaled * unit_values, axis=-1, keepdims=True)
    )


def roll_forward(tensor):
    half_rows = tensor.shape[0] // 2
    half_cols = WCOL // 2
    from_next = from_behind(tensor[:half_rows], ("var", "lat"), -1)
    row_moved = jnp.concatenate([tensor[half_rows:], from_next], axis=0)
    from_east = from_behind(row_moved[:, :, :half_cols], "lon", -1)
    return jnp.concatenate([row_moved[:, :, half_cols:], from_east], axis=2)


def roll_back(tensor):
    row_count = tensor.shape[0]
    col_count = tensor.shape[2]
    half_rows = row_count // 2
    half_cols = WCOL // 2
    from_before = from_behind(tensor[row_count - half_rows :], ("var", "lat"), 1)
    row_moved = jnp.concatenate([from_before, tensor[: row_count - half_rows]], axis=0)
    from_west = from_behind(row_moved[:, :, col_count - half_cols :], "lon", 1)
    return jnp.concatenate([from_west, row_moved[:, :, : col_count - half_cols]], axis=2)


def per_device(
    pixels, var_order, embed_weight, level_mix, norm_gain, w_qkv, w_proj, mask_ids, cotangent
):
    channels = var_order.shape[0]
    every_weight = lax.all_gather(embed_weight, "var", axis=0, tiled=True)
    slot_weight = every_weight[var_order].reshape(channels, PSIDE, PSIDE, D)
    slot_mix = level_mix[var_order]
    level_weight = (
        slot_mix.T[:, :, None, None, None] * slot_weight[None].astype(jnp.float32)
    ).astype(jnp.bfloat16)
    received = lax.all_to_all(pixels, "var", split_axis=0, concat_axis=2, tiled=True)
    row_count = received.shape[1]
    col_count = received.shape[4] // PSIDE
    grid = received[0].reshape(row_count, channels, PSIDE, col_count, PSIDE)
    arrived = (
        jnp.einsum(
            "rsacb,lsabd->rlcd", grid, level_weight, preferred_element_type=jnp.float32
        ).astype(jnp.bfloat16),
        grid,
    )
    tokens, patch_grid = arrived
    level_count = tokens.shape[1]
    shifted = roll_forward(tokens)
    grad_branch = None
    row_count, level_count, col_count = shifted.shape[:3]
    normed, unit_values, inverse_std = layer_norm(shifted, norm_gain)
    normed_flat = normed.reshape(-1, D)
    projected = jnp.dot(normed_flat, w_qkv, preferred_element_type=jnp.float32).astype(jnp.bfloat16)
    windows = to_windows(projected.reshape(row_count, level_count, col_count, 3 * D))
    window_count, token_count = windows.shape[:2]
    query_rows, key_rows, value_rows = split_heads(windows)
    region_ids = to_windows(mask_ids[..., None])[..., 0]
    attention = window_probs(query_rows, key_rows, region_ids)
    rounded_probs = attention.astype(jnp.bfloat16)
    attended_win = jnp.einsum(
        "whqk,wkhe->wqhe", rounded_probs, value_rows, preferred_element_type=jnp.float32
    ).astype(jnp.bfloat16)
    attended = from_windows(
        attended_win.reshape(window_count, token_count, D), row_count, level_count
    )
    attended_flat = attended.reshape(-1, D)
    branch_out = jnp.dot(attended_flat, w_proj, preferred_element_type=jnp.float32).astype(
        jnp.bfloat16
    )
    branch_out = branch_out.reshape(row_count, level_count, col_count, D)
    block_out = (tokens.astype(jnp.float32) + roll_back(branch_out).astype(jnp.float32)).astype(
        jnp.bfloat16
    )
    grad_branch = roll_forward(cotangent)
    grad_branch_flat = grad_branch.reshape(-1, D)
    grad_proj_part = jnp.dot(attended_flat.T, grad_branch_flat, preferred_element_type=jnp.float32)
    grad_attended = jnp.dot(grad_branch_flat, w_proj.T, preferred_element_type=jnp.float32).astype(
        jnp.bfloat16
    )
    grad_out = to_windows(grad_attended.reshape(row_count, level_count, col_count, D))
    grad_out = grad_out.reshape(window_count, token_count, HEADS, HDIM)
    grad_value = jnp.einsum(
        "whqk,wqhe->wkhe", rounded_probs, grad_out, preferred_element_type=jnp.float32
    ).astype(jnp.bfloat16)
    grad_prob = jnp.einsum(
        "wqhe,wkhe->whqk", grad_out, value_rows, preferred_element_type=jnp.float32
    )
    centred = grad_prob - jnp.sum(attention * grad_prob, axis=-1, keepdims=True)
    grad_score = (attention * centred * (1.0 / math.sqrt(HDIM))).astype(jnp.bfloat16)
    grad_query = jnp.einsum(
        "whqk,wkhe->wqhe", grad_score, key_rows, preferred_element_type=jnp.float32
    ).astype(jnp.bfloat16)
    grad_key = jnp.einsum(
        "whqk,wqhe->wkhe", grad_score, query_rows, preferred_element_type=jnp.float32
    ).astype(jnp.bfloat16)
    grad_stacked = jnp.stack([grad_query, grad_key, grad_value], axis=2).reshape(
        window_count, token_count, 3 * D
    )
    grad_projected = from_windows(grad_stacked, row_count, level_count).reshape(-1, 3 * D)
    grad_qkv_part = jnp.dot(normed_flat.T, grad_projected, preferred_element_type=jnp.float32)
    grad_normed = jnp.dot(grad_projected, w_qkv.T, preferred_element_type=jnp.float32)
    grad_normed = grad_normed.reshape(row_count, level_count, col_count, D)
    grad_shifted = norm_back(grad_normed, unit_values, inverse_std, norm_gain).astype(jnp.bfloat16)
    grad_tokens = (
        cotangent.astype(jnp.float32) + roll_back(grad_shifted).astype(jnp.float32)
    ).astype(jnp.bfloat16)
    grad_level = jnp.einsum(
        "rsacb,rlcd->lsabd", patch_grid, grad_tokens, preferred_element_type=jnp.float32
    )
    grad_slot = jnp.sum(slot_mix.T[:, :, None, None, None] * grad_level, axis=0)
    grad_slot = grad_slot.reshape(channels, PSIDE * PSIDE, D)
    by_variable = jnp.zeros((channels, PSIDE * PSIDE, D), jnp.float32).at[var_order].set(grad_slot)
    grad_qkv, grad_proj = lax.psum((grad_qkv_part, grad_proj_part), ("var", "lat", "lon"))
    owner_part = lax.psum_scatter(
        by_variable.astype(jnp.bfloat16), "var", scatter_dimension=0, tiled=True
    )
    grad_embed = lax.psum(owner_part, ("lat", "lon")).astype(jnp.float32)
    return (block_out, grad_embed, grad_qkv, grad_proj)


def solution(mesh):
    in_specs = (
        P(None, "lat", "var", None, "lon"),
        P(),
        P("var", None, None),
        P(),
        P(),
        P(),
        P(),
        P(("var", "lat"), None, "lon"),
        P(("var", "lat"), None, "lon", None),
    )
    out_specs = (P(("var", "lat"), None, "lon", None), P("var", None, None), P(), P())
    return jax.shard_map(
        per_device, mesh=mesh, in_specs=in_specs, out_specs=out_specs, check_vma=False
    )
```

profile of v0, /device:TPU:1, one launch (start us, length us, event | category | flops | bytes accessed | tf_op | source)
XLA Modules:
  0.0 586.3 jit_solution(15339395349373335673)
XLA Ops:
  7.9 9.7 %all-to-all-start = ((bf16[32,12,2,4,192]{4,3,2,1,0:T(4,128)(2,1)}), bf16[32,12,2,4,192]{4,3,2,1,0:T(4,128)(2,1)S(1)}, u32[]{:S(2)}, u32[]{:S(2)}) async-start(bf16[32,12,2,4,192]{4,3,2,1,0:T(4,128)(2,1)} %param.9), calls=%async_computation | async-start | bytes 3145728 | tf_op jit(solution)/shard_map/all_to_all | solution.py:104
  17.7 2.4 fusion.84
  20.1 1.3 collective-permute-start.4
  23.7 16.7 %all-to-all-done = bf16[32,12,2,4,192]{4,3,2,1,0:T(4,128)(2,1)S(1)} async-done(((bf16[32,12,2,4,192]{4,3,2,1,0:T(4,128)(2,1)}), bf16[32,12,2,4,192]{4,3,2,1,0:T(4,128)(2,1)S(1)}, u32[]{:S(2)}, u32[]{:S(2)}) %all-to-all-start) | async-done | bytes 1179680 | tf_op jit(solution)/shard_map/all_to_all | solution.py:104
  40.4 9.5 %copy.66 = bf16[1,12,32,2,4,192]{1,5,4,3,2,0:T(8,128)(2,1)} copy(bf16[1,12,32,2,4,192]{5,4,3,1,2,0:T(4,128)(2,1)S(1)} %bitcast.144) | data formatting | bytes 2359296 | tf_op jit(solution)/shard_map/all_to_all | solution.py:104
  49.9 22.9 %copy.67 = bf16[12,64,4,48,4]{1,3,4,2,0:T(8,128)(2,1)} copy(bf16[12,64,4,48,4]{0,4,3,2,1:T(4,128)(2,1)} %bitcast.139) | data formatting | bytes 2359296 | tf_op jit(solution)/shard_map/reshape;squeeze | solution.py:107
  72.8 1.8 gather_fusion.1
  76.3 1.5 fusion.62
  78.9 5.3 collective-permute-start
  85.2 2.5 collective-permute-start.5
  87.7 1.4 slice_maximum_fusion
  89.1 8.3 %collective-permute-done.5 = bf16[12,2,3,512]{3,2,1,0:T(4,128)(2,1)S(1)} collective-permute-done((bf16[12,2,3,512]{3,2,1,0:T(4,128)(2,1)S(1)}, bf16[12,2,3,512]{3,2,1,0:T(4,128)(2,1)S(1)}, u32[]{:S(2)}, u32[]{:S(2)}) %collective-permute-start.5) | collective-permute-done | bytes 73760 | tf_op jit(solution)/shard_map/ppermute | solution.py:20
  98.6 1.8 convolution_convert_fusion.1
  100.4 2.2 reshape_reshape.28
  102.6 1.5 copy.84
  104.1 4.0 reshape_reshape.29
  108.2 4.9 copy.85
  114.8 1.4 slice_maximum_fusion.1
  116.1 3.1 collective-permute-done.1
  119.6 1.7 copy.68
  122.4 2.1 fusion.22
  124.5 3.8 convolution_convert_fusion
  128.3 6.6 %reshape_reshape.24 = bf16[12,2,8,6,1536]{4,3,2,1,0:T(8,128)(2,1)} reshape(bf16[1152,1536]{1,0:T(8,128)(2,1)} %convolution_convert_fusion) | data formatting | bytes 7077888 | tf_op jit(solution)/shard_map/reshape;reshape | solution.py:26
  134.9 5.5 copy.71
  140.4 9.6 %reshape_reshape.25 = bf16[8,144,3,8,64]{4,3,2,0,1:T(8,128)(2,1)} reshape(bf16[8,12,2,6,1536]{4,0,3,2,1:T(8,128)(2,1)} %copy.71) | data formatting | bytes 7077888 | tf_op jit(solution)/shard_map/reshape;reshape | solution.py:42
  149.9 6.9 %fusion.82 = (bf16[8,144,1,8,64]{4,3,2,0,1:T(8,128)(2,1)}, bf16[8,144,1,8,64]{4,3,2,0,1:T(8,128)(2,1)}, bf16[8,144,1,8,64]{4,3,2,0,1:T(8,128)(2,1)}) fusion(bf16[8,144,3,8,64]{4,3,2,0,1:T(8,128)(2,1)} %reshape_reshape.25), kind=kLoop, calls=%fused_computation.95 | loop fusion | bytes 7077888 | tf_op jit(solution)/shard_map/slice | solution.py:43
  156.8 4.8 copy.111
  161.6 4.8 copy.113
  166.3 4.7 copy.112
  171.1 3.7 fusion.32
  174.8 5.2 fusion.87
  180.0 7.8 %fusion.36 = f32[8,8,144,144]{2,3,1,0:T(8,128)} fusion(bf16[8,144,8,64]{1,3,2,0:T(8,128)(2,1)} %copy.85, bf16[8,144,1,8,64]{1,4,3,0,2:T(8,128)(2,1)} %copy.111), kind=kOutput, calls=%fused_computation.52 | convolution fusion | flops 169869312 | bytes 7667712 | tf_op jit(solution)/shard_map/wqhe,wkhe->whqk/dot_general | solution.py:153
  187.9 3.0 convert_bitcast_fusion
  190.9 16.9 %convert_bitcast_fusion.1 = bf16[8,144,1,8,64]{1,4,3,0,2:T(8,128)(2,1)} fusion(f32[8,8,144,144]{2,3,1,0:T(8,128)} %fusion.36, bf16[8,144,1,8,64]{1,4,3,0,2:T(8,128)(2,1)} %copy.112, f32[8,8,144,144]{2,3,1,0:T(8,128)} %get-tuple-element.34, f32[8,8,144]{2,1,0:T(8,128)S(1)} %get-tuple-element.33), kind=kOutput, calls=%fused_computation.56 | convolution fusion | flops 179758224 | bytes 13012992 | tf_op jit(solution)/shard_map/whqk,wqhe->wkhe/dot_general | solution.py:161
  207.8 16.8 %convert_bitcast_fusion.2 = bf16[8,144,1,8,64]{1,4,3,0,2:T(8,128)(2,1)} fusion(f32[8,8,144,144]{2,3,1,0:T(8,128)} %fusion.36, bf16[8,144,1,8,64]{1,4,3,0,2:T(8,128)(2,1)} %copy.113, f32[8,8,144,144]{2,3,1,0:T(8,128)} %get-tuple-element.34, f32[8,8,144]{2,1,0:T(8,128)S(1)} %get-tuple-element.33), kind=kOutput, calls=%fused_computation.57 | convolution fusion | flops 179758224 | bytes 13012992 | tf_op jit(solution)/shard_map/whqk,wkhe->wqhe/dot_general | solution.py:158
  224.7 6.9 %pad_maximum_fusion = bf16[8,144,3,8,64]{1,4,3,0,2:T(8,128)(2,1)} fusion(bf16[8,144,1,8,64]{1,4,3,0,2:T(8,128)(2,1)} %convert_bitcast_fusion, bf16[8,144,1,8,64]{1,4,3,0,2:T(8,128)(2,1)} %convert_bitcast_fusion.1, bf16[8,144,1,8,64]{1,4,3,0,2:T(8,128)(2,1)} %convert_bitcast_fusion.2), kind=kLoop, calls=%fused_computation.12 | loop fusion | flops 3538944 | bytes 7077888 | tf_op jit(solution)/shard_map/stack | solution.py:164
  231.5 12.0 %copy.90 = bf16[8,144,3,8,64]{4,3,2,0,1:T(8,128)(2,1)} copy(bf16[8,144,3,8,64]{1,4,3,0,2:T(8,128)(2,1)} %pad_maximum_fusion) | data formatting | bytes 7077888 | tf_op jit(solution)/shard_map/stack | solution.py:164
  243.6 10.3 %reshape_reshape.30 = bf16[8,12,2,6,1536]{4,0,3,2,1:T(8,128)(2,1)} reshape(bf16[8,144,3,8,64]{4,3,2,0,1:T(8,128)(2,1)} %copy.90) | data formatting | bytes 7077888 | tf_op jit(solution)/shard_map/reshape;reshape | solution.py:34
  253.9 5.6 copy.91
  259.6 2.3 multiply_reduce_fusion.3
  261.9 1.9 multiply_convert_fusion.2
  264.8 17.9 %collective-permute-done.6 = bf16[6,2,48,512]{3,2,0,1:T(8,128)(2,1)S(1)} collective-permute-done((bf16[6,2,48,512]{3,2,0,1:T(8,128)(2,1)S(1)}, bf16[6,2,48,512]{3,2,0,1:T(8,128)(2,1)S(1)}, u32[]{:S(2)}, u32[]{:S(2)}) %collective-permute-start.6) | collective-permute-done | bytes 589856 | tf_op jit(solution)/shard_map/ppermute | solution.py:20
  283.4 22.8 %copy.94 = bf16[12,64,4,48,4]{1,3,0,4,2:T(8,128)(2,1)} copy(bf16[12,64,4,48,4]{0,4,3,2,1:T(4,128)(2,1)} %bitcast.140) | data formatting | bytes 2359296 | tf_op jit(solution)/shard_map/reshape;squeeze | solution.py:107
  306.1 5.9 %copy.97 = bf16[12,2,8,6,1536]{4,3,2,1,0:T(8,128)(2,1)} copy(bf16[12,2,8,6,1536]{4,2,3,1,0:T(8,128)(2,1)} %bitcast.142) | data formatting | bytes 7077888 | tf_op jit(solution)/shard_map/transpose | solution.py:35
  312.0 1.9 fusion.15
  313.9 2.5 copy.95
  316.5 1.6 broadcast_in_dim.19
  318.0 9.9 %scatter_fusion = f32[64,16,512]{2,1,0:T(8,128)} fusion(f32[64,16,512]{2,1,0:T(8,128)} %broadcast_in_dim.19, s32[64]{0:T(128)S(1)} %compare_select_fusion, f32[64,16,512]{2,1,0:T(8,128)} %copy.95), kind=kCustom, calls=%fused_computation.2 | custom fusion | bytes 6291712 | tf_op jit(solution)/shard_map/scatter | solution.py:180
  328.0 2.7 convert_element_type.146
  330.8 6.6 %convert_bitcast_fusion.3 = bf16[8,144,8,64]{1,3,2,0:T(8,128)(2,1)} fusion(bf16[8,144,1,8,64]{1,4,3,0,2:T(8,128)(2,1)} %copy.111, f32[8,8,144,144]{2,3,1,0:T(8,128)} %get-tuple-element.34, f32[8,8,144]{2,1,0:T(8,128)S(1)} %get-tuple-element.33), kind=kOutput, calls=%fused_computation.58 | convolution fusion | flops 173113344 | bytes 7704576 | tf_op jit(solution)/shard_map/whqk,wkhe->wqhe/dot_general | solution.py:128
  337.3 4.9 copy.78
  342.2 4.2 reshape_reshape.26
  346.4 1.8 copy.79
  349.5 2.4 copy.96
  352.0 6.8 %reshape_reshape.31 = bf16[1152,1536]{1,0:T(8,128)(2,1)} reshape(bf16[12,2,8,6,1536]{4,3,2,1,0:T(8,128)(2,1)} %copy.97) | data formatting | bytes 7077888 | tf_op jit(solution)/shard_map/reshape;reshape | solution.py:167
  358.8 3.3 fusion.89
  362.1 5.2 fusion.88
  369.7 13.2 %collective-permute-done.2 = bf16[6,2,48,512]{3,2,0,1:T(8,128)(2,1)S(1)} collective-permute-done((bf16[6,2,48,512]{3,2,0,1:T(8,128)(2,1)S(1)}, bf16[6,2,48,512]{3,2,0,1:T(8,128)(2,1)S(1)}, u32[]{:S(2)}, u32[]{:S(2)}) %collective-permute-start.2) | collective-permute-done | bytes 589856 | tf_op jit(solution)/shard_map/ppermute | solution.py:20
  383.0 3.8 collective-permute-start.3
  386.8 2.3 collective-permute-done.3
  390.9 22.3 %reduce-scatter.2.cloned.1.call-done = bf16[2,16,512]{2,1,0:T(8,128)(2,1)} async-done(((bf16[64,16,512]{2,1,0:T(8,128)(2,1)}), bf16[2,16,512]{2,1,0:T(8,128)(2,1)}) %reduce-scatter.2.cloned.1.call-update) | async-done | bytes 32784 | tf_op jit(solution)/shard_map/reduce_scatter | solution.py:182
  413.1 14.6 %psum.21 = bf16[2,16,512]{2,1,0:T(8,128)(2,1)S(1)} all-reduce(bf16[2,16,512]{2,1,0:T(8,128)(2,1)} %reduce-scatter.2.cloned.1.call-done), channel_id=1, replica_groups=mesh['var'=32,'lat'=2,'lon'=2] {'lat','lon'}, use_global_device_ids=true, to_apply=%region_10.11 | all-reduce | flops 16384 | bytes 65536 | tf_op jit(solution)/shard_map/psum | solution.py:185
  428.4 146.3 %all-reduce.3.cloned.1.call-done = (f32[512,1536]{1,0:T(8,128)}, f32[512,512]{1,0:T(8,128)}) async-done(((f32[512,1536]{1,0:T(8,128)}, f32[512,512]{1,0:T(8,128)}), (f32[512,1536]{1,0:T(8,128)}, f32[512,512]{1,0:T(8,128)})) %all-reduce.3.cloned.1.call-update) | async-done | bytes 4194320 | tf_op jit(solution)/shard_map/psum | solution.py:181
  574.8 3.8 copy.127
  (95 shorter events, 19.9 us)
Async XLA Ops:
  7.2 117.3 %copy-start = (bf16[512,1536]{1,0:T(8,128)(2,1)S(1)}, bf16[512,1536]{1,0:T(8,128)(2,1)}, u32[]{:S(2)}) copy-start(bf16[512,1536]{1,0:T(8,128)(2,1)} %param.14) | copy-start | bytes 4718596
  7.2 65.6 %all-gather.2.cloned.1.call-start = ((), (), s32[]{:S(2)}) async-start(), calls=%async_computation.2 | async-start | bytes 1081344 | tf_op jit(solution)/shard_map/all_gather | solution.py:98
  7.9 13.6 %copy-start.17 = (f32[64,2]{0,1:T(2,128)S(1)}, f32[64,2]{0,1:T(2,128)}, u32[]{:S(2)}) copy-start(f32[64,2]{0,1:T(2,128)} %param.12) | copy-start | bytes 1540
  7.9 13.6 %copy-start.20 = (s32[64]{0:T(128)S(1)}, s32[64]{0:T(128)}, u32[]{:S(2)}) copy-start(s32[64]{0:T(128)} %param.10) | copy-start | bytes 772
  7.9 14.3 %copy-start.15 = (s32[12,2,48]{2,1,0:T(2,128)S(1)}, s32[12,2,48]{2,1,0:T(2,128)}, u32[]{:S(2)}) copy-start(s32[12,2,48]{2,1,0:T(2,128)} %param.16) | copy-start | bytes 13828
  7.9 32.5 %all-to-all-start = ((bf16[32,12,2,4,192]{4,3,2,1,0:T(4,128)(2,1)}), bf16[32,12,2,4,192]{4,3,2,1,0:T(4,128)(2,1)S(1)}, u32[]{:S(2)}, u32[]{:S(2)}) async-start(bf16[32,12,2,4,192]{4,3,2,1,0:T(4,128)(2,1)} %param.9), calls=%async_computation | async-start | bytes 3145728 | tf_op jit(solution)/shard_map/all_to_all | solution.py:104
  17.7 395.4 %reduce-scatter.2.cloned.1.call-start = ((), (), s32[]{:S(2)}) async-start(), calls=%async_computation.3 | async-start | bytes 1081344 | tf_op jit(solution)/shard_map/reduce_scatter | solution.py:182
  20.1 64.1 %collective-permute-start.4 = (bf16[6,2,48,512]{3,2,1,0:T(8,128)(2,1)}, bf16[6,2,48,512]{3,2,1,0:T(8,128)(2,1)}, u32[]{:S(2)}, u32[]{:S(2)}) collective-permute-start(bf16[6,2,48,512]{3,2,1,0:T(8,128)(2,1)} %get-tuple-element.28), channel_id=1, source_target_pairs={{0,126},{2,0},{4,2},{6,4},{8,6},{10,8},{12,10},{14,12},{16,14},{18... | collective-permute-start | bytes 1769480 | tf_op jit(solution)/shard_map/ppermute | solution.py:20
  74.6 1.7 copy-start.8
  77.8 11.3 %copy-start.4 = (bf16[12,2,48,512]{3,2,0,1:T(8,128)(2,1)}, bf16[12,2,48,512]{3,2,0,1:T(8,128)(2,1)S(1)}, u32[]{:S(2)}) copy-start(bf16[12,2,48,512]{3,2,0,1:T(8,128)(2,1)S(1)} %fusion.62) | copy-start | bytes 3538948
  77.8 6.4 %copy-start.2 = (bf16[6,2,48,512]{3,2,1,0:T(8,128)(2,1)S(1)}, bf16[6,2,48,512]{3,2,1,0:T(8,128)(2,1)}, u32[]{:S(2)}) copy-start(bf16[6,2,48,512]{3,2,1,0:T(8,128)(2,1)} %get-tuple-element.27) | copy-start | bytes 1769476
  78.9 34.1 %collective-permute-start = (bf16[6,2,48,512]{3,2,0,1:T(8,128)(2,1)}, bf16[6,2,48,512]{3,2,0,1:T(8,128)(2,1)}, u32[]{:S(2)}, u32[]{:S(2)}) collective-permute-start(bf16[6,2,48,512]{3,2,0,1:T(8,128)(2,1)} %get-tuple-element.32), channel_id=1, source_target_pairs={{0,126},{2,0},{4,2},{6,4},{8,6},{10,8},{12,10},{14,12},{16,14},{18... | collective-permute-start | bytes 1769480 | tf_op jit(solution)/shard_map/ppermute | solution.py:20
  85.2 13.4 %copy-start.18 = (bf16[512,512]{1,0:T(8,128)(2,1)S(1)}, bf16[512,512]{1,0:T(8,128)(2,1)}, u32[]{:S(2)}) copy-start(bf16[512,512]{1,0:T(8,128)(2,1)} %param.15) | copy-start | bytes 1572868
  85.2 12.2 %collective-permute-start.5 = (bf16[12,2,3,512]{3,2,1,0:T(4,128)(2,1)S(1)}, bf16[12,2,3,512]{3,2,1,0:T(4,128)(2,1)S(1)}, u32[]{:S(2)}, u32[]{:S(2)}) collective-permute-start(bf16[12,2,3,512]{3,2,1,0:T(4,128)(2,1)S(1)} %pad_maximum_fusion.5), channel_id=1, source_target_pairs={{0,1},{1,0},{2,3},{3,2},{4,5},{5,4},{6,7},{7,6},{8,9},{9,8},{10,11... | collective-permute-start | bytes 221192 | tf_op jit(solution)/shard_map/ppermute | solution.py:20
  97.5 1.0 copy-start.10
  108.2 4.9 copy-start.3
  114.0 5.2 collective-permute-start.1
  121.3 1.1 copy-start.16
  171.1 3.7 copy-start.14
  180.0 7.8 %copy-start.1 = (bf16[8,144,8,64]{1,3,2,0:T(8,128)(2,1)S(1)}, bf16[8,144,8,64]{1,3,2,0:T(8,128)(2,1)}, u32[]{:S(2)}) copy-start(bf16[8,144,8,64]{1,3,2,0:T(8,128)(2,1)} %copy.85) | copy-start | bytes 3538948
  180.0 7.8 %copy-start.21 = (f32[8,8,144,144]{2,3,1,0:T(8,128)S(1)}, f32[8,8,144,144]{2,3,1,0:T(8,128)}, u32[]{:S(2)}) copy-start(f32[8,8,144,144]{2,3,1,0:T(8,128)} %get-tuple-element.34) | copy-start | bytes 15925252
  263.9 18.8 %collective-permute-start.6 = (bf16[6,2,48,512]{3,2,0,1:T(8,128)(2,1)S(1)}, bf16[6,2,48,512]{3,2,0,1:T(8,128)(2,1)S(1)}, u32[]{:S(2)}, u32[]{:S(2)}) collective-permute-start(bf16[6,2,48,512]{3,2,0,1:T(8,128)(2,1)S(1)} %get-tuple-element.25), channel_id=1, source_target_pairs={{0,2},{2,4},{4,6},{6,8},{8,10},{10,12},{12,14},{14,16},{16,18},{18... | collective-permute-start | bytes 1769480 | tf_op jit(solution)/shard_map/ppermute | solution.py:20
  282.8 29.2 %collective-permute-start.7 = (bf16[12,2,3,512]{3,2,0,1:T(4,128)(2,1)S(1)}, bf16[12,2,3,512]{3,2,0,1:T(4,128)(2,1)S(1)}, u32[]{:S(2)}, u32[]{:S(2)}) collective-permute-start(bf16[12,2,3,512]{3,2,0,1:T(4,128)(2,1)S(1)} %pad_maximum_fusion.4), channel_id=1, source_target_pairs={{0,1},{1,0},{2,3},{3,2},{4,5},{5,4},{6,7},{7,6},{8,9},{9,8},{10,11... | collective-permute-start | bytes 221192 | tf_op jit(solution)/shard_map/ppermute | solution.py:20
  306.1 5.9 %copy-start.7 = (bf16[12,64,4,48,4]{1,3,0,4,2:T(8,128)(2,1)S(1)}, bf16[12,64,4,48,4]{1,3,0,4,2:T(8,128)(2,1)}, u32[]{:S(2)}) copy-start(bf16[12,64,4,48,4]{1,3,0,4,2:T(8,128)(2,1)} %copy.94) | copy-start | bytes 3538948
  306.1 5.9 %copy-start.9 = (bf16[12,2,48,512]{3,2,1,0:T(8,128)(2,1)S(1)}, bf16[12,2,48,512]{3,2,1,0:T(8,128)(2,1)}, u32[]{:S(2)}) copy-start(bf16[12,2,48,512]{3,2,1,0:T(8,128)(2,1)} %param.17) | copy-start | bytes 3538948
  330.7 244.0 %all-reduce.3.cloned.1.call-start = ((), (), s32[]{:S(2)}) async-start(), calls=%async_computation.4 | async-start | bytes 8388608 | tf_op jit(solution)/shard_map/psum | solution.py:181
  352.0 6.8 %copy-start.11 = (bf16[12,2,48,512]{3,2,1,0:T(8,128)(2,1)S(1)}, bf16[12,2,48,512]{3,2,1,0:T(8,128)(2,1)}, u32[]{:S(2)}) copy-start(bf16[12,2,48,512]{3,2,1,0:T(8,128)(2,1)} %copy-done.10) | copy-start | bytes 3538948
  358.8 3.3 copy-start.6
  367.3 1.3 copy-start.12
  367.3 1.4 copy-start.19
  369.5 19.5 %copy-start.5 = (bf16[12,2,48,512]{3,2,0,1:T(8,128)(2,1)S(1)}, bf16[12,2,48,512]{3,2,0,1:T(8,128)(2,1)}, u32[]{:S(2)}) copy-start(bf16[12,2,48,512]{3,2,0,1:T(8,128)(2,1)} %copy-done.4) | copy-start | bytes 3538948
  369.6 13.2 %collective-permute-start.2 = (bf16[6,2,48,512]{3,2,0,1:T(8,128)(2,1)S(1)}, bf16[6,2,48,512]{3,2,0,1:T(8,128)(2,1)S(1)}, u32[]{:S(2)}, u32[]{:S(2)}) collective-permute-start(bf16[6,2,48,512]{3,2,0,1:T(8,128)(2,1)S(1)} %copy.80), channel_id=1, source_target_pairs={{0,2},{2,4},{4,6},{6,8},{8,10},{10,12},{12,14},{14,16},{16,18},{18... | collective-permute-start | bytes 1769480 | tf_op jit(solution)/shard_map/ppermute | solution.py:20
  383.0 6.1 %collective-permute-start.3 = (bf16[12,2,3,512]{3,2,0,1:T(4,128)(2,1)S(1)}, bf16[12,2,3,512]{3,2,0,1:T(4,128)(2,1)S(1)}, u32[]{:S(2)}, u32[]{:S(2)}) collective-permute-start(bf16[12,2,3,512]{3,2,0,1:T(4,128)(2,1)S(1)} %slice.97), channel_id=1, source_target_pairs={{0,1},{1,0},{2,3},{3,2},{4,5},{5,4},{6,7},{7,6},{8,9},{9,8},{10,11... | collective-permute-start | bytes 221192 | tf_op jit(solution)/shard_map/ppermute | solution.py:20
  574.8 3.8 copy-start.13
Sparse Core Ops, SparseCore 0:
  10.3 57.9 all-gather.1
  330.8 82.2 reduce-scatter.1
  419.6 155.0 all-reduce.2
where the time goes:
time: 596 us; the launch traced here: 586 us
  waiting for transfers between devices  231 us (39%)
  local copies, waits for them, and re-layouts  199 us (33%)
  matrix products  75.6 us (13%)
  other arithmetic  27.1 us (5%)
  starting transfers between devices  25.2 us (4%)
  blocking collectives  14.6 us (2%)
  between operations  14.4 us (2%)
    psum x1, waiting for transfers between devices, per_device(): lax.psum((grad_qkv_part, grad_proj_part), ('var', 'lat', 'lon'))  146 us
    another operation x2, local copies, waits for them, and re-layouts, per_device(): grid = received[0].reshape(row_count, channels, PSIDE, col_count, PSIDE)  45.7 us
    ppermute x8, waiting for transfers between devices, from_behind(): lax.ppermute(array, axis, [(i, (i + by) % count) for i in range(count)])  44.7 us
    unnamed x53, local copies, waits for them, and re-layouts  24 us
    reduce_scatter x1, waiting for transfers between devices, per_device(): lax.psum_scatter(by_variable.astype(jnp.bfloat16), 'var', scatter_dimensi...  22.3 us
    dot_general x1, matrix products, per_device(): jnp.einsum('whqk,wqhe->wkhe', grad_score, query_rows, preferred_element_t...  16.9 us
    dot_general x1, matrix products, per_device(): jnp.einsum('whqk,wkhe->wqhe', grad_score, key_rows, preferred_element_typ...  16.8 us
    all_to_all x1, waiting for transfers between devices, per_device(): lax.all_to_all(pixels, 'var', split_axis=0, concat_axis=2, tiled=True)  16.7 us
  transfers between devices with their start and end apart: 12, of which 8 were waited for; matrix products, arithmetic and copies ran while one was open for 22% of the time, Pallas kernels for 0%

commit v1 on v0

v1 whole, which is shorter than its diff:
```python
import functools

import jax
import jax.numpy as jnp
import numpy as np
from jax import lax
from jax.experimental import pallas as pl
from jax.experimental.pallas import tpu as pltpu
from jax.sharding import Mesh, PartitionSpec as P

D = 512
HEADS = 8
HDIM = 64
PSIDE = 4
WCOL = 6
ROWS = 12
HALF = 6
COLS = 48
WINDOWS = 8
LEVELS = 2
TOKENS = 1152
WTOK = 144
PATCHES = 576
LANES = 1152
EPS = 1e-05
BF = jnp.bfloat16
F32 = jnp.float32
VMEM_LIMIT = 58 * 1024 * 1024

NN = (((1,), (0,)), ((), ()))
NT = (((1,), (1,)), ((), ()))
TN = (((0,), (0,)), ((), ()))


def dot(a, b, dims=NN):
    return lax.dot_general(a, b, dims, preferred_element_type=F32)


def pixel_lane(b, patch):
    return np.where(patch < 256, 256 * b + patch, 1024 + 32 * b + patch - 256)


def edge_place():
    place = np.zeros((HALF, 128, 128), np.float32)
    for j in range(HALF):
        lane = np.arange(12)
        place[j, lane, j * 12 + lane] = 1
    return place


def pixel_place():
    main = np.zeros((HALF, 4 * COLS, LANES), np.float32)
    edge = np.zeros((128, LANES), np.float32)
    for j in range(HALF):
        for c in range(COLS):
            for b in range(PSIDE):
                col = c - 3 if c >= 3 else COLS - 3 + c
                patch = (col // WCOL) * 36 + j * WCOL + col % WCOL
                lane = pixel_lane(b, patch)
                if c >= 3:
                    main[j, c * PSIDE + b, lane] = 1
                else:
                    edge[j * 12 + c * PSIDE + b, lane] = 1
    return main, edge


def patch_place():
    main = np.zeros((2, PATCHES, 256), np.float32)
    rest = np.zeros((2, PSIDE, PATCHES, 128), np.float32)
    for half in range(2):
        for w in range(WINDOWS):
            for i in range(36):
                patch = w * 36 + i
                row = w * 72 + half * 36 + i
                if patch < 256:
                    main[half, row, patch] = 1
                else:
                    for b in range(PSIDE):
                        rest[half, b, row, 32 * b + patch - 256] = 1
    return main, rest


def token_place():
    place = np.zeros((TOKENS, TOKENS + 128), np.float32)
    for w in range(WINDOWS):
        for level in range(LEVELS):
            for half in range(2):
                for j in range(HALF):
                    for c6 in range(WCOL):
                        t = w * WTOK + level * 72 + half * 36 + j * WCOL + c6
                        c = w * WCOL + c6 + 3
                        if c < COLS:
                            place[t, half * PATCHES + (j * LEVELS + level) * COLS + c] = 1
                        else:
                            place[t, TOKENS + half * 36 + (j * LEVELS + level) * 3 + c - COLS] = 1
    return place


def half_rows(pix_ref, half, j, lanes):
    rows = pix_ref[:, half * HALF + j, :, :, :lanes].astype(F32)
    merged = jnp.concatenate([rows[:, 0], rows[:, 1]], axis=1)
    return merged.reshape(merged.shape[0] * 8, lanes).astype(BF)


def edge_kernel(pix_ref, place_ref, out_ref):
    for half in range(2):
        total = None
        for j in range(HALF):
            term = dot(half_rows(pix_ref, half, j, 128), place_ref[j])
            total = term if total is None else total + term
        out_ref[half] = total.astype(BF)


def pack_kernel(info_ref, pix_ref, main_ref, edge_ref, halo_ref, out_ref):
    lat = info_ref[0]
    bands = out_ref.shape[0]
    for half in range(2):
        total = dot(halo_ref[half], edge_ref[...])
        for j in range(HALF):
            total = total + dot(half_rows(pix_ref, half, j, 4 * COLS), main_ref[j])
        block = total.reshape(bands, 8, LANES).astype(BF)
        if half == 1:
            out_ref[:, lat] = block
        else:

            @pl.when(lat == 0)
            def _():
                out_ref[: bands - 1, 1] = block[1:]
                out_ref[bands - 1 :, 1] = block[:1]

            @pl.when(lat == 1)
            def _():
                out_ref[:, 0] = block


def block_kernel(
    info_ref,
    recv_ref,
    wown_ref,
    woth_ref,
    idxc_ref,
    idxr_ref,
    mix_ref,
    gain_ref,
    wqkv_ref,
    wproj_ref,
    mcol_ref,
    mrow_ref,
    cown_ref,
    cnext_ref,
    cedge_ref,
    pmain_ref,
    prest_ref,
    tok_ref,
    tokt_ref,
    top_ref,
    bot_ref,
    edge_ref,
    gown_ref,
    goth_ref,
    a_s,
    at_s,
    lw_s,
    t_s,
    unit_s,
    inv_s,
    norm_s,
    qkv_s,
    gb_s,
    ga_s,
    att_s,
    gp_s,
    bo_s,
    gt_s,
    gs_s,
):
    lat = info_ref[0]
    core = info_ref[1]
    gain = gain_ref[...]

    halves = []
    for half in range(2):
        src = lat if half == 0 else 1 - lat
        part = recv_ref[:, src].astype(F32)
        halves.append(part.reshape(256, LANES).astype(BF))
    for b in range(PSIDE):
        rows = None
        columns = None
        for half in range(2):
            main = halves[half][:, 256 * b : 256 * b + 256]
            rest = halves[half][:, 1024:1152]
            r = dot(pmain_ref[half], main, NT) + dot(prest_ref[half, b], rest, NT)
            c = dot(main, pmain_ref[half], NT) + dot(rest, prest_ref[half, b], NT)
            rows = r if rows is None else rows + r
            columns = c if columns is None else columns + c
        a_s[:, 256 * b : 256 * b + 256] = rows.astype(BF)
        at_s[256 * b : 256 * b + 256, :] = columns.astype(BF)
        lane = lax.broadcasted_iota(jnp.int32, (256, 512), 1)
        idx = idxc_ref[256 * b : 256 * b + 256, :]
        pick_own = jnp.where(lane == idx, 1.0, 0.0).astype(BF)
        pick_oth = jnp.where(lane + 512 == idx, 1.0, 0.0).astype(BF)
        weight = dot(pick_own, wown_ref[...]) + dot(pick_oth, woth_ref[...])
        for level in range(LEVELS):
            lw_s[256 * b : 256 * b + 256, level * D : level * D + D] = (
                weight * mix_ref[:, level : level + 1]
            ).astype(BF)
    for level in range(LEVELS):
        tok = dot(a_s[...], lw_s[:, level * D : level * D + D]).astype(BF).astype(F32)
        for w in range(WINDOWS):
            t_s[w * WTOK + level * 72 : w * WTOK + level * 72 + 72, :] = tok[w * 72 : w * 72 + 72]

    def norm_step(w, carry):
        rows = pl.ds(pl.multiple_of(w * WTOK, WTOK), WTOK)
        x = t_s[rows, :]
        centred = x - jnp.mean(x, axis=-1, keepdims=True)
        inv = lax.rsqrt(jnp.mean(centred * centred, axis=-1, keepdims=True) + EPS)
        unit = centred * inv
        unit_s[rows, :] = unit
        inv_s[rows, :] = inv
        norm_s[rows, :] = (unit * gain).astype(BF)
        return carry

    lax.fori_loop(0, WINDOWS, norm_step, 0)
    for n in range(3):
        qkv_s[:, n * D : n * D + D] = dot(norm_s[...], wqkv_ref[:, n * D : n * D + D]).astype(BF)

    gb = dot(tok_ref[:, :PATCHES], cown_ref[...])
    gb = gb + dot(tok_ref[:, PATCHES:TOKENS], cnext_ref[...])
    gb = gb + dot(tok_ref[:, TOKENS:], cedge_ref[...])
    gb_s[...] = gb.astype(BF)
    ga_s[...] = dot(gb_s[...], wproj_ref[...], NT).astype(BF)

    lane = lax.broadcasted_iota(jnp.int32, (1, 128), 1)
    low = lane < HDIM
    keep = [
        jnp.where(low, 1.0, 0.0).astype(BF),
        jnp.where(low, 0.0, 1.0).astype(BF),
    ]

    def window_step(w, carry):
        rows = pl.ds(pl.multiple_of(w * WTOK, WTOK), WTOK)
        same = mcol_ref[w] == mrow_ref[w]
        for pair in range(HEADS // 2):
            at = pair * 128
            q2 = qkv_s[rows, at : at + 128]
            k2 = qkv_s[rows, D + at : D + at + 128]
            v2 = qkv_s[rows, 2 * D + at : 2 * D + at + 128]
            g2 = ga_s[rows, at : at + 128]
            parts = []
            for e in range(2):
                score = dot(q2 * (keep[e] * 0.125), k2, NT)
                score = jnp.where(same, score, -1e30)
                ex = jnp.exp(score - jnp.max(score, axis=-1, keepdims=True))
                prob = ex * (1.0 / jnp.sum(ex, axis=-1, keepdims=True))
                half_prob = prob.astype(BF)
                out = dot(half_prob, v2)
                gv = dot(half_prob, g2, TN)
                gprob = dot(g2 * keep[e], v2, NT)
                centred = gprob - jnp.sum(prob * gprob, axis=-1, keepdims=True)
                gscore = (prob * centred * 0.125).astype(BF)
                gq = dot(gscore, k2)
                gk = dot(gscore, q2, TN)
                parts.append((out, gq, gk, gv))
            out, gq, gk, gv = (jnp.where(low, x, y).astype(BF) for x, y in zip(*parts))
            att_s[rows, at : at + 128] = out
            gp_s[rows, at : at + 128] = gq
            gp_s[rows, D + at : D + at + 128] = gk
            gp_s[rows, 2 * D + at : 2 * D + at + 128] = gv
        return carry

    lax.fori_loop(0, WINDOWS, window_step, 0)

    branch = dot(att_s[...], wproj_ref[...]).astype(BF).astype(F32)
    bo_s[...] = (t_s[...] + branch).astype(BF)
    top_ref[...] = dot(tokt_ref[:PATCHES], bo_s[...]).astype(BF)
    bot_ref[...] = dot(tokt_ref[PATCHES:TOKENS], bo_s[...]).astype(BF)
    edge_ref[...] = dot(tokt_ref[TOKENS:], bo_s[...]).astype(BF)

    for ref, which in ((gown_ref, core), (goth_ref, 1 - core)):
        at = pl.multiple_of(which * 768, 256)
        ref[:, 0:768] = dot(norm_s[...], gp_s[:, pl.ds(at, 768)], TN).astype(BF)
        at = pl.multiple_of(which * 256, 256)
        ref[:, 768:1024] = dot(att_s[...], gb_s[:, pl.ds(at, 256)], TN).astype(BF)

    for w in range(WINDOWS):
        rows = slice(w * WTOK, w * WTOK + WTOK)
        h = dot(gp_s[rows, :], wqkv_ref[...], NT) * gain
        unit = unit_s[rows, :]
        shifted = inv_s[rows, :] * (
            h
            - jnp.mean(h, axis=-1, keepdims=True)
            - unit * jnp.mean(h * unit, axis=-1, keepdims=True)
        )
        total = (gb_s[rows, :].astype(F32) + shifted.astype(BF).astype(F32)).astype(BF).astype(F32)
        for level in range(LEVELS):
            gt_s[level, w * 72 : w * 72 + 72, :] = total[level * 72 : level * 72 + 72]

    for b in range(PSIDE):
        slot = None
        for level in range(LEVELS):
            part = dot(at_s[256 * b : 256 * b + 256, :], gt_s[level].astype(BF))
            part = part * mix_ref[:, level : level + 1]
            slot = part if slot is None else slot + part
        gs_s[256 * b : 256 * b + 256, :] = slot.astype(BF)
    row = lax.broadcasted_iota(jnp.int32, (512, 1024), 0)
    idx = idxr_ref[...]
    for ref, offset in ((gown_ref, 0), (goth_ref, 512)):
        pick = jnp.where(row + offset == idx, 1.0, 0.0).astype(BF)
        ref[:, 1024:1536] = dot(pick, gs_s[...]).astype(BF)


def shape(*dims, dtype=BF):
    return jax.ShapeDtypeStruct(dims, dtype)


def vmem_call(kernel, outs, scratch=(), smem_first=False, count=0):
    specs = [pl.BlockSpec(memory_space=pltpu.VMEM)] * count
    if smem_first:
        specs[0] = pl.BlockSpec(memory_space=pltpu.SMEM)
    many = isinstance(outs, (list, tuple))
    vm = pl.BlockSpec(memory_space=pltpu.VMEM)
    return pl.pallas_call(
        kernel,
        out_shape=outs,
        in_specs=specs,
        out_specs=[vm] * len(outs) if many else vm,
        scratch_shapes=list(scratch),
        compiler_params=pltpu.CompilerParams(vmem_limit_bytes=VMEM_LIMIT),
    )


def per_device(
    counts,
    pixels,
    var_order,
    embed_weight,
    level_mix,
    norm_gain,
    w_qkv,
    w_proj,
    mask_ids,
    cotangent,
):
    chips, lats, lons = counts
    bands = chips * 2
    lat = lax.axis_index("lat")
    core = lax.axis_index("core")
    lon = lax.axis_index("lon")
    info = jnp.stack([lat, core]).astype(jnp.int32)
    rows_ring = ("chip", "core", "lat")
    everyone = ("chip", "core", "lat", "lon")
    ring = bands * lats
    group = ("chip", "lat", "lon")
    group_size = chips * lats * lons

    swap_lon = [(0, 1), (1, 0)]
    swap_core = [(0, 1), (1, 0)]

    own_weight = lax.all_gather(embed_weight.reshape(32, D), "chip", axis=0, tiled=True)
    oth_weight = lax.ppermute(own_weight, "core", swap_core)

    cot_first = cotangent[:HALF]
    cot_next = lax.ppermute(cot_first, rows_ring, [(i, (i - 1) % ring) for i in range(ring)])
    strip_first = cotangent[:HALF, :, :3].reshape(36, D)
    strip_last = cotangent[HALF:, :, :3].reshape(36, D)
    east = lax.ppermute(strip_last, "lon", swap_lon)
    north_east = lax.ppermute(
        strip_first,
        everyone,
        [(i * 2 + k, ((i - 1) % ring) * 2 + 1 - k) for i in range(ring) for k in range(2)],
    )
    cot_edge = jnp.concatenate([east, north_east, jnp.zeros((128 - 72, D), BF)], axis=0)

    place_e = jnp.asarray(edge_place(), BF)
    main, edge = pixel_place()
    border = vmem_call(edge_kernel, shape(2, bands * 8, 128), count=2)(pixels, place_e)
    halo = lax.ppermute(border, "lon", swap_lon)
    packed = vmem_call(pack_kernel, shape(bands, 2, 8, LANES), smem_first=True, count=5)(
        info, pixels, jnp.asarray(main, BF), jnp.asarray(edge, BF), halo
    )
    recv = lax.all_to_all(
        packed.reshape(bands * 2, 8, LANES), rows_ring, split_axis=0, concat_axis=0, tiled=True
    ).reshape(bands, 2, 8, LANES)

    device = var_order // 2
    base = jnp.where(device % 2 == core, 0, 512) + (device // 2) * 32 + (var_order % 2) * 16
    index = base[None, :, None] + (
        jnp.arange(4)[:, None, None] + 4 * jnp.arange(4)[None, None, :]
    )
    index = index.reshape(1024).astype(jnp.int32)
    slot_mix = jnp.repeat(level_mix[var_order], 4, axis=0)

    ids = mask_ids.reshape(2, HALF, LEVELS, WINDOWS, WCOL).transpose(3, 2, 0, 1, 4)
    ids = ids.reshape(WINDOWS, WTOK)

    pmain, prest = patch_place()
    tok = token_place()
    top, bot, strip, gown, goth = vmem_call(
        block_kernel,
        [
            shape(PATCHES, D),
            shape(PATCHES, D),
            shape(128, D),
            shape(512, 1536),
            shape(512, 1536),
        ],
        [
            pltpu.VMEM((PATCHES, 1024), BF),
            pltpu.VMEM((1024, PATCHES), BF),
            pltpu.VMEM((1024, 1024), BF),
            pltpu.VMEM((TOKENS, D), F32),
            pltpu.VMEM((TOKENS, D), F32),
            pltpu.VMEM((TOKENS, 1), F32),
            pltpu.VMEM((TOKENS, D), BF),
            pltpu.VMEM((TOKENS, 3 * D), BF),
            pltpu.VMEM((TOKENS, D), BF),
            pltpu.VMEM((TOKENS, D), BF),
            pltpu.VMEM((TOKENS, D), BF),
            pltpu.VMEM((TOKENS, 3 * D), BF),
            pltpu.VMEM((TOKENS, D), BF),
            pltpu.VMEM((LEVELS, PATCHES, D), F32),
            pltpu.VMEM((1024, D), BF),
        ],
        smem_first=True,
        count=19,
    )(
        info,
        recv,
        own_weight,
        oth_weight,
        index[:, None],
        index[None, :],
        slot_mix,
        norm_gain[None, :],
        w_qkv,
        w_proj,
        ids[:, :, None],
        ids[:, None, :],
        cotangent[HALF:].reshape(PATCHES, D),
        cot_next.reshape(PATCHES, D),
        cot_edge,
        jnp.asarray(pmain, BF),
        jnp.asarray(prest, BF),
        jnp.asarray(tok, BF),
        jnp.asarray(tok.T, BF),
    )

    from_core = lax.ppermute(goth, "core", swap_core)
    chip_sum = (gown.astype(F32) + from_core.astype(F32)).astype(BF)
    terms = lax.all_to_all(
        chip_sum.reshape(group_size, 8, 1536), group, split_axis=0, concat_axis=0, tiled=True
    )
    owned = jnp.sum(terms.astype(F32), axis=0).astype(BF)
    copies = jnp.broadcast_to(owned[None, :, :1024], (group_size, 8, 1024))
    mine = lax.all_to_all(copies, group, split_axis=0, concat_axis=0, tiled=True)
    mine = mine.reshape(512, 1024)
    other = lax.ppermute(mine, "core", swap_core)
    first = jnp.where(core == 0, mine, other).astype(F32)
    second = jnp.where(core == 0, other, mine).astype(F32)
    grad_qkv = jnp.concatenate([first[:, :768], second[:, :768]], axis=1)
    grad_proj = jnp.concatenate([first[:, 768:], second[:, 768:]], axis=1)

    embed_part = owned[:, 1024:]
    pieces = [embed_part]
    for dlat, dlon in ((0, 1), (1, 0), (1, 1)):
        pieces.append(
            lax.ppermute(
                embed_part,
                ("lat", "lon"),
                [(i * 2 + k, (i ^ dlat) * 2 + (k ^ dlon)) for i in range(2) for k in range(2)],
            )
        )
    stacked = jnp.stack(pieces)
    tile = lat * 2 + lon
    grad_embed = jnp.concatenate(
        [lax.dynamic_index_in_dim(stacked, tile ^ t, 0, keepdims=False) for t in range(4)], axis=0
    )
    grad_embed = grad_embed.reshape(2, 16, D).astype(F32)

    from_before = lax.ppermute(bot, rows_ring, [(i, (i + 1) % ring) for i in range(ring)])
    west = lax.ppermute(strip[:36], "lon", swap_lon)
    south_west = lax.ppermute(
        strip[36:72],
        everyone,
        [(i * 2 + k, ((i + 1) % ring) * 2 + 1 - k) for i in range(ring) for k in range(2)],
    )
    body = jnp.concatenate([from_before, top], axis=0).reshape(ROWS, LEVELS, COLS, D)
    sides = jnp.concatenate([south_west, west], axis=0).reshape(ROWS, LEVELS, 3, D)
    block_out = jnp.concatenate([sides, body[:, :, 3:]], axis=2)
    return (block_out, grad_embed, grad_qkv, grad_proj)


def solution(mesh):
    var, lats, lons = (mesh.shape[name] for name in ("var", "lat", "lon"))
    chips = var // 2
    fine = Mesh(mesh.devices.reshape(chips, 2, lats, lons), ("chip", "core", "lat", "lon"))
    both = ("chip", "core")
    in_specs = (
        P(None, "lat", both, None, "lon"),
        P(),
        P(both, None, None),
        P(),
        P(),
        P(),
        P(),
        P(("chip", "core", "lat"), None, "lon"),
        P(("chip", "core", "lat"), None, "lon", None),
    )
    out_specs = (P(("chip", "core", "lat"), None, "lon", None), P(both, None, None), P(), P())
    return jax.shard_map(
        functools.partial(per_device, (chips, lats, lons)),
        mesh=fine,
        in_specs=in_specs,
        out_specs=out_specs,
        check_vma=False,
    )
```

time: 596 us -> 228 us (0.38); the launches traced: 586 us -> 225 us
  waiting for transfers between devices: 231 us -> 21.2 us
  local copies, waits for them, and re-layouts: 199 us -> 9.34 us
  Pallas kernels: 0 us -> 83.6 us
  matrix products: 75.6 us -> 0 us
  blocking collectives: 14.6 us -> 58.8 us
  other arithmetic: 27.1 us -> 9.33 us
  starting transfers between devices: 25.2 us -> 42.2 us
  between operations: 14.4 us -> 0.88 us
    psum x1 -> x0, waiting for transfers between devices: 146 us -> none  [per_device(): lax.psum((grad_qkv_part, grad_proj_part), ('var', 'lat', 'lon'))]
    another operation x12 -> x3, local copies, waits for them, and re-layouts: 108 us -> 1.74 us  [the longest x1 1.01 us: per_device(): ids[:, :, None]]
    pallas_call x0 -> x3, Pallas kernels: none -> 83.6 us  [the longest x1 73.5 us: per_device(): vmem_call(block_kernel, [shape(PATCHES, D), shape(PATCHES, D), shape(128,...]
    dot_general x14 -> x0, matrix products: 75.6 us -> none  [the longest x1 16.9 us: per_device(): jnp.einsum('whqk,wqhe->wkhe', grad_score, query_rows, preferred_element_t...]
    ppermute x8 -> x13, waiting for transfers between devices: 44.7 us -> 9.32 us  [the longest x1 4.6 us: per_device(): west = lax.ppermute(strip[:36], 'lon', swap_lon)]
    all_to_all x0 -> x1, blocking collectives: none -> 31.2 us  [per_device(): lax.all_to_all(chip_sum.reshape(group_size, 8, 1536), group, split_axis=0...]
    all_gather x0 -> x1, blocking collectives: none -> 27.6 us  [per_device(): lax.all_gather(embed_weight.reshape(32, D), 'chip', axis=0, tiled=True)]
    unnamed x53 -> x23, local copies, waits for them, and re-layouts: 24 us -> 1.26 us
  transfers between devices with their start and end apart: 12 -> 15, of which waited for: 8 -> 5; matrix products, arithmetic and copies ran while one was open for 22% -> 4% of each run, Pallas kernels for 0% -> 3%
where the time goes in v1:
time: 228 us; the launch traced here: 225 us
  Pallas kernels  83.6 us (37%)
  blocking collectives  58.8 us (26%)
  starting transfers between devices  42.2 us (19%)
  waiting for transfers between devices  21.2 us (9%)
  local copies, waits for them, and re-layouts  9.34 us (4%)
  other arithmetic  9.33 us (4%)
    pallas_call x1, Pallas kernels, per_device(): vmem_call(block_kernel, [shape(PATCHES, D), shape(PATCHES, D), shape(128,...  73.5 us
    all_to_all x1, blocking collectives, per_device(): lax.all_to_all(chip_sum.reshape(group_size, 8, 1536), group, split_axis=0...  31.2 us
    all_gather x1, blocking collectives, per_device(): lax.all_gather(embed_weight.reshape(32, D), 'chip', axis=0, tiled=True)  27.6 us
    all_to_all x1, waiting for transfers between devices, per_device(): lax.all_to_all(copies, group, split_axis=0, concat_axis=0, tiled=True)  11.9 us
    all_to_all x1, starting transfers between devices, per_device(): lax.all_to_all(packed.reshape(bands * 2, 8, LANES), rows_ring, split_axis...  9.72 us
    pallas_call x1, Pallas kernels, per_device(): vmem_call(pack_kernel, shape(bands, 2, 8, LANES), smem_first=True, count=5)  7.58 us
    ppermute x1, starting transfers between devices, per_device(): oth_weight = lax.ppermute(own_weight, 'core', swap_core)  6.08 us
    all_to_all x1, starting transfers between devices, per_device(): lax.all_to_all(copies, group, split_axis=0, concat_axis=0, tiled=True)  5.29 us
  transfers between devices with their start and end apart: 15, of which 5 were waited for; matrix products, arithmetic and copies ran while one was open for 4% of the time, Pallas kernels for 3%

profile of v1, /device:TPU:1, one launch (start us, length us, event | category | flops | bytes accessed | tf_op | source)
XLA Modules:
  0.0 225.3 jit_solution(17194489932159544094)
XLA Ops:
  0.6 2.5 %shard_map.183 = bf16[2,256,128]{2,1,0:T(8,128)(2,1)} custom-call(bf16[32,12,2,4,192]{4,3,2,1,0:T(4,128)(2,1)} %pix_ref.3, bf16[6,128,128]{2,1,0:T(8,128)(2,1)} %constant.91.clone.place_ref), custom_call_target="tpu_custom_call" | custom-call | tf_op jit(solution)/shard_map/pallas_call | solution.py:376
  3.2 3.6 %collective-permute-start = (bf16[2,256,128]{2,1,0:T(8,128)(2,1)}, bf16[2,256,128]{2,1,0:T(8,128)(2,1)S(1)}, u32[]{:S(2)}, u32[]{:S(2)}) collective-permute-start(bf16[2,256,128]{2,1,0:T(8,128)(2,1)} %shard_map.183), channel_id=1, source_target_pairs={{0,1},{1,0},{2,3},{3,2},{4,5},{5,4},{6,7},{7,6},{8,9},{9,8},{10,11... | collective-permute-start | bytes 393224 | tf_op jit(solution)/shard_map/ppermute | solution.py:377
  6.8 0.1 collective-permute-start.3
  7.0 3.9 %collective-permute-start.4 = (bf16[36,512]{1,0:T(8,128)(2,1)S(1)}, bf16[36,512]{1,0:T(8,128)(2,1)S(1)}, u32[]{:S(2)}, u32[]{:S(2)}) collective-permute-start(bf16[36,512]{1,0:T(8,128)(2,1)S(1)} %reshape.131), channel_id=1, source_target_pairs={{0,127},{1,126},{2,1},{3,0},{4,3},{5,2},{6,5},{7,4},{8,7},{9,6},{1... | collective-permute-start | bytes 110600 | tf_op jit(solution)/shard_map/ppermute | solution.py:367
  10.9 0.9 fusion.5
  11.8 0.2 collective-permute-start.2
  12.0 0.7 pad_add_fusion.info_ref
  12.7 0.0 collective-permute-done.halo_ref
  12.7 0.7 copy-done.5
  13.3 7.6 %shard_map.184 = bf16[32,2,8,1152]{3,2,1,0:T(8,128)(2,1)} custom-call(s32[2]{0:T(128)} %pad_add_fusion.info_ref, bf16[32,12,2,4,192]{4,3,2,1,0:T(4,128)(2,1)} %pix_ref.3, bf16[6,192,1152]{2,1,0:T(8,128)(2,1)} %constant.92.clone.main_ref, bf16[128,1152]{1,0:T(8,128)(2,1)} %constant.93.clone.edge_ref, bf16[2,256,128]{2,1,0:T(8,128)(2,1)} %copy-done.5), custom_call_target="tpu_custom_call" | custom-call | tf_op jit(solution)/shard_map/pallas_call | solution.py:378
  20.9 9.7 %all-to-all-start = ((bf16[64,8,1152]{2,1,0:T(8,128)(2,1)}), bf16[64,8,1152]{2,1,0:T(8,128)(2,1)S(1)}, u32[]{:S(2)}, u32[]{:S(2)}) async-start(bf16[64,8,1152]{2,1,0:T(8,128)(2,1)} %bitcast.33), calls=%async_computation | async-start | bytes 2359296 | tf_op jit(solution)/shard_map/all_to_all | solution.py:381
  30.6 0.0 copy-start.9
  30.7 27.6 %all_gather.3.wown_ref = bf16[512,512]{1,0:T(8,128)(2,1)S(1)} all-gather(bf16[32,512]{1,0:T(8,128)(2,1)S(1)} %bitcast.40), channel_id=1, replica_groups=mesh['chip'=16,'core'=2,'lat'=2,'lon'=2] {'chip'}, dimensions={0}, use_global_device_ids=true | all-gather | bytes 557056 | tf_op jit(solution)/shard_map/all_gather | solution.py:359
  58.3 6.1 %collective-permute-start.1 = (bf16[512,512]{1,0:T(8,128)(2,1)S(1)}, bf16[512,512]{1,0:T(8,128)(2,1)}, u32[]{:S(2)}, u32[]{:S(2)}) collective-permute-start(bf16[512,512]{1,0:T(8,128)(2,1)S(1)} %all_gather.3.wown_ref), channel_id=1, source_target_pairs={{0,4},{4,0},{1,5},{5,1},{2,6},{6,2},{3,7},{7,3},{8,12},{12,8},{9,1... | collective-permute-start | bytes 1572872 | tf_op jit(solution)/shard_map/ppermute | solution.py:360
  64.4 0.1 broadcast_add_fusion
  64.5 1.0 add.114.idxc_ref
  65.5 0.7 add.105.idxr_ref
  66.2 0.1 reshape.127
  66.4 1.0 broadcast_in_dim_reshape.10.mcol_ref
  67.4 0.7 broadcast_in_dim_reshape.11.mrow_ref
  68.1 0.1 copy.22
  68.2 0.6 gather_fusion
  68.8 0.1 pad.20.clone
  68.9 0.0 collective-permute-done.3
  68.9 0.0 collective-permute-done.4
  68.9 0.7 maximum_maximum_fusion.cedge_ref
  69.6 0.0 collective-permute-done.1.woth_ref
  69.6 0.0 collective-permute-done.2
  69.6 0.0 all-to-all-done
  69.6 0.0 copy-start
  69.6 0.7 broadcast_in_dim.29
  70.4 0.1 copy-done.3
  70.5 0.4 copy-done
  70.9 73.5 %shard_map.185 = (bf16[576,512]{1,0:T(8,128)(2,1)}, bf16[576,512]{1,0:T(8,128)(2,1)}, bf16[128,512]{1,0:T(8,128)(2,1)}, bf16[512,1536]{1,0:T(8,128)(2,1)}, bf16[512,1536]{1,0:T(8,128)(2,1)}) custom-call(s32[2]{0:T(128)} %pad_add_fusion.info_ref, bf16[32,2,8,1152]{3,2,1,0:T(8,128)(2,1)} %bitcast.31, bf16[512,512]{1,0:T(8,128)(2,1)} %copy-done.1, ...), custom_call_target="tpu_custom_call" | custom-call | tf_op jit(solution)/shard_map/pallas_call | solution.py:398
  144.3 0.0 collective-permute-start.8
  144.3 3.6 %collective-permute-done.8 = bf16[512,1536]{1,0:T(8,128)(2,1)S(1)} collective-permute-done((bf16[512,1536]{1,0:T(8,128)(2,1)}, bf16[512,1536]{1,0:T(8,128)(2,1)S(1)}, u32[]{:S(2)}, u32[]{:S(2)}) %collective-permute-start.8) | collective-permute-done | bytes 1572896 | tf_op jit(solution)/shard_map/ppermute | solution.py:448
  148.0 1.8 fusion
  149.7 31.2 %all_to_all.15 = bf16[64,8,1536]{2,1,0:T(8,128)(2,1)S(1)} all-to-all(bf16[64,8,1536]{2,1,0:T(8,128)(2,1)S(1)} %fusion), channel_id=1, replica_groups=mesh['chip'=16,'core'=2,'lat'=2,'lon'=2] {'chip','lat','lon'}, dimensions={0} | all-to-all | bytes 3145728 | tf_op jit(solution)/shard_map/all_to_all | solution.py:450
  180.9 0.2 reduce_sum.12
  181.2 1.1 broadcast_in_dim.32
  182.3 5.3 %all-to-all-start.2 = ((bf16[64,8,1024]{2,1,0:T(8,128)(2,1)}), bf16[64,8,1024]{2,1,0:T(8,128)(2,1)S(1)}, u32[]{:S(2)}, u32[]{:S(2)}) async-start(bf16[64,8,1024]{2,1,0:T(8,128)(2,1)} %broadcast_in_dim.32), calls=%async_computation.2 | async-start | bytes 2097152 | tf_op jit(solution)/shard_map/all_to_all | solution.py:455
  187.6 1.4 collective-permute-start.7
  189.0 4.3 %collective-permute-start.5 = (bf16[36,512]{1,0:T(8,128)(2,1)S(1)}, bf16[36,512]{1,0:T(8,128)(2,1)S(1)}, u32[]{:S(2)}, u32[]{:S(2)}) collective-permute-start(bf16[36,512]{1,0:T(8,128)(2,1)S(1)} %get-tuple-element.20), channel_id=1, source_target_pairs={{0,3},{1,2},{2,5},{3,4},{4,7},{5,6},{6,9},{7,8},{8,11},{9,10},{10,... | collective-permute-start | bytes 110600 | tf_op jit(solution)/shard_map/ppermute | solution.py:482
  193.3 0.3 collective-permute-start.6
  193.5 11.9 %all-to-all-done.2 = bf16[64,8,1024]{2,1,0:T(8,128)(2,1)S(1)} async-done(((bf16[64,8,1024]{2,1,0:T(8,128)(2,1)}), bf16[64,8,1024]{2,1,0:T(8,128)(2,1)S(1)}, u32[]{:S(2)}, u32[]{:S(2)}) %all-to-all-start.2) | async-done | bytes 1048608 | tf_op jit(solution)/shard_map/all_to_all | solution.py:455
  205.4 4.0 %collective-permute-start.12 = (bf16[512,1024]{1,0:T(8,128)(2,1)S(1)}, bf16[512,1024]{1,0:T(8,128)(2,1)S(1)}, u32[]{:S(2)}, u32[]{:S(2)}) collective-permute-start(bf16[512,1024]{1,0:T(8,128)(2,1)S(1)} %bitcast.34), channel_id=1, source_target_pairs={{0,4},{4,0},{1,5},{5,1},{2,6},{6,2},{3,7},{7,3},{8,12},{12,8},{9,1... | collective-permute-start | bytes 3145736 | tf_op jit(solution)/shard_map/ppermute | solution.py:457
  209.4 0.0 collective-permute-done.5
  209.4 4.6 %collective-permute-done.6 = bf16[36,512]{1,0:T(8,128)(2,1)S(1)} collective-permute-done((bf16[36,512]{1,0:T(8,128)(2,1)S(1)}, bf16[36,512]{1,0:T(8,128)(2,1)S(1)}, u32[]{:S(2)}, u32[]{:S(2)}) %collective-permute-start.6) | collective-permute-done | bytes 36896 | tf_op jit(solution)/shard_map/ppermute | solution.py:481
  214.1 0.1 collective-permute-done.7
  214.2 0.1 pad_maximum_fusion.1
  214.3 0.6 slice.54
  214.9 2.3 %collective-permute-start.9 = (bf16[8,512]{1,0:T(8,128)(2,1)S(1)}, bf16[8,512]{1,0:T(8,128)(2,1)S(1)}, u32[]{:S(2)}, u32[]{:S(2)}) collective-permute-start(bf16[8,512]{1,0:T(8,128)(2,1)S(1)} %get-tuple-element.27), channel_id=1, source_target_pairs={{0,1},{1,0},{2,3},{3,2},{4,5},{5,4},{6,7},{7,6},{8,9},{9,8},{10,11... | collective-permute-start | bytes 24584 | tf_op jit(solution)/shard_map/ppermute | solution.py:467
  217.1 0.0 collective-permute-start.10
  217.1 1.1 collective-permute-start.11
  218.2 1.6 pad_maximum_fusion.2
  219.8 0.0 collective-permute-done.9
  219.8 0.0 collective-permute-done.10
  219.8 1.0 collective-permute-done.11
  220.9 0.6 convert.2
  221.5 0.3 select_convert_fusion.1
  221.8 0.1 slice.57
  222.0 0.1 slice.58
  222.1 1.1 pad_maximum_fusion.3
  223.3 2.0 pad_maximum_fusion
  (37 shorter events, 0.4 us)
Async XLA Ops:
  0.6 6.1 %copy-start.2 = (bf16[12,2,48,512]{3,2,1,0:T(8,128)(2,1)S(1)}, bf16[12,2,48,512]{3,2,1,0:T(8,128)(2,1)}, u32[]{:S(2)}) copy-start(bf16[12,2,48,512]{3,2,1,0:T(8,128)(2,1)} %param.24) | copy-start | bytes 3538948
  3.2 9.5 %collective-permute-start = (bf16[2,256,128]{2,1,0:T(8,128)(2,1)}, bf16[2,256,128]{2,1,0:T(8,128)(2,1)S(1)}, u32[]{:S(2)}, u32[]{:S(2)}) collective-permute-start(bf16[2,256,128]{2,1,0:T(8,128)(2,1)} %shard_map.183), channel_id=1, source_target_pairs={{0,1},{1,0},{2,3},{3,2},{4,5},{5,4},{6,7},{7,6},{8,9},{9,8},{10,11... | collective-permute-start | bytes 393224 | tf_op jit(solution)/shard_map/ppermute | solution.py:377
  6.8 62.0 %collective-permute-start.3 = (bf16[36,512]{1,0:T(8,128)(2,1)S(1)}, bf16[36,512]{1,0:T(8,128)(2,1)S(1)}, u32[]{:S(2)}, u32[]{:S(2)}) collective-permute-start(bf16[36,512]{1,0:T(8,128)(2,1)S(1)} %reshape.130), channel_id=1, source_target_pairs={{0,1},{1,0},{2,3},{3,2},{4,5},{5,4},{6,7},{7,6},{8,9},{9,8},{10,11... | collective-permute-start | bytes 110600 | tf_op jit(solution)/shard_map/ppermute | solution.py:366
  7.0 61.9 %collective-permute-start.4 = (bf16[36,512]{1,0:T(8,128)(2,1)S(1)}, bf16[36,512]{1,0:T(8,128)(2,1)S(1)}, u32[]{:S(2)}, u32[]{:S(2)}) collective-permute-start(bf16[36,512]{1,0:T(8,128)(2,1)S(1)} %reshape.131), channel_id=1, source_target_pairs={{0,127},{1,126},{2,1},{3,0},{4,3},{5,2},{6,5},{7,4},{8,7},{9,6},{1... | collective-permute-start | bytes 110600 | tf_op jit(solution)/shard_map/ppermute | solution.py:367
  11.8 57.8 %collective-permute-start.2 = (bf16[6,2,48,512]{3,2,1,0:T(8,128)(2,1)S(1)}, bf16[6,2,48,512]{3,2,1,0:T(8,128)(2,1)S(1)}, u32[]{:S(2)}, u32[]{:S(2)}) collective-permute-start(bf16[6,2,48,512]{3,2,1,0:T(8,128)(2,1)S(1)} %get-tuple-element.18), channel_id=1, source_target_pairs={{0,126},{2,0},{4,2},{6,4},{8,6},{10,8},{12,10},{14,12},{16,14},{18... | collective-permute-start | bytes 1769480 | tf_op jit(solution)/shard_map/ppermute | solution.py:363
  12.7 0.7 copy-start.5
  20.9 9.8 %copy-start.7 = (bf16[2,16,512]{2,1,0:T(8,128)(2,1)S(1)}, bf16[2,16,512]{2,1,0:T(8,128)(2,1)}, u32[]{:S(2)}) copy-start(bf16[2,16,512]{2,1,0:T(8,128)(2,1)} %param.18) | copy-start | bytes 98308
  20.9 43.5 %copy-start.10 = (s32[64]{0:T(128)S(1)}, s32[64]{0:T(128)}, u32[]{:S(2)}) copy-start(s32[64]{0:T(128)} %param.17) | copy-start | bytes 772
  20.9 45.3 %copy-start.8 = (s32[12,2,48]{2,1,0:T(2,128)S(1)}, s32[12,2,48]{2,1,0:T(2,128)}, u32[]{:S(2)}) copy-start(s32[12,2,48]{2,1,0:T(2,128)} %param.23) | copy-start | bytes 13828
  20.9 48.7 %all-to-all-start = ((bf16[64,8,1152]{2,1,0:T(8,128)(2,1)}), bf16[64,8,1152]{2,1,0:T(8,128)(2,1)S(1)}, u32[]{:S(2)}, u32[]{:S(2)}) async-start(bf16[64,8,1152]{2,1,0:T(8,128)(2,1)} %bitcast.33), calls=%async_computation | async-start | bytes 2359296 | tf_op jit(solution)/shard_map/all_to_all | solution.py:381
  30.6 37.5 %copy-start.9 = (f32[64,2]{0,1:T(2,128)S(1)}, f32[64,2]{0,1:T(2,128)}, u32[]{:S(2)}) copy-start(f32[64,2]{0,1:T(2,128)} %param.19) | copy-start | bytes 1540
  58.3 12.1 %copy-start.1 = (bf16[512,512]{1,0:T(8,128)(2,1)}, bf16[512,512]{1,0:T(8,128)(2,1)S(1)}, u32[]{:S(2)}) copy-start(bf16[512,512]{1,0:T(8,128)(2,1)S(1)} %all_gather.3.wown_ref) | copy-start | bytes 1572868
  58.3 11.3 %collective-permute-start.1 = (bf16[512,512]{1,0:T(8,128)(2,1)S(1)}, bf16[512,512]{1,0:T(8,128)(2,1)}, u32[]{:S(2)}, u32[]{:S(2)}) collective-permute-start(bf16[512,512]{1,0:T(8,128)(2,1)S(1)} %all_gather.3.wown_ref), channel_id=1, source_target_pairs={{0,4},{4,0},{1,5},{5,1},{2,6},{6,2},{3,7},{7,3},{8,12},{12,8},{9,1... | collective-permute-start | bytes 1572872 | tf_op jit(solution)/shard_map/ppermute | solution.py:360
  69.6 0.8 copy-start.3
  69.6 1.2 copy-start
  144.3 3.6 %collective-permute-start.8 = (bf16[512,1536]{1,0:T(8,128)(2,1)}, bf16[512,1536]{1,0:T(8,128)(2,1)S(1)}, u32[]{:S(2)}, u32[]{:S(2)}) collective-permute-start(bf16[512,1536]{1,0:T(8,128)(2,1)} %get-tuple-element.13), channel_id=1, source_target_pairs={{0,4},{4,0},{1,5},{5,1},{2,6},{6,2},{3,7},{7,3},{8,12},{12,8},{9,1... | collective-permute-start | bytes 4718600 | tf_op jit(solution)/shard_map/ppermute | solution.py:448
  181.2 7.8 %copy-start.6 = (bf16[128,512]{1,0:T(8,128)(2,1)S(1)}, bf16[128,512]{1,0:T(8,128)(2,1)}, u32[]{:S(2)}) copy-start(bf16[128,512]{1,0:T(8,128)(2,1)} %get-tuple-element.9) | copy-start | bytes 393220
  182.3 31.9 %copy-start.4 = (bf16[576,512]{1,0:T(8,128)(2,1)S(1)}, bf16[576,512]{1,0:T(8,128)(2,1)}, u32[]{:S(2)}) copy-start(bf16[576,512]{1,0:T(8,128)(2,1)} %get-tuple-element.11) | copy-start | bytes 1769476
  182.3 23.1 %all-to-all-start.2 = ((bf16[64,8,1024]{2,1,0:T(8,128)(2,1)}), bf16[64,8,1024]{2,1,0:T(8,128)(2,1)S(1)}, u32[]{:S(2)}, u32[]{:S(2)}) async-start(bf16[64,8,1024]{2,1,0:T(8,128)(2,1)} %broadcast_in_dim.32), calls=%async_computation.2 | async-start | bytes 2097152 | tf_op jit(solution)/shard_map/all_to_all | solution.py:455
  187.6 26.6 %collective-permute-start.7 = (bf16[576,512]{1,0:T(8,128)(2,1)}, bf16[576,512]{1,0:T(8,128)(2,1)S(1)}, u32[]{:S(2)}, u32[]{:S(2)}) collective-permute-start(bf16[576,512]{1,0:T(8,128)(2,1)} %get-tuple-element.10), channel_id=1, source_target_pairs={{0,2},{2,4},{4,6},{6,8},{8,10},{10,12},{12,14},{14,16},{16,18},{18... | collective-permute-start | bytes 1769480 | tf_op jit(solution)/shard_map/ppermute | solution.py:480
  189.0 20.5 %collective-permute-start.5 = (bf16[36,512]{1,0:T(8,128)(2,1)S(1)}, bf16[36,512]{1,0:T(8,128)(2,1)S(1)}, u32[]{:S(2)}, u32[]{:S(2)}) collective-permute-start(bf16[36,512]{1,0:T(8,128)(2,1)S(1)} %get-tuple-element.20), channel_id=1, source_target_pairs={{0,3},{1,2},{2,5},{3,4},{4,7},{5,6},{6,9},{7,8},{8,11},{9,10},{10,... | collective-permute-start | bytes 110600 | tf_op jit(solution)/shard_map/ppermute | solution.py:482
  193.3 20.8 %collective-permute-start.6 = (bf16[36,512]{1,0:T(8,128)(2,1)S(1)}, bf16[36,512]{1,0:T(8,128)(2,1)S(1)}, u32[]{:S(2)}, u32[]{:S(2)}) collective-permute-start(bf16[36,512]{1,0:T(8,128)(2,1)S(1)} %get-tuple-element.21), channel_id=1, source_target_pairs={{0,1},{1,0},{2,3},{3,2},{4,5},{5,4},{6,7},{7,6},{8,9},{9,8},{10,11... | collective-permute-start | bytes 110600 | tf_op jit(solution)/shard_map/ppermute | solution.py:481
  205.4 16.1 %collective-permute-start.12 = (bf16[512,1024]{1,0:T(8,128)(2,1)S(1)}, bf16[512,1024]{1,0:T(8,128)(2,1)S(1)}, u32[]{:S(2)}, u32[]{:S(2)}) collective-permute-start(bf16[512,1024]{1,0:T(8,128)(2,1)S(1)} %bitcast.34), channel_id=1, source_target_pairs={{0,4},{4,0},{1,5},{5,1},{2,6},{6,2},{3,7},{7,3},{8,12},{12,8},{9,1... | collective-permute-start | bytes 3145736 | tf_op jit(solution)/shard_map/ppermute | solution.py:457
  214.9 5.0 %collective-permute-start.9 = (bf16[8,512]{1,0:T(8,128)(2,1)S(1)}, bf16[8,512]{1,0:T(8,128)(2,1)S(1)}, u32[]{:S(2)}, u32[]{:S(2)}) collective-permute-start(bf16[8,512]{1,0:T(8,128)(2,1)S(1)} %get-tuple-element.27), channel_id=1, source_target_pairs={{0,1},{1,0},{2,3},{3,2},{4,5},{5,4},{6,7},{7,6},{8,9},{9,8},{10,11... | collective-permute-start | bytes 24584 | tf_op jit(solution)/shard_map/ppermute | solution.py:467
  217.1 2.7 %collective-permute-start.10 = (bf16[8,512]{1,0:T(8,128)(2,1)S(1)}, bf16[8,512]{1,0:T(8,128)(2,1)S(1)}, u32[]{:S(2)}, u32[]{:S(2)}) collective-permute-start(bf16[8,512]{1,0:T(8,128)(2,1)S(1)} %get-tuple-element.27), channel_id=1, source_target_pairs={{0,2},{1,3},{2,0},{3,1},{4,6},{5,7},{6,4},{7,5},{8,10},{9,11},{10,... | collective-permute-start | bytes 24584 | tf_op jit(solution)/shard_map/ppermute | solution.py:467
  217.1 3.7 %collective-permute-start.11 = (bf16[8,512]{1,0:T(8,128)(2,1)S(1)}, bf16[8,512]{1,0:T(8,128)(2,1)S(1)}, u32[]{:S(2)}, u32[]{:S(2)}) collective-permute-start(bf16[8,512]{1,0:T(8,128)(2,1)S(1)} %get-tuple-element.27), channel_id=1, source_target_pairs={{0,3},{1,2},{2,1},{3,0},{4,7},{5,6},{6,5},{7,4},{8,11},{9,10},{10,... | collective-permute-start | bytes 24584 | tf_op jit(solution)/shard_map/ppermute | solution.py:467

commit v2 on v1

v2 whole, which is shorter than its diff:
```python
import functools

import jax
import jax.numpy as jnp
import numpy as np
from jax import lax
from jax.experimental import pallas as pl
from jax.experimental.pallas import tpu as pltpu
from jax.sharding import Mesh, PartitionSpec as P

D = 512
HEADS = 8
HDIM = 64
PSIDE = 4
WCOL = 6
ROWS = 12
HALF = 6
COLS = 48
WINDOWS = 8
LEVELS = 2
TOKENS = 1152
WTOK = 144
PATCHES = 576
LANES = 1152
STRIP = 48
EPS = 1e-05
BF = jnp.bfloat16
F32 = jnp.float32

NN = (((1,), (0,)), ((), ()))
NT = (((1,), (1,)), ((), ()))
TN = (((0,), (0,)), ((), ()))


def dot(a, b, dims=NN):
    return lax.dot_general(a, b, dims, preferred_element_type=F32)


def patch_index(w, j, c6):
    if w == WINDOWS - 1:
        return 252 + j * 3 + c6 if c6 < 3 else 267 + j * 3 + c6
    return w * 36 + j * WCOL + c6


def pixel_lane(b, patch):
    return 256 * b + patch if patch < 256 else 1024 + 32 * b + patch - 256


def edge_place():
    place = np.zeros((HALF, 128, 128), np.float32)
    for j in range(HALF):
        lane = np.arange(12)
        place[j, lane, j * 12 + lane] = 1
    return place


def pixel_place():
    main = np.zeros((HALF * PSIDE * COLS, LANES), np.float32)
    edge = np.zeros((128, 128), np.float32)
    for j in range(HALF):
        for c in range(COLS):
            for b in range(PSIDE):
                col = c - 3 if c >= 3 else COLS - 3 + c
                lane = pixel_lane(b, patch_index(col // WCOL, j, col % WCOL))
                if c >= 3:
                    main[(j * COLS + c) * PSIDE + b, lane] = 1
                else:
                    edge[j * 12 + c * PSIDE + b, lane - 1024] = 1
    return main, edge


def patch_place():
    main = np.zeros((2, PATCHES, 256), np.float32)
    rest = np.zeros((2, PSIDE, PATCHES, 128), np.float32)
    for half in range(2):
        for w in range(WINDOWS):
            for i in range(36):
                patch = patch_index(w, i // WCOL, i % WCOL)
                row = w * 72 + half * 36 + i
                if patch < 256:
                    main[half, row, patch] = 1
                else:
                    for b in range(PSIDE):
                        rest[half, b, row, 32 * b + patch - 256] = 1
    return main, rest


def token_place():
    place = np.zeros((TOKENS, TOKENS + 128), np.float32)
    for w in range(WINDOWS):
        for level in range(LEVELS):
            for half in range(2):
                for j in range(HALF):
                    for c6 in range(WCOL):
                        t = w * WTOK + level * 72 + half * 36 + j * WCOL + c6
                        c = w * WCOL + c6 + 3
                        if c < COLS:
                            place[t, half * PATCHES + (j * LEVELS + level) * COLS + c] = 1
                        else:
                            place[t, TOKENS + half * STRIP + (j * LEVELS + level) * 3 + c - COLS] = 1
    return place


def half_rows(pix_ref, half, j, lanes):
    rows = pix_ref[:, half * HALF + j, :, :, :lanes].astype(F32)
    merged = jnp.concatenate([rows[:, 0], rows[:, 1]], axis=1)
    return merged.reshape(merged.shape[0] * 8, lanes)


def strip_place():
    place = np.zeros((2 * STRIP, ROWS * LEVELS * 16), np.float32)
    for half in range(2):
        for i in range(HALF * LEVELS):
            for c in range(3):
                place[half * STRIP + i * 3 + c, (half * HALF * LEVELS + i) * 16 + c] = 1
    return place


def edge_kernel(
    pix_ref, cot_ref, weight_ref, place_ref, strip_ref, west_ref, ahead_ref, corner_ref, copies_ref
):
    size = (west_ref.shape[0] - 4 * STRIP) // 2
    for half in range(2):
        total = None
        for j in range(HALF):
            term = dot(half_rows(pix_ref, half, j, 128).astype(BF), place_ref[j])
            total = term if total is None else total + term
        west_ref[half * size : half * size + size, :] = total.astype(BF)
    strips = cot_ref[:, :, :16, :].reshape(ROWS * LEVELS * 16, D)
    strips = dot(strip_ref[...], strips).astype(BF)
    corner_ref[...] = strips[:STRIP]
    for t in range(4):
        at = 2 * size + t * STRIP
        west_ref[at : at + STRIP, :] = strips[STRIP:, 128 * t : 128 * t + 128]
    ahead_ref[...] = cot_ref[:HALF].reshape(PATCHES, D)
    copies_ref[...] = jnp.broadcast_to(weight_ref[...][None], copies_ref.shape)


def store_half(out_ref, half, lat, lanes, block):
    bands = out_ref.shape[0]
    if half == 1:
        out_ref[:, lat, :, lanes] = block
        return

    @pl.when(lat == 0)
    def _():
        out_ref[: bands - 1, 1, :, lanes] = block[1:]
        out_ref[bands - 1 :, 1, :, lanes] = block[:1]

    @pl.when(lat == 1)
    def _():
        out_ref[:, 0, :, lanes] = block


def pack_kernel(info_ref, pix_ref, main_ref, out_ref, rows_s):
    bands = out_ref.shape[0]
    size = bands * 8
    for half in range(2):
        for i in range(HALF // 2):
            pair = [half_rows(pix_ref, half, 2 * i + k, 4 * COLS) for k in range(2)]
            rows_s[half * size : half * size + size, 384 * i : 384 * i + 384] = jnp.concatenate(
                pair, axis=1
            ).astype(BF)
    for n in range(3):
        lanes = slice(384 * n, 384 * n + 384)
        block = dot(rows_s[...], main_ref[:, lanes])
        for half in range(2):
            part = block[half * size : half * size + size].reshape(bands, 8, 384).astype(BF)
            store_half(out_ref, half, info_ref[0], lanes, part)


def halo_kernel(info_ref, packed_ref, edge_ref, halo_ref, out_ref):
    bands = out_ref.shape[0]
    lat = info_ref[0]
    for half in range(2):
        rows = halo_ref[half * bands * 8 : (half + 1) * bands * 8, :]
        block = dot(rows, edge_ref[...]).reshape(bands, 8, 128)
        store_half(out_ref, half, lat, slice(0, 128), block.astype(BF))
    out_ref[...] = out_ref[...] + packed_ref[...]


def prepare_kernel(
    idx_ref,
    mix_ref,
    wown_ref,
    woth_ref,
    cot_ref,
    ahead_ref,
    halo_ref,
    corner_ref,
    tok_ref,
    wproj_ref,
    lw_ref,
    gb_ref,
    ga_ref,
):
    start = halo_ref.shape[0] - 4 * STRIP
    east = jnp.concatenate(
        [halo_ref[start + STRIP * t : start + STRIP * t + STRIP, :] for t in range(4)], axis=1
    )
    sides = jnp.concatenate([east, corner_ref[...], jnp.zeros((128 - 2 * STRIP, D), BF)], axis=0)
    gb = dot(tok_ref[:, :PATCHES], cot_ref[HALF:].reshape(PATCHES, D))
    gb = gb + dot(tok_ref[:, PATCHES:TOKENS], ahead_ref[...])
    gb = gb + dot(tok_ref[:, TOKENS:], sides)
    gb_ref[...] = gb.astype(BF)
    ga_ref[...] = dot(gb_ref[...], wproj_ref[...], NT).astype(BF)
    lane = lax.broadcasted_iota(jnp.int32, (256, 512), 1)
    for b in range(PSIDE):
        at = slice(256 * b, 256 * b + 256)
        idx = idx_ref[at, :]
        weight = dot(jnp.where(lane == idx, 1.0, 0.0).astype(BF), wown_ref[...])
        weight = weight + dot(jnp.where(lane + 512 == idx, 1.0, 0.0).astype(BF), woth_ref[...])
        for level in range(LEVELS):
            lw_ref[at, level * D : level * D + D] = (
                weight * mix_ref[:, level : level + 1]
            ).astype(BF)


def block_kernel(
    info_ref,
    recv_ref,
    lw_ref,
    gb_ref,
    ga_ref,
    idxr_ref,
    mix_ref,
    gain_ref,
    wqkv_ref,
    wproj_ref,
    mcol_ref,
    mrow_ref,
    pmain_ref,
    prest_ref,
    tokt_ref,
    top_ref,
    bot_ref,
    side_top_ref,
    side_bot_ref,
    gown_ref,
    goth_ref,
    a_s,
    at_s,
    t_s,
    unit_s,
    inv_s,
    norm_s,
    qkv_s,
    att_s,
    gp_s,
    bo_s,
    gt_s,
    gs_s,
):
    lat = info_ref[0]
    core = info_ref[1]
    gain = gain_ref[...]

    halves = []
    for half in range(2):
        src = lat if half == 0 else 1 - lat
        part = recv_ref[:, src].astype(F32)
        halves.append(part.reshape(256, LANES).astype(BF))
    for b in range(PSIDE):
        rows = None
        columns = None
        for half in range(2):
            main = halves[half][:, 256 * b : 256 * b + 256]
            rest = halves[half][:, 1024:1152]
            r = dot(pmain_ref[half], main, NT) + dot(prest_ref[half, b], rest, NT)
            c = dot(main, pmain_ref[half], NT) + dot(rest, prest_ref[half, b], NT)
            rows = r if rows is None else rows + r
            columns = c if columns is None else columns + c
        a_s[:, 256 * b : 256 * b + 256] = rows.astype(BF)
        at_s[256 * b : 256 * b + 256, :] = columns.astype(BF)
    for level in range(LEVELS):
        tok = dot(a_s[...], lw_ref[:, level * D : level * D + D]).astype(BF).astype(F32)
        for w in range(WINDOWS):
            t_s[w * WTOK + level * 72 : w * WTOK + level * 72 + 72, :] = tok[w * 72 : w * 72 + 72]

    def norm_step(w, carry):
        rows = pl.ds(pl.multiple_of(w * WTOK, WTOK), WTOK)
        x = t_s[rows, :]
        centred = x - jnp.mean(x, axis=-1, keepdims=True)
        inv = lax.rsqrt(jnp.mean(centred * centred, axis=-1, keepdims=True) + EPS)
        unit = centred * inv
        unit_s[rows, :] = unit
        inv_s[rows, :] = inv
        norm_s[rows, :] = (unit * gain).astype(BF)
        return carry

    lax.fori_loop(0, WINDOWS, norm_step, 0)
    for n in range(3):
        qkv_s[:, n * D : n * D + D] = dot(norm_s[...], wqkv_ref[:, n * D : n * D + D]).astype(BF)

    low = lax.broadcasted_iota(jnp.int32, (1, 128), 1) < HDIM
    lane = lax.broadcasted_iota(jnp.int32, (1, 256), 1) // HDIM
    keep = [jnp.where(lane == e, 1.0, 0.0).astype(BF) for e in range(4)]

    def by_head(x):
        return jnp.concatenate([x * keep[e] for e in range(4)], axis=0)

    def own_heads(x):
        left = jnp.where(low, x[:WTOK, :128], x[WTOK : 2 * WTOK, :128])
        right = jnp.where(low, x[2 * WTOK : 3 * WTOK, 128:], x[3 * WTOK :, 128:])
        return jnp.concatenate([left, right], axis=1).astype(BF)

    def window_step(w, carry):
        rows = pl.ds(pl.multiple_of(w * WTOK, WTOK), WTOK)
        same = mcol_ref[w] == mrow_ref[w]
        for part in range(2):
            at = part * 256
            keys = qkv_s[rows, D + at : D + at + 256]
            values = qkv_s[rows, 2 * D + at : 2 * D + at + 256]
            queries = by_head(qkv_s[rows, at : at + 256] * 0.125)
            grads = by_head(ga_ref[rows, at : at + 256])
            score = jnp.where(same, dot(keys, queries, NT), -1e30)
            ex = jnp.exp(score - jnp.max(score, axis=0, keepdims=True))
            prob = ex * (1.0 / jnp.sum(ex, axis=0, keepdims=True))
            gprob = dot(values, grads, NT)
            centred = gprob - jnp.sum(prob * gprob, axis=0, keepdims=True)
            gscore = (prob * centred).astype(BF)
            prob = prob.astype(BF)
            att_s[rows, at : at + 256] = own_heads(dot(prob, values, TN))
            gp_s[rows, at : at + 256] = own_heads(dot(gscore, keys * 0.125, TN))
            gp_s[rows, D + at : D + at + 256] = dot(gscore, queries).astype(BF)
            gp_s[rows, 2 * D + at : 2 * D + at + 256] = dot(prob, grads).astype(BF)
        return carry

    lax.fori_loop(0, WINDOWS, window_step, 0)

    branch = dot(att_s[...], wproj_ref[...]).astype(BF).astype(F32)
    bo_s[...] = (t_s[...] + branch).astype(BF)
    top_ref[...] = dot(tokt_ref[:PATCHES], bo_s[...]).astype(BF)
    bot_ref[...] = dot(tokt_ref[PATCHES:TOKENS], bo_s[...]).astype(BF)
    sides = dot(tokt_ref[TOKENS:], bo_s[...]).astype(BF)
    side_top_ref[...] = sides[:STRIP]
    side_bot_ref[...] = sides[STRIP : 2 * STRIP]

    for ref, which in ((gown_ref, core), (goth_ref, 1 - core)):
        at = pl.multiple_of(which * 768, 256)
        ref[:, 0:768] = dot(norm_s[...], gp_s[:, pl.ds(at, 768)], TN).astype(BF)
        at = pl.multiple_of(which * 256, 256)
        ref[:, 768:1024] = dot(att_s[...], gb_ref[:, pl.ds(at, 256)], TN).astype(BF)

    for w in range(WINDOWS):
        rows = slice(w * WTOK, w * WTOK + WTOK)
        h = dot(gp_s[rows, :], wqkv_ref[...], NT) * gain
        unit = unit_s[rows, :]
        shifted = inv_s[rows, :] * (
            h
            - jnp.mean(h, axis=-1, keepdims=True)
            - unit * jnp.mean(h * unit, axis=-1, keepdims=True)
        )
        total = (gb_ref[rows, :].astype(F32) + shifted.astype(BF).astype(F32)).astype(BF).astype(F32)
        for level in range(LEVELS):
            gt_s[level, w * 72 : w * 72 + 72, :] = total[level * 72 : level * 72 + 72]

    for b in range(PSIDE):
        slot = None
        for level in range(LEVELS):
            part = dot(at_s[256 * b : 256 * b + 256, :], gt_s[level].astype(BF))
            part = part * mix_ref[:, level : level + 1]
            slot = part if slot is None else slot + part
        gs_s[256 * b : 256 * b + 256, :] = slot.astype(BF)
    row = lax.broadcasted_iota(jnp.int32, (512, 1024), 0)
    idx = idxr_ref[...]
    for ref, offset in ((gown_ref, 0), (goth_ref, 512)):
        pick = jnp.where(row + offset == idx, 1.0, 0.0).astype(BF)
        ref[:, 1024:1536] = dot(pick, gs_s[...]).astype(BF)


def shape(*dims, dtype=BF):
    return jax.ShapeDtypeStruct(dims, dtype)


def cost(us):
    return pl.CostEstimate(flops=int(us * 1e9), bytes_accessed=0, transcendentals=0)


def vmem_call(kernel, outs, scratch=(), smem_first=False, count=0, mib=58, us=1):
    specs = [pl.BlockSpec(memory_space=pltpu.VMEM)] * count
    if smem_first:
        specs[0] = pl.BlockSpec(memory_space=pltpu.SMEM)
    many = isinstance(outs, (list, tuple))
    vm = pl.BlockSpec(memory_space=pltpu.VMEM)
    return pl.pallas_call(
        kernel,
        out_shape=outs,
        in_specs=specs,
        out_specs=[vm] * len(outs) if many else vm,
        scratch_shapes=list(scratch),
        compiler_params=pltpu.CompilerParams(vmem_limit_bytes=mib * 1024 * 1024),
        cost_estimate=cost(us),
    )


def per_device(
    counts,
    pixels,
    var_order,
    embed_weight,
    level_mix,
    norm_gain,
    w_qkv,
    w_proj,
    mask_ids,
    cotangent,
):
    chips, lats, lons = counts
    bands = chips * 2
    lat = lax.axis_index("lat")
    core = lax.axis_index("core")
    lon = lax.axis_index("lon")
    info = jnp.stack([lat, core]).astype(jnp.int32)
    rows_ring = ("chip", "core", "lat")
    everyone = ("chip", "core", "lat", "lon")
    ring = bands * lats
    group = ("chip", "lat", "lon")
    group_size = chips * lats * lons

    swap_lon = [(0, 1), (1, 0)]
    swap_core = [(0, 1), (1, 0)]

    main, edge = pixel_place()
    border, ahead, corner, copies = vmem_call(
        edge_kernel,
        [
            shape(2 * bands * 8 + 4 * STRIP, 128),
            shape(PATCHES, D),
            shape(STRIP, D),
            shape(chips, 32, D),
        ],
        count=5,
        us=3,
    )(
        pixels,
        cotangent,
        embed_weight.reshape(32, D),
        jnp.asarray(edge_place(), BF),
        jnp.asarray(strip_place(), BF),
    )
    halo = lax.ppermute(border, "lon", swap_lon)
    ahead = lax.ppermute(ahead, rows_ring, [(i, (i - 1) % ring) for i in range(ring)])
    corner = lax.ppermute(
        corner,
        everyone,
        [(i * 2 + k, ((i - 1) % ring) * 2 + 1 - k) for i in range(ring) for k in range(2)],
    )
    own_weight = lax.all_to_all(copies, "chip", split_axis=0, concat_axis=0, tiled=True)
    own_weight = own_weight.reshape(512, D)
    oth_weight = lax.ppermute(own_weight, "core", swap_core)

    packed = vmem_call(
        pack_kernel,
        shape(bands, 2, 8, LANES),
        [pltpu.VMEM((2 * bands * 8, LANES), BF)],
        smem_first=True,
        count=3,
        us=6,
    )(info, pixels, jnp.asarray(main, BF))
    halo, ahead, corner = lax.optimization_barrier((halo, ahead, corner))
    vm = pl.BlockSpec(memory_space=pltpu.VMEM)
    last = pl.BlockSpec((bands, 2, 8, 128), lambda i: (0, 0, 0, LANES // 128 - 1))
    packed = pl.pallas_call(
        halo_kernel,
        grid=(1,),
        out_shape=shape(bands, 2, 8, LANES),
        in_specs=[pl.BlockSpec(memory_space=pltpu.SMEM), last, vm, vm],
        out_specs=last,
        input_output_aliases={1: 0},
        compiler_params=pltpu.CompilerParams(vmem_limit_bytes=58 * 1024 * 1024),
        cost_estimate=cost(2),
    )(info, packed, jnp.asarray(edge, BF), halo)
    recv = lax.all_to_all(
        packed.reshape(bands * 2, 8, LANES), rows_ring, split_axis=0, concat_axis=0, tiled=True
    ).reshape(bands, 2, 8, LANES)

    device = var_order // 2
    base = jnp.where(device % 2 == core, 0, 512) + (device // 2) * 32 + (var_order % 2) * 16
    index = base[None, :, None] + (
        jnp.arange(4)[:, None, None] + 4 * jnp.arange(4)[None, None, :]
    )
    index = index.reshape(1024).astype(jnp.int32)
    slot_mix = jnp.repeat(level_mix[var_order], 4, axis=0)

    ids = mask_ids.reshape(2, HALF, LEVELS, WINDOWS, WCOL).transpose(3, 2, 0, 1, 4)
    ids = ids.reshape(WINDOWS, WTOK)

    tok = token_place()
    level_weight, grad_branch, grad_attended = vmem_call(
        prepare_kernel, [shape(1024, 1024), shape(TOKENS, D), shape(TOKENS, D)], count=10, us=8
    )(
        index[:, None],
        slot_mix,
        own_weight,
        oth_weight,
        cotangent,
        ahead,
        halo,
        corner,
        jnp.asarray(tok, BF),
        w_proj,
    )

    pmain, prest = patch_place()
    top, bot, side_top, side_bot, gown, goth = vmem_call(
        block_kernel,
        [
            shape(PATCHES, D),
            shape(PATCHES, D),
            shape(STRIP, D),
            shape(STRIP, D),
            shape(512, 1536),
            shape(512, 1536),
        ],
        [
            pltpu.VMEM((PATCHES, 1024), BF),
            pltpu.VMEM((1024, PATCHES), BF),
            pltpu.VMEM((TOKENS, D), F32),
            pltpu.VMEM((TOKENS, D), F32),
            pltpu.VMEM((TOKENS, 1), F32),
            pltpu.VMEM((TOKENS, D), BF),
            pltpu.VMEM((TOKENS, 3 * D), BF),
            pltpu.VMEM((TOKENS, D), BF),
            pltpu.VMEM((TOKENS, 3 * D), BF),
            pltpu.VMEM((TOKENS, D), BF),
            pltpu.VMEM((LEVELS, PATCHES, D), F32),
            pltpu.VMEM((1024, D), BF),
        ],
        smem_first=True,
        count=15,
        us=38,
    )(
        info,
        recv,
        level_weight,
        grad_branch,
        grad_attended,
        index[None, :],
        slot_mix,
        norm_gain[None, :],
        w_qkv,
        w_proj,
        ids[:, :, None],
        jnp.tile(ids, (1, 4))[:, None, :],
        jnp.asarray(pmain, BF),
        jnp.asarray(prest, BF),
        jnp.asarray(tok.T, BF),
    )

    from_core = lax.ppermute(goth, "core", swap_core)
    chip_sum = (gown.astype(F32) + from_core.astype(F32)).astype(BF)
    terms = lax.all_to_all(
        chip_sum.reshape(group_size, 8, 1536), group, split_axis=0, concat_axis=0, tiled=True
    )
    owned = jnp.sum(terms.astype(F32), axis=0).astype(BF)
    copies = jnp.broadcast_to(owned[None, :, :1024], (group_size, 8, 1024))
    mine = lax.all_to_all(copies, group, split_axis=0, concat_axis=0, tiled=True)
    mine = mine.reshape(512, 1024)

    embed_part = owned[:, 1024:]
    pieces = [embed_part]
    for dlat, dlon in ((0, 1), (1, 0), (1, 1)):
        pieces.append(
            lax.ppermute(
                embed_part,
                ("lat", "lon"),
                [(i * 2 + k, (i ^ dlat) * 2 + (k ^ dlon)) for i in range(2) for k in range(2)],
            )
        )
    stacked = jnp.stack(pieces)
    tile = lat * 2 + lon
    grad_embed = jnp.concatenate(
        [lax.dynamic_index_in_dim(stacked, tile ^ t, 0, keepdims=False) for t in range(4)], axis=0
    )
    grad_embed = grad_embed.reshape(2, 16, D).astype(F32)

    from_before = lax.ppermute(bot, rows_ring, [(i, (i + 1) % ring) for i in range(ring)])
    west = lax.ppermute(side_top, "lon", swap_lon)
    south_west = lax.ppermute(
        side_bot,
        everyone,
        [(i * 2 + k, ((i + 1) % ring) * 2 + 1 - k) for i in range(ring) for k in range(2)],
    )
    _, from_before, west, south_west = lax.optimization_barrier((owned, from_before, west, south_west))
    body = jnp.concatenate([from_before, top], axis=0).reshape(ROWS, LEVELS, COLS, D)
    sides = jnp.concatenate([south_west[:36], west[:36]], axis=0).reshape(ROWS, LEVELS, 3, D)
    block_out = jnp.concatenate([sides, body[:, :, 3:]], axis=2)

    mine, block_out, grad_embed = lax.optimization_barrier((mine, block_out, grad_embed))
    other = lax.ppermute(mine, "core", swap_core)
    first = jnp.where(core == 0, mine, other).astype(F32)
    second = jnp.where(core == 0, other, mine).astype(F32)
    grad_qkv = jnp.concatenate([first[:, :768], second[:, :768]], axis=1)
    grad_proj = jnp.concatenate([first[:, 768:], second[:, 768:]], axis=1)
    return (block_out, grad_embed, grad_qkv, grad_proj)


def solution(mesh):
    var, lats, lons = (mesh.shape[name] for name in ("var", "lat", "lon"))
    chips = var // 2
    fine = Mesh(mesh.devices.reshape(chips, 2, lats, lons), ("chip", "core", "lat", "lon"))
    both = ("chip", "core")
    in_specs = (
        P(None, "lat", both, None, "lon"),
        P(),
        P(both, None, None),
        P(),
        P(),
        P(),
        P(),
        P(("chip", "core", "lat"), None, "lon"),
        P(("chip", "core", "lat"), None, "lon", None),
    )
    out_specs = (P(("chip", "core", "lat"), None, "lon", None), P(both, None, None), P(), P())
    return jax.shard_map(
        functools.partial(per_device, (chips, lats, lons)),
        mesh=fine,
        in_specs=in_specs,
        out_specs=out_specs,
        check_vma=False,
    )
```

time: 228 us -> 169 us (0.74); the launches traced: 225 us -> 169 us
  blocking collectives: 58.8 us -> 0 us
  Pallas kernels: 83.6 us -> 58.2 us
  waiting for transfers between devices: 21.2 us -> 43.8 us
  starting transfers between devices: 42.2 us -> 47.1 us
    all_to_all x1 -> x0, blocking collectives: 31.2 us -> none  [per_device(): lax.all_to_all(chip_sum.reshape(group_size, 8, 1536), group, split_axis=0...]
    all_gather x1 -> x0, blocking collectives: 27.6 us -> none  [per_device(): lax.all_gather(embed_weight.reshape(32, D), 'chip', axis=0, tiled=True)]
    pallas_call x3 -> x5, Pallas kernels: 83.6 us -> 58.2 us  [the longest x1 38.2 us: per_device(): vmem_call(block_kernel, [shape(PATCHES, D), shape(PATCHES, D), shape(STRI...]
    all_to_all x0 -> x2, waiting for transfers between devices: none -> 23.4 us  [the longest x1 19.5 us: per_device(): lax.all_to_all(chip_sum.reshape(group_size, 8, 1536), group, split_axis=0...]
    all_to_all x0 -> x2, starting transfers between devices: none -> 14.5 us  [the longest x1 7.85 us: per_device(): lax.all_to_all(copies, 'chip', split_axis=0, concat_axis=0, tiled=True)]
    all_to_all x1, waiting for transfers between devices: 11.9 us -> 3.73 us  [per_device(): lax.all_to_all(copies, group, split_axis=0, concat_axis=0, tiled=True)]
    ppermute x3, waiting for transfers between devices: 1.02 us -> 6.3 us  [per_device(): lax.ppermute(embed_part, ('lat', 'lon'), [(i * 2 + k, (i ^ dlat) * 2 + (k...]
    all_to_all x1, waiting for transfers between devices: 0.01 us -> 4.83 us  [per_device(): lax.all_to_all(packed.reshape(bands * 2, 8, LANES), rows_ring, split_axis...]
  transfers between devices with their start and end apart: 15 -> 16, of which waited for: 5 -> 7; matrix products, arithmetic and copies ran while one was open for 4% -> 6% of each run, Pallas kernels for 3% -> 10%
where the time goes in v2:
time: 169 us
  Pallas kernels  58.2 us (34%)
  starting transfers between devices  47.1 us (28%)
  waiting for transfers between devices  43.8 us (26%)
  other arithmetic  9.78 us (6%)
  local copies, waits for them, and re-layouts  8.97 us (5%)
    pallas_call x1, Pallas kernels, per_device(): vmem_call(block_kernel, [shape(PATCHES, D), shape(PATCHES, D), shape(STRI...  38.2 us
    all_to_all x1, waiting for transfers between devices, per_device(): lax.all_to_all(chip_sum.reshape(group_size, 8, 1536), group, split_axis=0...  19.5 us
    pallas_call x1, Pallas kernels, per_device(): vmem_call(prepare_kernel, [shape(1024, 1024), shape(TOKENS, D), shape(TOK...  8.43 us
    all_to_all x1, starting transfers between devices, per_device(): lax.all_to_all(copies, 'chip', split_axis=0, concat_axis=0, tiled=True)  7.85 us
    all_to_all x1, starting transfers between devices, per_device(): lax.all_to_all(chip_sum.reshape(group_size, 8, 1536), group, split_axis=0...  6.63 us
    ppermute x3, waiting for transfers between devices, per_device(): lax.ppermute(embed_part, ('lat', 'lon'), [(i * 2 + k, (i ^ dlat) * 2 + (k...  6.3 us
    all_to_all x1, starting transfers between devices, per_device(): lax.all_to_all(packed.reshape(bands * 2, 8, LANES), rows_ring, split_axis...  6.26 us
    pallas_call x1, Pallas kernels, per_device(): vmem_call(pack_kernel, shape(bands, 2, 8, LANES), [pltpu.VMEM((2 * bands...  5.98 us
  transfers between devices with their start and end apart: 16, of which 7 were waited for; matrix products, arithmetic and copies ran while one was open for 6% of the time, Pallas kernels for 10%

profile of v2, /device:TPU:1, one launch (start us, length us, event | category | flops | bytes accessed | tf_op | source)
XLA Modules:
  0.0 168.7 jit_solution(8706539262683930588)
XLA Ops:
  0.6 3.3 %shard_map.193 = (bf16[704,128]{1,0:T(8,128)(2,1)}, bf16[576,512]{1,0:T(8,128)(2,1)}, bf16[48,512]{1,0:T(8,128)(2,1)}, bf16[16,32,512]{2,1,0:T(8,128)(2,1)}) custom-call(bf16[32,12,2,4,192]{4,3,2,1,0:T(4,128)(2,1)} %pix_ref.3, bf16[12,2,48,512]{3,2,1,0:T(8,128)(2,1)} %cot_ref.3, bf16[32,512]{1,0:T(8,128)(2,1)} %bitcast.42, ...), custom_call_target="tpu_custom_call" | custom-call | flops 3000000000 | tf_op jit(solution)/shard_map/pallas_call | solution.py:425
  3.9 2.6 %collective-permute-start.1 = (bf16[576,512]{1,0:T(8,128)(2,1)}, bf16[576,512]{1,0:T(8,128)(2,1)S(1)}, u32[]{:S(2)}, u32[]{:S(2)}) collective-permute-start(bf16[576,512]{1,0:T(8,128)(2,1)} %get-tuple-element.27), channel_id=1, source_target_pairs={{0,126},{2,0},{4,2},{6,4},{8,6},{10,8},{12,10},{14,12},{16,14},{18... | collective-permute-start | bytes 1769480 | tf_op jit(solution)/shard_map/ppermute | solution.py:443
  6.5 2.4 %collective-permute-start = (bf16[704,128]{1,0:T(8,128)(2,1)}, bf16[704,128]{1,0:T(8,128)(2,1)S(1)}, u32[]{:S(2)}, u32[]{:S(2)}) collective-permute-start(bf16[704,128]{1,0:T(8,128)(2,1)} %get-tuple-element.26), channel_id=1, source_target_pairs={{0,1},{1,0},{2,3},{3,2},{4,5},{5,4},{6,7},{7,6},{8,9},{9,8},{10,11... | collective-permute-start | bytes 540680 | tf_op jit(solution)/shard_map/ppermute | solution.py:442
  9.0 0.7 collective-permute-start.2
  9.6 7.9 %all-to-all-start.1 = ((bf16[16,32,512]{2,1,0:T(8,128)(2,1)}), bf16[16,32,512]{2,1,0:T(8,128)(2,1)S(1)}, u32[]{:S(2)}, u32[]{:S(2)}) async-start(bf16[16,32,512]{2,1,0:T(8,128)(2,1)} %get-tuple-element.30), calls=%async_computation.1 | async-start | bytes 1048576 | tf_op jit(solution)/shard_map/all_to_all | solution.py:449
  17.5 0.7 pad_add_fusion.info_ref
  18.2 6.0 %shard_map.192.packed_ref = bf16[32,2,8,1152]{3,2,1,0:T(8,128)(2,1)} custom-call(s32[2]{0:T(128)} %pad_add_fusion.info_ref, bf16[32,12,2,4,192]{4,3,2,1,0:T(4,128)(2,1)} %pix_ref.3, bf16[1152,1152]{1,0:T(8,128)(2,1)} %constant.94.clone.main_ref), custom_call_target="tpu_custom_call" | custom-call | flops 6000000000 | tf_op jit(solution)/shard_map/pallas_call | solution.py:453
  24.2 3.9 %all-to-all-done.1 = bf16[16,32,512]{2,1,0:T(8,128)(2,1)S(1)} async-done(((bf16[16,32,512]{2,1,0:T(8,128)(2,1)}), bf16[16,32,512]{2,1,0:T(8,128)(2,1)S(1)}, u32[]{:S(2)}, u32[]{:S(2)}) %all-to-all-start.1) | async-done | bytes 524320 | tf_op jit(solution)/shard_map/all_to_all | solution.py:449
  28.1 1.9 %collective-permute-start.3 = (bf16[512,512]{1,0:T(8,128)(2,1)S(1)}, bf16[512,512]{1,0:T(8,128)(2,1)S(1)}, u32[]{:S(2)}, u32[]{:S(2)}) collective-permute-start(bf16[512,512]{1,0:T(8,128)(2,1)S(1)} %bitcast.33), channel_id=1, source_target_pairs={{0,4},{4,0},{1,5},{5,1},{2,6},{6,2},{3,7},{7,3},{8,12},{12,8},{9,1... | collective-permute-start | bytes 1572872 | tf_op jit(solution)/shard_map/ppermute | solution.py:451
  30.0 0.0 collective-permute-done.2.corner_ref
  30.0 0.0 collective-permute-done.halo_ref
  30.0 0.0 collective-permute-done.1.ahead_ref
  30.0 0.7 copy-done.9
  30.7 2.2 %shard_map.194 = bf16[32,2,8,1152]{3,2,1,0:T(8,128)(2,1)} custom-call(s32[2]{0:T(128)} %pad_add_fusion.info_ref, bf16[32,2,8,1152]{3,2,1,0:T(8,128)(2,1)} %shard_map.192.packed_ref, bf16[128,128]{1,0:T(8,128)(2,1)} %constant.95.clone.edge_ref, bf16[704,128]{1,0:T(8,128)(2,1)} %copy-done.9), custom_call_target="tpu_custom_call", output_to_operand_aliasing={{}: (1, {})} | custom-call | flops 2000000000 | tf_op jit(solution)/shard_map/pallas_call | solution.py:464
  33.0 0.0 copy-start.3
  33.0 6.3 %all-to-all-start = ((bf16[64,8,1152]{2,1,0:T(8,128)(2,1)}), bf16[64,8,1152]{2,1,0:T(8,128)(2,1)S(1)}, u32[]{:S(2)}, u32[]{:S(2)}) async-start(bf16[64,8,1152]{2,1,0:T(8,128)(2,1)} %bitcast.32), calls=%async_computation | async-start | bytes 2359296 | tf_op jit(solution)/shard_map/all_to_all | solution.py:474
  39.3 0.0 copy-start.4
  39.3 0.1 broadcast_add_fusion
  39.4 1.0 add.114.idx_ref
  40.4 0.7 add.107.idxr_ref
  41.1 0.1 reshape.125
  41.2 1.0 broadcast_in_dim_reshape.6.mcol_ref
  42.2 0.1 tile.9
  42.3 0.1 copy.24
  42.5 0.7 tile.11.mrow_ref
  43.2 0.6 gather_fusion
  43.8 0.0 collective-permute-done.3.woth_ref
  43.8 0.7 broadcast_in_dim.26
  44.5 0.1 copy-done.8
  44.6 8.4 %shard_map.195 = (bf16[1024,1024]{1,0:T(8,128)(2,1)}, bf16[1152,512]{1,0:T(8,128)(2,1)}, bf16[1152,512]{1,0:T(8,128)(2,1)}) custom-call(s32[1024,1]{1,0:T(8,128)} %add.114.idx_ref, f32[256,2]{1,0:T(8,128)} %bitcast.36, bf16[512,512]{1,0:T(8,128)(2,1)} %bitcast.34, bf16[512,512]{1,0:T(8,128)(2,1)} %copy-done.8, bf16[12,2,48,512]{3,2,1,0:T(8,128)(2,1)} %cot_ref.3, ...), custom_call_target="tpu_custom_call" | custom-call | flops 8000000000 | tf_op jit(solution)/shard_map/pallas_call | solution.py:490
  53.1 4.8 %all-to-all-done = bf16[64,8,1152]{2,1,0:T(8,128)(2,1)S(1)} async-done(((bf16[64,8,1152]{2,1,0:T(8,128)(2,1)}), bf16[64,8,1152]{2,1,0:T(8,128)(2,1)S(1)}, u32[]{:S(2)}, u32[]{:S(2)}) %all-to-all-start) | async-done | bytes 1179680 | tf_op jit(solution)/shard_map/all_to_all | solution.py:474
  57.9 1.0 copy-done
  58.9 38.2 %shard_map.196 = (bf16[576,512]{1,0:T(8,128)(2,1)}, bf16[576,512]{1,0:T(8,128)(2,1)}, bf16[48,512]{1,0:T(8,128)(2,1)}, bf16[48,512]{1,0:T(8,128)(2,1)}, bf16[512...) custom-call(s32[2]{0:T(128)} %pad_add_fusion.info_ref, bf16[32,2,8,1152]{3,2,1,0:T(8,128)(2,1)} %bitcast.31, ...), custom_call_target="tpu_custom_call" | custom-call | flops 38000001024 | tf_op jit(solution)/shard_map/pallas_call | solution.py:506
  97.1 1.4 collective-permute-start.4
  98.5 3.2 %collective-permute-done.4 = bf16[512,1536]{1,0:T(8,128)(2,1)S(1)} collective-permute-done((bf16[512,1536]{1,0:T(8,128)(2,1)}, bf16[512,1536]{1,0:T(8,128)(2,1)S(1)}, u32[]{:S(2)}, u32[]{:S(2)}) %collective-permute-start.4) | collective-permute-done | bytes 1572896 | tf_op jit(solution)/shard_map/ppermute | solution.py:551
  101.8 2.9 %fusion = bf16[64,8,1536]{2,1,0:T(8,128)(2,1)} fusion(bf16[512,1536]{1,0:T(8,128)(2,1)S(1)} %collective-permute-done.4, bf16[512,1536]{1,0:T(8,128)(2,1)} %get-tuple-element.36), kind=kLoop, calls=%fused_computation.3 | loop fusion | flops 3145728 | bytes 4718592 | tf_op jit(solution)/shard_map/reshape | solution.py:554
  104.7 6.6 %all-to-all-start.2 = ((bf16[64,8,1536]{2,1,0:T(8,128)(2,1)}), bf16[64,8,1536]{2,1,0:T(8,128)(2,1)S(1)}, u32[]{:S(2)}, u32[]{:S(2)}) async-start(bf16[64,8,1536]{2,1,0:T(8,128)(2,1)} %fusion), calls=%async_computation.2 | async-start | bytes 3145728 | tf_op jit(solution)/shard_map/all_to_all | solution.py:553
  111.4 1.1 collective-permute-start.5
  112.5 2.4 %collective-permute-start.6 = (bf16[48,512]{1,0:T(8,128)(2,1)S(1)}, bf16[48,512]{1,0:T(8,128)(2,1)S(1)}, u32[]{:S(2)}, u32[]{:S(2)}) collective-permute-start(bf16[48,512]{1,0:T(8,128)(2,1)S(1)} %copy-done.11), channel_id=1, source_target_pairs={{0,1},{1,0},{2,3},{3,2},{4,5},{5,4},{6,7},{7,6},{8,9},{9,8},{10,11... | collective-permute-start | bytes 147464 | tf_op jit(solution)/shard_map/ppermute | solution.py:579
  114.8 1.8 %collective-permute-start.7 = (bf16[48,512]{1,0:T(8,128)(2,1)S(1)}, bf16[48,512]{1,0:T(8,128)(2,1)S(1)}, u32[]{:S(2)}, u32[]{:S(2)}) collective-permute-start(bf16[48,512]{1,0:T(8,128)(2,1)S(1)} %copy-done.10), channel_id=1, source_target_pairs={{0,3},{1,2},{2,5},{3,4},{4,7},{5,6},{6,9},{7,8},{8,11},{9,10},{10,... | collective-permute-start | bytes 147464 | tf_op jit(solution)/shard_map/ppermute | solution.py:580
  116.6 19.5 %all-to-all-done.2 = bf16[64,8,1536]{2,1,0:T(8,128)(2,1)S(1)} async-done(((bf16[64,8,1536]{2,1,0:T(8,128)(2,1)}), bf16[64,8,1536]{2,1,0:T(8,128)(2,1)S(1)}, u32[]{:S(2)}, u32[]{:S(2)}) %all-to-all-start.2) | async-done | bytes 1572896 | tf_op jit(solution)/shard_map/all_to_all | solution.py:553
  136.1 0.2 reduce_sum.12
  136.4 1.1 broadcast_in_dim.28
  137.5 5.0 %all-to-all-start.3 = ((bf16[64,8,1024]{2,1,0:T(8,128)(2,1)}), bf16[64,8,1024]{2,1,0:T(8,128)(2,1)S(1)}, u32[]{:S(2)}, u32[]{:S(2)}) async-start(bf16[64,8,1024]{2,1,0:T(8,128)(2,1)} %broadcast_in_dim.28), calls=%async_computation.3 | async-start | bytes 2097152 | tf_op jit(solution)/shard_map/all_to_all | solution.py:558
  142.5 2.5 %collective-permute-start.8 = (bf16[8,512]{1,0:T(8,128)(2,1)S(1)}, bf16[8,512]{1,0:T(8,128)(2,1)S(1)}, u32[]{:S(2)}, u32[]{:S(2)}) collective-permute-start(bf16[8,512]{1,0:T(8,128)(2,1)S(1)} %get-tuple-element.55), channel_id=1, source_target_pairs={{0,1},{1,0},{2,3},{3,2},{4,5},{5,4},{6,7},{7,6},{8,9},{9,8},{10,11... | collective-permute-start | bytes 24584 | tf_op jit(solution)/shard_map/ppermute | solution.py:565
  145.0 0.3 collective-permute-start.9
  145.3 0.0 collective-permute-done.6
  145.3 0.6 collective-permute-start.10
  145.9 0.0 collective-permute-done.5
  146.0 0.1 pad_maximum_fusion.1
  146.1 0.6 slice.39
  146.7 1.6 pad_maximum_fusion.2
  148.3 6.3 %collective-permute-done.8 = bf16[8,512]{1,0:T(8,128)(2,1)S(1)} collective-permute-done((bf16[8,512]{1,0:T(8,128)(2,1)S(1)}, bf16[8,512]{1,0:T(8,128)(2,1)S(1)}, u32[]{:S(2)}, u32[]{:S(2)}) %collective-permute-start.8) | collective-permute-done | bytes 8224 | tf_op jit(solution)/shard_map/ppermute | solution.py:565
  154.6 0.0 collective-permute-done.9
  154.6 0.0 collective-permute-done.10
  154.7 0.6 convert.2
  155.3 3.7 %all-to-all-done.3 = bf16[64,8,1024]{2,1,0:T(8,128)(2,1)S(1)} async-done(((bf16[64,8,1024]{2,1,0:T(8,128)(2,1)}), bf16[64,8,1024]{2,1,0:T(8,128)(2,1)S(1)}, u32[]{:S(2)}, u32[]{:S(2)}) %all-to-all-start.3) | async-done | bytes 1048608 | tf_op jit(solution)/shard_map/all_to_all | solution.py:558
  159.0 3.6 %collective-permute-start.11 = (bf16[512,1024]{1,0:T(8,128)(2,1)S(1)}, bf16[512,1024]{1,0:T(8,128)(2,1)S(1)}, u32[]{:S(2)}, u32[]{:S(2)}) collective-permute-start(bf16[512,1024]{1,0:T(8,128)(2,1)S(1)} %bitcast.29), channel_id=1, source_target_pairs={{0,4},{4,0},{1,5},{5,1},{2,6},{6,2},{3,7},{7,3},{8,12},{12,8},{9,1... | collective-permute-start | bytes 3145736 | tf_op jit(solution)/shard_map/ppermute | solution.py:591
  162.6 2.3 %collective-permute-done.11 = bf16[512,1024]{1,0:T(8,128)(2,1)S(1)} collective-permute-done((bf16[512,1024]{1,0:T(8,128)(2,1)S(1)}, bf16[512,1024]{1,0:T(8,128)(2,1)S(1)}, u32[]{:S(2)}, u32[]{:S(2)}) %collective-permute-start.11) | collective-permute-done | bytes 1048608 | tf_op jit(solution)/shard_map/ppermute | solution.py:591
  164.9 0.3 select_convert_fusion.1
  165.2 0.1 slice.41
  165.4 0.1 slice.42
  165.5 1.1 pad_maximum_fusion.3
  166.6 2.0 %pad_maximum_fusion = f32[512,1536]{1,0:T(8,128)} fusion(f32[512,768]{1,0:T(8,128)S(1)} %slice.42, f32[512,768]{1,0:T(8,128)S(1)} %slice.41), kind=kLoop, calls=%fused_computation.1 | loop fusion | flops 786432 | bytes 6291456 | tf_op jit(solution)/shard_map/concatenate | solution.py:594
  (39 shorter events, 0.3 us)
Async XLA Ops:
  3.9 26.1 %collective-permute-start.1 = (bf16[576,512]{1,0:T(8,128)(2,1)}, bf16[576,512]{1,0:T(8,128)(2,1)S(1)}, u32[]{:S(2)}, u32[]{:S(2)}) collective-permute-start(bf16[576,512]{1,0:T(8,128)(2,1)} %get-tuple-element.27), channel_id=1, source_target_pairs={{0,126},{2,0},{4,2},{6,4},{8,6},{10,8},{12,10},{14,12},{16,14},{18... | collective-permute-start | bytes 1769480 | tf_op jit(solution)/shard_map/ppermute | solution.py:443
  6.5 23.5 %collective-permute-start = (bf16[704,128]{1,0:T(8,128)(2,1)}, bf16[704,128]{1,0:T(8,128)(2,1)S(1)}, u32[]{:S(2)}, u32[]{:S(2)}) collective-permute-start(bf16[704,128]{1,0:T(8,128)(2,1)} %get-tuple-element.26), channel_id=1, source_target_pairs={{0,1},{1,0},{2,3},{3,2},{4,5},{5,4},{6,7},{7,6},{8,9},{9,8},{10,11... | collective-permute-start | bytes 540680 | tf_op jit(solution)/shard_map/ppermute | solution.py:442
  9.0 21.0 %collective-permute-start.2 = (bf16[48,512]{1,0:T(8,128)(2,1)}, bf16[48,512]{1,0:T(8,128)(2,1)S(1)}, u32[]{:S(2)}, u32[]{:S(2)}) collective-permute-start(bf16[48,512]{1,0:T(8,128)(2,1)} %get-tuple-element.28), channel_id=1, source_target_pairs={{0,127},{1,126},{2,1},{3,0},{4,3},{5,2},{6,5},{7,4},{8,7},{9,6},{1... | collective-permute-start | bytes 147464 | tf_op jit(solution)/shard_map/ppermute | solution.py:444
  9.6 18.4 %all-to-all-start.1 = ((bf16[16,32,512]{2,1,0:T(8,128)(2,1)}), bf16[16,32,512]{2,1,0:T(8,128)(2,1)S(1)}, u32[]{:S(2)}, u32[]{:S(2)}) async-start(bf16[16,32,512]{2,1,0:T(8,128)(2,1)} %get-tuple-element.30), calls=%async_computation.1 | async-start | bytes 1048576 | tf_op jit(solution)/shard_map/all_to_all | solution.py:449
  28.1 4.9 %copy-start.2 = (bf16[16,32,512]{2,1,0:T(8,128)(2,1)}, bf16[16,32,512]{2,1,0:T(8,128)(2,1)S(1)}, u32[]{:S(2)}) copy-start(bf16[16,32,512]{2,1,0:T(8,128)(2,1)S(1)} %all-to-all-done.1) | copy-start | bytes 1572868
  28.1 15.7 %collective-permute-start.3 = (bf16[512,512]{1,0:T(8,128)(2,1)S(1)}, bf16[512,512]{1,0:T(8,128)(2,1)S(1)}, u32[]{:S(2)}, u32[]{:S(2)}) collective-permute-start(bf16[512,512]{1,0:T(8,128)(2,1)S(1)} %bitcast.33), channel_id=1, source_target_pairs={{0,4},{4,0},{1,5},{5,1},{2,6},{6,2},{3,7},{7,3},{8,12},{12,8},{9,1... | collective-permute-start | bytes 1572872 | tf_op jit(solution)/shard_map/ppermute | solution.py:451
  30.0 3.0 %copy-start.12 = (bf16[48,512]{1,0:T(8,128)(2,1)}, bf16[48,512]{1,0:T(8,128)(2,1)S(1)}, u32[]{:S(2)}) copy-start(bf16[48,512]{1,0:T(8,128)(2,1)S(1)} %collective-permute-done.2.corner_ref) | copy-start | bytes 147460
  30.0 0.7 copy-start.9
  30.7 2.2 %copy-start.7 = (bf16[576,512]{1,0:T(8,128)(2,1)}, bf16[576,512]{1,0:T(8,128)(2,1)S(1)}, u32[]{:S(2)}) copy-start(bf16[576,512]{1,0:T(8,128)(2,1)S(1)} %collective-permute-done.1.ahead_ref) | copy-start | bytes 1769476
  32.9 6.3 %copy-start.5 = (s32[64]{0:T(128)S(1)}, s32[64]{0:T(128)}, u32[]{:S(2)}) copy-start(s32[64]{0:T(128)} %param.18) | copy-start | bytes 772
  33.0 8.1 %copy-start.3 = (s32[12,2,48]{2,1,0:T(2,128)S(1)}, s32[12,2,48]{2,1,0:T(2,128)}, u32[]{:S(2)}) copy-start(s32[12,2,48]{2,1,0:T(2,128)} %param.24) | copy-start | bytes 13828
  33.0 24.9 %all-to-all-start = ((bf16[64,8,1152]{2,1,0:T(8,128)(2,1)}), bf16[64,8,1152]{2,1,0:T(8,128)(2,1)S(1)}, u32[]{:S(2)}, u32[]{:S(2)}) async-start(bf16[64,8,1152]{2,1,0:T(8,128)(2,1)} %bitcast.32), calls=%async_computation | async-start | bytes 2359296 | tf_op jit(solution)/shard_map/all_to_all | solution.py:474
  39.3 3.1 %copy-start.4 = (f32[64,2]{0,1:T(2,128)S(1)}, f32[64,2]{0,1:T(2,128)}, u32[]{:S(2)}) copy-start(f32[64,2]{0,1:T(2,128)} %param.20) | copy-start | bytes 1540
  43.8 0.9 copy-start.8
  57.9 1.0 copy-start
  97.1 4.6 %collective-permute-start.4 = (bf16[512,1536]{1,0:T(8,128)(2,1)}, bf16[512,1536]{1,0:T(8,128)(2,1)S(1)}, u32[]{:S(2)}, u32[]{:S(2)}) collective-permute-start(bf16[512,1536]{1,0:T(8,128)(2,1)} %get-tuple-element.37), channel_id=1, source_target_pairs={{0,4},{4,0},{1,5},{5,1},{2,6},{6,2},{3,7},{7,3},{8,12},{12,8},{9,1... | collective-permute-start | bytes 4718600 | tf_op jit(solution)/shard_map/ppermute | solution.py:551
  104.7 6.6 %copy-start.6 = (bf16[576,512]{1,0:T(8,128)(2,1)S(1)}, bf16[576,512]{1,0:T(8,128)(2,1)}, u32[]{:S(2)}) copy-start(bf16[576,512]{1,0:T(8,128)(2,1)} %get-tuple-element.38) | copy-start | bytes 1769476
  104.7 7.7 %copy-start.11 = (bf16[48,512]{1,0:T(8,128)(2,1)S(1)}, bf16[48,512]{1,0:T(8,128)(2,1)}, u32[]{:S(2)}) copy-start(bf16[48,512]{1,0:T(8,128)(2,1)} %get-tuple-element.39) | copy-start | bytes 147460
  104.7 10.1 %copy-start.10 = (bf16[48,512]{1,0:T(8,128)(2,1)S(1)}, bf16[48,512]{1,0:T(8,128)(2,1)}, u32[]{:S(2)}) copy-start(bf16[48,512]{1,0:T(8,128)(2,1)} %get-tuple-element.40) | copy-start | bytes 147460
  104.7 31.4 %all-to-all-start.2 = ((bf16[64,8,1536]{2,1,0:T(8,128)(2,1)}), bf16[64,8,1536]{2,1,0:T(8,128)(2,1)S(1)}, u32[]{:S(2)}, u32[]{:S(2)}) async-start(bf16[64,8,1536]{2,1,0:T(8,128)(2,1)} %fusion), calls=%async_computation.2 | async-start | bytes 3145728 | tf_op jit(solution)/shard_map/all_to_all | solution.py:553
  111.4 34.6 %collective-permute-start.5 = (bf16[576,512]{1,0:T(8,128)(2,1)S(1)}, bf16[576,512]{1,0:T(8,128)(2,1)S(1)}, u32[]{:S(2)}, u32[]{:S(2)}) collective-permute-start(bf16[576,512]{1,0:T(8,128)(2,1)S(1)} %copy-done.6), channel_id=1, source_target_pairs={{0,2},{2,4},{4,6},{6,8},{8,10},{10,12},{12,14},{14,16},{16,18},{18... | collective-permute-start | bytes 1769480 | tf_op jit(solution)/shard_map/ppermute | solution.py:578
  112.5 32.9 %collective-permute-start.6 = (bf16[48,512]{1,0:T(8,128)(2,1)S(1)}, bf16[48,512]{1,0:T(8,128)(2,1)S(1)}, u32[]{:S(2)}, u32[]{:S(2)}) collective-permute-start(bf16[48,512]{1,0:T(8,128)(2,1)S(1)} %copy-done.11), channel_id=1, source_target_pairs={{0,1},{1,0},{2,3},{3,2},{4,5},{5,4},{6,7},{7,6},{8,9},{9,8},{10,11... | collective-permute-start | bytes 147464 | tf_op jit(solution)/shard_map/ppermute | solution.py:579
  114.8 31.1 %collective-permute-start.7 = (bf16[48,512]{1,0:T(8,128)(2,1)S(1)}, bf16[48,512]{1,0:T(8,128)(2,1)S(1)}, u32[]{:S(2)}, u32[]{:S(2)}) collective-permute-start(bf16[48,512]{1,0:T(8,128)(2,1)S(1)} %copy-done.10), channel_id=1, source_target_pairs={{0,3},{1,2},{2,5},{3,4},{4,7},{5,6},{6,9},{7,8},{8,11},{9,10},{10,... | collective-permute-start | bytes 147464 | tf_op jit(solution)/shard_map/ppermute | solution.py:580
  137.5 8.6 %copy-start.1 = (bf16[576,512]{1,0:T(8,128)(2,1)S(1)}, bf16[576,512]{1,0:T(8,128)(2,1)}, u32[]{:S(2)}) copy-start(bf16[576,512]{1,0:T(8,128)(2,1)} %get-tuple-element.44) | copy-start | bytes 1769476
  137.5 21.6 %all-to-all-start.3 = ((bf16[64,8,1024]{2,1,0:T(8,128)(2,1)}), bf16[64,8,1024]{2,1,0:T(8,128)(2,1)S(1)}, u32[]{:S(2)}, u32[]{:S(2)}) async-start(bf16[64,8,1024]{2,1,0:T(8,128)(2,1)} %broadcast_in_dim.28), calls=%async_computation.3 | async-start | bytes 2097152 | tf_op jit(solution)/shard_map/all_to_all | solution.py:558
  142.5 12.1 %collective-permute-start.8 = (bf16[8,512]{1,0:T(8,128)(2,1)S(1)}, bf16[8,512]{1,0:T(8,128)(2,1)S(1)}, u32[]{:S(2)}, u32[]{:S(2)}) collective-permute-start(bf16[8,512]{1,0:T(8,128)(2,1)S(1)} %get-tuple-element.55), channel_id=1, source_target_pairs={{0,1},{1,0},{2,3},{3,2},{4,5},{5,4},{6,7},{7,6},{8,9},{9,8},{10,11... | collective-permute-start | bytes 24584 | tf_op jit(solution)/shard_map/ppermute | solution.py:565
  145.0 9.6 %collective-permute-start.9 = (bf16[8,512]{1,0:T(8,128)(2,1)S(1)}, bf16[8,512]{1,0:T(8,128)(2,1)S(1)}, u32[]{:S(2)}, u32[]{:S(2)}) collective-permute-start(bf16[8,512]{1,0:T(8,128)(2,1)S(1)} %get-tuple-element.55), channel_id=1, source_target_pairs={{0,2},{1,3},{2,0},{3,1},{4,6},{5,7},{6,4},{7,5},{8,10},{9,11},{10,... | collective-permute-start | bytes 24584 | tf_op jit(solution)/shard_map/ppermute | solution.py:565
  145.3 9.3 %collective-permute-start.10 = (bf16[8,512]{1,0:T(8,128)(2,1)S(1)}, bf16[8,512]{1,0:T(8,128)(2,1)S(1)}, u32[]{:S(2)}, u32[]{:S(2)}) collective-permute-start(bf16[8,512]{1,0:T(8,128)(2,1)S(1)} %get-tuple-element.55), channel_id=1, source_target_pairs={{0,3},{1,2},{2,1},{3,0},{4,7},{5,6},{6,5},{7,4},{8,11},{9,10},{10,... | collective-permute-start | bytes 24584 | tf_op jit(solution)/shard_map/ppermute | solution.py:565
  159.0 5.9 %collective-permute-start.11 = (bf16[512,1024]{1,0:T(8,128)(2,1)S(1)}, bf16[512,1024]{1,0:T(8,128)(2,1)S(1)}, u32[]{:S(2)}, u32[]{:S(2)}) collective-permute-start(bf16[512,1024]{1,0:T(8,128)(2,1)S(1)} %bitcast.29), channel_id=1, source_target_pairs={{0,4},{4,0},{1,5},{5,1},{2,6},{6,2},{3,7},{7,3},{8,12},{12,8},{9,1... | collective-permute-start | bytes 3145736 | tf_op jit(solution)/shard_map/ppermute | solution.py:591

commit v3 on v2

--- a/solution.py
+++ b/solution.py
@@ -132,7 +132,7 @@
     for t in range(4):
         at = 2 * size + t * STRIP
         west_ref[at : at + STRIP, :] = strips[STRIP:, 128 * t : 128 * t + 128]
-    ahead_ref[...] = cot_ref[:HALF].reshape(PATCHES, D)
+    ahead_ref[...] = cot_ref[:HALF]
     copies_ref[...] = jnp.broadcast_to(weight_ref[...][None], copies_ref.shape)
 
 
@@ -152,7 +152,10 @@
         out_ref[:, 0, :, lanes] = block
 
 
-def pack_kernel(info_ref, pix_ref, main_ref, out_ref, rows_s):
+def pack_kernel(pix_ref, edge_ref, halo_ref, main_ref, out_ref, rows_s, main_s, sem):
+    move = pltpu.make_async_copy(main_ref, main_s, sem)
+    move.start()
+    lat = lax.axis_index("lat")
     bands = out_ref.shape[0]
     size = bands * 8
     for half in range(2):
@@ -161,22 +164,16 @@
             rows_s[half * size : half * size + size, 384 * i : 384 * i + 384] = jnp.concatenate(
                 pair, axis=1
             ).astype(BF)
+    move.wait()
     for n in range(3):
         lanes = slice(384 * n, 384 * n + 384)
-        block = dot(rows_s[...], main_ref[:, lanes])
+        block = dot(rows_s[...], main_s[:, lanes])
+        if n == 2:
+            halo = dot(halo_ref[: 2 * size, :], edge_ref[...])
+            block = jnp.concatenate([block[:, :256], block[:, 256:] + halo], axis=1)
         for half in range(2):
             part = block[half * size : half * size + size].reshape(bands, 8, 384).astype(BF)
-            store_half(out_ref, half, info_ref[0], lanes, part)
-
-
-def halo_kernel(info_ref, packed_ref, edge_ref, halo_ref, out_ref):
-    bands = out_ref.shape[0]
-    lat = info_ref[0]
-    for half in range(2):
-        rows = halo_ref[half * bands * 8 : (half + 1) * bands * 8, :]
-        block = dot(rows, edge_ref[...]).reshape(bands, 8, 128)
-        store_half(out_ref, half, lat, slice(0, 128), block.astype(BF))
-    out_ref[...] = out_ref[...] + packed_ref[...]
+            store_half(out_ref, half, lat, lanes, part)
 
 
 def prepare_kernel(
@@ -200,7 +197,7 @@
     )
     sides = jnp.concatenate([east, corner_ref[...], jnp.zeros((128 - 2 * STRIP, D), BF)], axis=0)
     gb = dot(tok_ref[:, :PATCHES], cot_ref[HALF:].reshape(PATCHES, D))
-    gb = gb + dot(tok_ref[:, PATCHES:TOKENS], ahead_ref[...])
+    gb = gb + dot(tok_ref[:, PATCHES:TOKENS], ahead_ref[...].reshape(PATCHES, D))
     gb = gb + dot(tok_ref[:, TOKENS:], sides)
     gb_ref[...] = gb.astype(BF)
     ga_ref[...] = dot(gb_ref[...], wproj_ref[...], NT).astype(BF)
@@ -217,27 +214,35 @@
 
 
 def block_kernel(
-    info_ref,
     recv_ref,
-    lw_ref,
-    gb_ref,
-    ga_ref,
     idxr_ref,
     mix_ref,
     gain_ref,
-    wqkv_ref,
-    wproj_ref,
     mcol_ref,
     mrow_ref,
     pmain_ref,
     prest_ref,
+    lw_far,
+    wqkv_far,
+    gb_far,
+    ga_far,
+    wproj_far,
+    tokt_far,
+    top_far,
+    bot_far,
+    side_top_ref,
+    side_bot_ref,
+    gown_far,
+    goth_far,
+    lw_ref,
+    wqkv_ref,
+    gb_ref,
+    ga_ref,
+    wproj_ref,
     tokt_ref,
     top_ref,
     bot_ref,
-    side_top_ref,
-    side_bot_ref,
-    gown_ref,
-    goth_ref,
+    g_ref,
     a_s,
     at_s,
     t_s,
@@ -250,9 +255,23 @@
     bo_s,
     gt_s,
     gs_s,
+    sem_in,
+    sem_out,
 ):
-    lat = info_ref[0]
-    core = info_ref[1]
+    far = [lw_far, wqkv_far, gb_far, ga_far, wproj_far, tokt_far]
+    near = [lw_ref, wqkv_ref, gb_ref, ga_ref, wproj_ref, tokt_ref]
+    moves = [pltpu.make_async_copy(x, y, sem_in.at[i]) for i, (x, y) in enumerate(zip(far, near))]
+    for move in moves:
+        move.start()
+    sent = []
+
+    def send(source, target):
+        move = pltpu.make_async_copy(source, target, sem_out.at[len(sent)])
+        move.start()
+        sent.append(move)
+
+    lat = lax.axis_index("lat")
+    core = lax.axis_index("core")
     gain = gain_ref[...]
 
     halves = []
@@ -261,17 +280,16 @@
         part = recv_ref[:, src].astype(F32)
         halves.append(part.reshape(256, LANES).astype(BF))
     for b in range(PSIDE):
-        rows = None
-        columns = None
+        place = []
+        pixels = []
         for half in range(2):
-            main = halves[half][:, 256 * b : 256 * b + 256]
-            rest = halves[half][:, 1024:1152]
-            r = dot(pmain_ref[half], main, NT) + dot(prest_ref[half, b], rest, NT)
-            c = dot(main, pmain_ref[half], NT) + dot(rest, prest_ref[half, b], NT)
-            rows = r if rows is None else rows + r
-            columns = c if columns is None else columns + c
-        a_s[:, 256 * b : 256 * b + 256] = rows.astype(BF)
-        at_s[256 * b : 256 * b + 256, :] = columns.astype(BF)
+            place += [pmain_ref[half], prest_ref[half, b]]
+            pixels += [halves[half][:, 256 * b : 256 * b + 256], halves[half][:, 1024:1152]]
+        place = jnp.concatenate(place, axis=1)
+        pixels = jnp.concatenate(pixels, axis=1)
+        a_s[:, 256 * b : 256 * b + 256] = dot(place, pixels, NT).astype(BF)
+        at_s[256 * b : 256 * b + 256, :] = dot(pixels, place, NT).astype(BF)
+    moves[0].wait()
     for level in range(LEVELS):
         tok = dot(a_s[...], lw_ref[:, level * D : level * D + D]).astype(BF).astype(F32)
         for w in range(WINDOWS):
@@ -289,9 +307,12 @@
         return carry
 
     lax.fori_loop(0, WINDOWS, norm_step, 0)
+    moves[1].wait()
     for n in range(3):
         qkv_s[:, n * D : n * D + D] = dot(norm_s[...], wqkv_ref[:, n * D : n * D + D]).astype(BF)
 
+    for move in moves[2:]:
+        move.wait()
     low = lax.broadcasted_iota(jnp.int32, (1, 128), 1) < HDIM
     lane = lax.broadcasted_iota(jnp.int32, (1, 256), 1) // HDIM
     keep = [jnp.where(lane == e, 1.0, 0.0).astype(BF) for e in range(4)]
@@ -307,19 +328,25 @@
     def window_step(w, carry):
         rows = pl.ds(pl.multiple_of(w * WTOK, WTOK), WTOK)
         same = mcol_ref[w] == mrow_ref[w]
+        state = []
         for part in range(2):
             at = part * 256
             keys = qkv_s[rows, D + at : D + at + 256]
             values = qkv_s[rows, 2 * D + at : 2 * D + at + 256]
             queries = by_head(qkv_s[rows, at : at + 256] * 0.125)
             grads = by_head(ga_ref[rows, at : at + 256])
-            score = jnp.where(same, dot(keys, queries, NT), -1e30)
+            state.append((keys, values, queries, grads, dot(keys, queries, NT), dot(values, grads, NT)))
+        ready = []
+        for keys, values, queries, grads, score, gprob in state:
+            score = jnp.where(same, score, -1e30)
             ex = jnp.exp(score - jnp.max(score, axis=0, keepdims=True))
             prob = ex * (1.0 / jnp.sum(ex, axis=0, keepdims=True))
-            gprob = dot(values, grads, NT)
             centred = gprob - jnp.sum(prob * gprob, axis=0, keepdims=True)
-            gscore = (prob * centred).astype(BF)
-            prob = prob.astype(BF)
+            ready.append(((prob * centred).astype(BF), prob.astype(BF)))
+        for part in range(2):
+            at = part * 256
+            keys, values, queries, grads = state[part][:4]
+            gscore, prob = ready[part]
             att_s[rows, at : at + 256] = own_heads(dot(prob, values, TN))
             gp_s[rows, at : at + 256] = own_heads(dot(gscore, keys * 0.125, TN))
             gp_s[rows, D + at : D + at + 256] = dot(gscore, queries).astype(BF)
@@ -332,18 +359,23 @@
     bo_s[...] = (t_s[...] + branch).astype(BF)
     top_ref[...] = dot(tokt_ref[:PATCHES], bo_s[...]).astype(BF)
     bot_ref[...] = dot(tokt_ref[PATCHES:TOKENS], bo_s[...]).astype(BF)
+    send(top_ref, top_far)
+    send(bot_ref, bot_far)
     sides = dot(tokt_ref[TOKENS:], bo_s[...]).astype(BF)
     side_top_ref[...] = sides[:STRIP]
     side_bot_ref[...] = sides[STRIP : 2 * STRIP]
 
-    for ref, which in ((gown_ref, core), (goth_ref, 1 - core)):
-        at = pl.multiple_of(which * 768, 256)
-        ref[:, 0:768] = dot(norm_s[...], gp_s[:, pl.ds(at, 768)], TN).astype(BF)
-        at = pl.multiple_of(which * 256, 256)
-        ref[:, 768:1024] = dot(att_s[...], gb_ref[:, pl.ds(at, 256)], TN).astype(BF)
-
-    for w in range(WINDOWS):
-        rows = slice(w * WTOK, w * WTOK + WTOK)
+    total = dot(norm_s[...], gp_s[...], TN)
+    for part in range(2):
+        g_ref[core ^ part, :, 0:768] = total[:, 768 * part : 768 * part + 768].astype(BF)
+    total = dot(att_s[...], gb_ref[...], TN)
+    for part in range(2):
+        g_ref[core ^ part, :, 768:1024] = total[:, 256 * part : 256 * part + 256].astype(BF)
+    for i, target in enumerate((gown_far, goth_far)):
+        send(g_ref.at[i, :, :1024], target.at[:, :1024])
+
+    for part in range(2):
+        rows = slice(part * PATCHES, part * PATCHES + PATCHES)
         h = dot(gp_s[rows, :], wqkv_ref[...], NT) * gain
         unit = unit_s[rows, :]
         shifted = inv_s[rows, :] * (
@@ -352,21 +384,28 @@
             - unit * jnp.mean(h * unit, axis=-1, keepdims=True)
         )
         total = (gb_ref[rows, :].astype(F32) + shifted.astype(BF).astype(F32)).astype(BF).astype(F32)
-        for level in range(LEVELS):
-            gt_s[level, w * 72 : w * 72 + 72, :] = total[level * 72 : level * 72 + 72]
-
+        for i in range(WINDOWS // 2):
+            w = part * (WINDOWS // 2) + i
+            for level in range(LEVELS):
+                at = i * WTOK + level * 72
+                gt_s[level, w * 72 : w * 72 + 72, :] = total[at : at + 72]
+
+    grads = [gt_s[level].astype(BF) for level in range(LEVELS)]
     for b in range(PSIDE):
         slot = None
         for level in range(LEVELS):
-            part = dot(at_s[256 * b : 256 * b + 256, :], gt_s[level].astype(BF))
+            part = dot(at_s[256 * b : 256 * b + 256, :], grads[level])
             part = part * mix_ref[:, level : level + 1]
             slot = part if slot is None else slot + part
         gs_s[256 * b : 256 * b + 256, :] = slot.astype(BF)
     row = lax.broadcasted_iota(jnp.int32, (512, 1024), 0)
     idx = idxr_ref[...]
-    for ref, offset in ((gown_ref, 0), (goth_ref, 512)):
-        pick = jnp.where(row + offset == idx, 1.0, 0.0).astype(BF)
-        ref[:, 1024:1536] = dot(pick, gs_s[...]).astype(BF)
+    for i, target in ((1, goth_far), (0, gown_far)):
+        pick = jnp.where(row + 512 * i == idx, 1.0, 0.0).astype(BF)
+        g_ref[i, :, 1024:1536] = dot(pick, gs_s[...]).astype(BF)
+        send(g_ref.at[i, :, 1024:], target.at[:, 1024:])
+    for move in sent:
+        move.wait()
 
 
 def shape(*dims, dtype=BF):
@@ -377,17 +416,16 @@
     return pl.CostEstimate(flops=int(us * 1e9), bytes_accessed=0, transcendentals=0)
 
 
-def vmem_call(kernel, outs, scratch=(), smem_first=False, count=0, mib=58, us=1):
-    specs = [pl.BlockSpec(memory_space=pltpu.VMEM)] * count
-    if smem_first:
-        specs[0] = pl.BlockSpec(memory_space=pltpu.SMEM)
+def vmem_call(kernel, outs, scratch=(), count=0, far=(), far_out=(), mib=58, us=1):
+    def spec(is_far):
+        return pl.BlockSpec(memory_space=pl.ANY if is_far else pltpu.VMEM)
+
     many = isinstance(outs, (list, tuple))
-    vm = pl.BlockSpec(memory_space=pltpu.VMEM)
     return pl.pallas_call(
         kernel,
         out_shape=outs,
-        in_specs=specs,
-        out_specs=[vm] * len(outs) if many else vm,
+        in_specs=[spec(i in far) for i in range(count)],
+        out_specs=[spec(i in far_out) for i in range(len(outs))] if many else spec(False),
         scratch_shapes=list(scratch),
         compiler_params=pltpu.CompilerParams(vmem_limit_bytes=mib * 1024 * 1024),
         cost_estimate=cost(us),
@@ -411,7 +449,6 @@
     lat = lax.axis_index("lat")
     core = lax.axis_index("core")
     lon = lax.axis_index("lon")
-    info = jnp.stack([lat, core]).astype(jnp.int32)
     rows_ring = ("chip", "core", "lat")
     everyone = ("chip", "core", "lat", "lon")
     ring = bands * lats
@@ -426,7 +463,7 @@
         edge_kernel,
         [
             shape(2 * bands * 8 + 4 * STRIP, 128),
-            shape(PATCHES, D),
+            shape(HALF, LEVELS, COLS, D),
             shape(STRIP, D),
             shape(chips, 32, D),
         ],
@@ -453,24 +490,16 @@
     packed = vmem_call(
         pack_kernel,
         shape(bands, 2, 8, LANES),
-        [pltpu.VMEM((2 * bands * 8, LANES), BF)],
-        smem_first=True,
-        count=3,
+        [
+            pltpu.VMEM((2 * bands * 8, LANES), BF),
+            pltpu.VMEM((LANES, LANES), BF),
+            pltpu.SemaphoreType.DMA,
+        ],
+        count=4,
+        far=(3,),
         us=6,
-    )(info, pixels, jnp.asarray(main, BF))
-    halo, ahead, corner = lax.optimization_barrier((halo, ahead, corner))
-    vm = pl.BlockSpec(memory_space=pltpu.VMEM)
-    last = pl.BlockSpec((bands, 2, 8, 128), lambda i: (0, 0, 0, LANES // 128 - 1))
-    packed = pl.pallas_call(
-        halo_kernel,
-        grid=(1,),
-        out_shape=shape(bands, 2, 8, LANES),
-        in_specs=[pl.BlockSpec(memory_space=pltpu.SMEM), last, vm, vm],
-        out_specs=last,
-        input_output_aliases={1: 0},
-        compiler_params=pltpu.CompilerParams(vmem_limit_bytes=58 * 1024 * 1024),
-        cost_estimate=cost(2),
-    )(info, packed, jnp.asarray(edge, BF), halo)
+    )(pixels, jnp.asarray(edge, BF), halo, jnp.asarray(main, BF))
+    packed, ahead, corner = lax.optimization_barrier((packed, ahead, corner))
     recv = lax.all_to_all(
         packed.reshape(bands * 2, 8, LANES), rows_ring, split_axis=0, concat_axis=0, tiled=True
     ).reshape(bands, 2, 8, LANES)
@@ -514,6 +543,15 @@
             shape(512, 1536),
         ],
         [
+            pltpu.VMEM((1024, 1024), BF),
+            pltpu.VMEM((D, 3 * D), BF),
+            pltpu.VMEM((TOKENS, D), BF),
+            pltpu.VMEM((TOKENS, D), BF),
+            pltpu.VMEM((D, D), BF),
+            pltpu.VMEM((TOKENS + 128, TOKENS), BF),
+            pltpu.VMEM((PATCHES, D), BF),
+            pltpu.VMEM((PATCHES, D), BF),
+            pltpu.VMEM((2, 512, 1536), BF),
             pltpu.VMEM((PATCHES, 1024), BF),
             pltpu.VMEM((1024, PATCHES), BF),
             pltpu.VMEM((TOKENS, D), F32),
@@ -526,25 +564,27 @@
             pltpu.VMEM((TOKENS, D), BF),
             pltpu.VMEM((LEVELS, PATCHES, D), F32),
             pltpu.VMEM((1024, D), BF),
+            pltpu.SemaphoreType.DMA((6,)),
+            pltpu.SemaphoreType.DMA((6,)),
         ],
-        smem_first=True,
-        count=15,
+        count=14,
+        far=range(8, 14),
+        far_out=(0, 1, 4, 5),
         us=38,
     )(
-        info,
         recv,
-        level_weight,
-        grad_branch,
-        grad_attended,
         index[None, :],
         slot_mix,
         norm_gain[None, :],
-        w_qkv,
-        w_proj,
         ids[:, :, None],
         jnp.tile(ids, (1, 4))[:, None, :],
         jnp.asarray(pmain, BF),
         jnp.asarray(prest, BF),
+        level_weight,
+        w_qkv,
+        grad_branch,
+        grad_attended,
+        w_proj,
         jnp.asarray(tok.T, BF),
     )
 
@@ -589,10 +629,12 @@
 
     mine, block_out, grad_embed = lax.optimization_barrier((mine, block_out, grad_embed))
     other = lax.ppermute(mine, "core", swap_core)
-    first = jnp.where(core == 0, mine, other).astype(F32)
-    second = jnp.where(core == 0, other, mine).astype(F32)
-    grad_qkv = jnp.concatenate([first[:, :768], second[:, :768]], axis=1)
-    grad_proj = jnp.concatenate([first[:, 768:], second[:, 768:]], axis=1)
+    grads = []
+    for lanes, width in ((slice(0, 768), 768), (slice(768, 1024), 256)):
+        own = jnp.concatenate([mine[:, lanes]] * 2, axis=1).astype(F32)
+        rest = other[:, lanes].astype(F32)
+        grads.append(lax.dynamic_update_slice(own, rest, (0, (1 - core) * width)))
+    grad_qkv, grad_proj = grads
     return (block_out, grad_embed, grad_qkv, grad_proj)
 
 

time: 169 us -> 159 us (0.941)
  Pallas kernels: 58.2 us -> 49.6 us
  other arithmetic: 9.78 us -> 6.34 us
  local copies, waits for them, and re-layouts: 8.97 us -> 11.2 us
  waiting for transfers between devices: 43.8 us -> 41.8 us
    pallas_call x1, Pallas kernels: 38.2 us -> 31 us  [per_device(): vmem_call(block_kernel, [shape(PATCHES, D), shape(PATCHES, D), shape(STRI...]
    concatenate x2 -> x0, other arithmetic: 3.17 us -> none  [the longest x1 2.04 us: per_device(): grad_qkv = jnp.concatenate([first[:, :768], second[:, :768]], axis=1)]
    all_to_all x1, starting transfers between devices: 6.26 us -> 9 us  [per_device(): lax.all_to_all(packed.reshape(bands * 2, 8, LANES), rows_ring, split_axis...]
    unnamed x27 -> x29, local copies, waits for them, and re-layouts: 1.93 us -> 4.35 us
    pallas_call x2 -> x1, Pallas kernels: 5.52 us -> 3.28 us  [per_device(): vmem_call(edge_kernel, [shape(2 * bands * 8 + 4 * STRIP, 128), shape(HALF...]
where the time goes in v3:
time: 159 us; the launch traced here: 158 us
  Pallas kernels  49.6 us (31%)
  starting transfers between devices  48.1 us (30%)
  waiting for transfers between devices  41.8 us (26%)
  local copies, waits for them, and re-layouts  11.2 us (7%)
  other arithmetic  6.34 us (4%)
    pallas_call x1, Pallas kernels, per_device(): vmem_call(block_kernel, [shape(PATCHES, D), shape(PATCHES, D), shape(STRI...  31 us
    all_to_all x1, waiting for transfers between devices, per_device(): lax.all_to_all(chip_sum.reshape(group_size, 8, 1536), group, split_axis=0...  19.5 us
    all_to_all x1, starting transfers between devices, per_device(): lax.all_to_all(packed.reshape(bands * 2, 8, LANES), rows_ring, split_axis...  9 us
    pallas_call x1, Pallas kernels, per_device(): vmem_call(prepare_kernel, [shape(1024, 1024), shape(TOKENS, D), shape(TOK...  8.49 us
    all_to_all x1, starting transfers between devices, per_device(): lax.all_to_all(copies, 'chip', split_axis=0, concat_axis=0, tiled=True)  7.77 us
    pallas_call x1, Pallas kernels, per_device(): vmem_call(pack_kernel, shape(bands, 2, 8, LANES), [pltpu.VMEM((2 * bands...  6.81 us
    ppermute x3, waiting for transfers between devices, per_device(): lax.ppermute(embed_part, ('lat', 'lon'), [(i * 2 + k, (i ^ dlat) * 2 + (k...  6.04 us
    all_to_all x1, starting transfers between devices, per_device(): lax.all_to_all(chip_sum.reshape(group_size, 8, 1536), group, split_axis=0...  5.2 us
  transfers between devices with their start and end apart: 16, of which 7 were waited for; matrix products, arithmetic and copies ran while one was open for 6% of the time, Pallas kernels for 10%

profile of v3, /device:TPU:1, one launch (start us, length us, event | category | flops | bytes accessed | tf_op | source)
XLA Modules:
  0.0 158.0 jit_solution(8589912677747222397)
XLA Ops:
  0.6 3.3 %shard_map.192 = (bf16[704,128]{1,0:T(8,128)(2,1)}, bf16[6,2,48,512]{3,2,1,0:T(8,128)(2,1)}, bf16[48,512]{1,0:T(8,128)(2,1)}, bf16[16,32,512]{2,1,0:T(8,128)(2,1)}) custom-call(bf16[32,12,2,4,192]{4,3,2,1,0:T(4,128)(2,1)} %pix_ref.3, bf16[12,2,48,512]{3,2,1,0:T(8,128)(2,1)} %cot_ref.3, bf16[32,512]{1,0:T(8,128)(2,1)} %bitcast.41, ...), custom_call_target="tpu_custom_call" | custom-call | flops 3000000000 | tf_op jit(solution)/shard_map/pallas_call | solution.py:462
  3.9 3.6 %collective-permute-start = (bf16[704,128]{1,0:T(8,128)(2,1)}, bf16[704,128]{1,0:T(8,128)(2,1)S(1)}, u32[]{:S(2)}, u32[]{:S(2)}) collective-permute-start(bf16[704,128]{1,0:T(8,128)(2,1)} %get-tuple-element.26), channel_id=1, source_target_pairs={{0,1},{1,0},{2,3},{3,2},{4,5},{5,4},{6,7},{7,6},{8,9},{9,8},{10,11... | collective-permute-start | bytes 540680 | tf_op jit(solution)/shard_map/ppermute | solution.py:479
  7.5 1.2 collective-permute-start.1
  8.6 0.6 collective-permute-start.2
  9.2 7.8 %all-to-all-start.1 = ((bf16[16,32,512]{2,1,0:T(8,128)(2,1)}), bf16[16,32,512]{2,1,0:T(8,128)(2,1)S(1)}, u32[]{:S(2)}, u32[]{:S(2)}) async-start(bf16[16,32,512]{2,1,0:T(8,128)(2,1)} %get-tuple-element.30), calls=%async_computation.1 | async-start | bytes 1048576 | tf_op jit(solution)/shard_map/all_to_all | solution.py:486
  17.0 0.0 collective-permute-done.halo_ref
  17.0 0.7 copy-done.10
  17.7 6.8 %shard_map.193 = bf16[32,2,8,1152]{3,2,1,0:T(8,128)(2,1)} custom-call(bf16[32,12,2,4,192]{4,3,2,1,0:T(4,128)(2,1)} %pix_ref.3, bf16[128,128]{1,0:T(8,128)(2,1)} %constant.100.clone.edge_ref, bf16[704,128]{1,0:T(8,128)(2,1)} %copy-done.10, bf16[1152,1152]{1,0:T(8,128)(2,1)} %constant.101.clone.main_ref), custom_call_target="tpu_custom_call" | custom-call | flops 6000000000 | tf_op jit(solution)/shard_map/pallas_call | solution.py:490
  24.5 0.0 copy-start.7
  24.5 2.8 %all-to-all-done.1 = bf16[16,32,512]{2,1,0:T(8,128)(2,1)S(1)} async-done(((bf16[16,32,512]{2,1,0:T(8,128)(2,1)}), bf16[16,32,512]{2,1,0:T(8,128)(2,1)S(1)}, u32[]{:S(2)}, u32[]{:S(2)}) %all-to-all-start.1) | async-done | bytes 524320 | tf_op jit(solution)/shard_map/all_to_all | solution.py:486
  27.3 2.1 %collective-permute-start.3 = (bf16[512,512]{1,0:T(8,128)(2,1)S(1)}, bf16[512,512]{1,0:T(8,128)(2,1)S(1)}, u32[]{:S(2)}, u32[]{:S(2)}) collective-permute-start(bf16[512,512]{1,0:T(8,128)(2,1)S(1)} %bitcast.32), channel_id=1, source_target_pairs={{0,4},{4,0},{1,5},{5,1},{2,6},{6,2},{3,7},{7,3},{8,12},{12,8},{9,1... | collective-permute-start | bytes 1572872 | tf_op jit(solution)/shard_map/ppermute | solution.py:488
  29.5 0.0 collective-permute-done.2.corner_ref
  29.5 0.0 collective-permute-done.1.ahead_ref
  29.5 0.0 copy-start.5
  29.5 9.0 %all-to-all-start = ((bf16[64,8,1152]{2,1,0:T(8,128)(2,1)}), bf16[64,8,1152]{2,1,0:T(8,128)(2,1)S(1)}, u32[]{:S(2)}, u32[]{:S(2)}) async-start(bf16[64,8,1152]{2,1,0:T(8,128)(2,1)} %bitcast.30), calls=%async_computation | async-start | bytes 2359296 | tf_op jit(solution)/shard_map/all_to_all | solution.py:503
  38.5 0.0 copy-start.6
  38.6 0.1 broadcast_add_fusion
  38.6 1.0 add.122.idx_ref
  39.6 0.7 add.110.idxr_ref
  40.4 0.1 reshape.124
  40.5 1.0 broadcast_in_dim_reshape.6.mcol_ref
  41.5 0.1 tile.9
  41.6 0.1 copy.23
  41.7 0.7 tile.11.mrow_ref
  42.4 0.6 gather_fusion
  43.0 0.0 collective-permute-done.3.woth_ref
  43.1 0.7 broadcast_in_dim.26
  43.8 0.1 copy-done.9
  43.9 8.5 %shard_map.194 = (bf16[1024,1024]{1,0:T(8,128)(2,1)}, bf16[1152,512]{1,0:T(8,128)(2,1)}, bf16[1152,512]{1,0:T(8,128)(2,1)}) custom-call(s32[1024,1]{1,0:T(8,128)} %add.122.idx_ref, f32[256,2]{1,0:T(8,128)} %bitcast.35, bf16[512,512]{1,0:T(8,128)(2,1)} %bitcast.33, bf16[512,512]{1,0:T(8,128)(2,1)} %copy-done.9, bf16[12,2,48,512]{3,2,1,0:T(8,128)(2,1)} %cot_ref.3, ...), custom_call_target="tpu_custom_call" | custom-call | flops 8000000000 | tf_op jit(solution)/shard_map/pallas_call | solution.py:519
  52.4 4.8 %all-to-all-done = bf16[64,8,1152]{2,1,0:T(8,128)(2,1)S(1)} async-done(((bf16[64,8,1152]{2,1,0:T(8,128)(2,1)}), bf16[64,8,1152]{2,1,0:T(8,128)(2,1)S(1)}, u32[]{:S(2)}, u32[]{:S(2)}) %all-to-all-start) | async-done | bytes 1179680 | tf_op jit(solution)/shard_map/all_to_all | solution.py:503
  57.1 1.0 copy-done.1
  58.2 31.0 %shard_map.195 = (bf16[576,512]{1,0:T(8,128)(2,1)}, bf16[576,512]{1,0:T(8,128)(2,1)}, bf16[48,512]{1,0:T(8,128)(2,1)}, bf16[48,512]{1,0:T(8,128)(2,1)}, bf16[512...) custom-call(bf16[32,2,8,1152]{3,2,1,0:T(8,128)(2,1)} %bitcast.31, s32[1,1024]{1,0:T(1,128)} %add.110.idxr_ref, ...), custom_call_target="tpu_custom_call" | custom-call | flops 38000001024 | tf_op jit(solution)/shard_map/pallas_call | solution.py:535
  89.2 1.4 collective-permute-start.4
  90.6 3.2 %collective-permute-done.4 = bf16[512,1536]{1,0:T(8,128)(2,1)S(1)} collective-permute-done((bf16[512,1536]{1,0:T(8,128)(2,1)}, bf16[512,1536]{1,0:T(8,128)(2,1)S(1)}, u32[]{:S(2)}, u32[]{:S(2)}) %collective-permute-start.4) | collective-permute-done | bytes 1572896 | tf_op jit(solution)/shard_map/ppermute | solution.py:591
  93.8 2.9 %fusion = bf16[64,8,1536]{2,1,0:T(8,128)(2,1)} fusion(bf16[512,1536]{1,0:T(8,128)(2,1)S(1)} %collective-permute-done.4, bf16[512,1536]{1,0:T(8,128)(2,1)} %get-tuple-element.36), kind=kLoop, calls=%fused_computation.2 | loop fusion | flops 3145728 | bytes 4718592 | tf_op jit(solution)/shard_map/reshape | solution.py:594
  96.8 5.2 %all-to-all-start.2 = ((bf16[64,8,1536]{2,1,0:T(8,128)(2,1)}), bf16[64,8,1536]{2,1,0:T(8,128)(2,1)S(1)}, u32[]{:S(2)}, u32[]{:S(2)}) async-start(bf16[64,8,1536]{2,1,0:T(8,128)(2,1)} %fusion), calls=%async_computation.2 | async-start | bytes 3145728 | tf_op jit(solution)/shard_map/all_to_all | solution.py:593
  102.0 1.1 collective-permute-start.5
  103.1 2.4 %collective-permute-start.6 = (bf16[48,512]{1,0:T(8,128)(2,1)S(1)}, bf16[48,512]{1,0:T(8,128)(2,1)S(1)}, u32[]{:S(2)}, u32[]{:S(2)}) collective-permute-start(bf16[48,512]{1,0:T(8,128)(2,1)S(1)} %copy-done.12), channel_id=1, source_target_pairs={{0,1},{1,0},{2,3},{3,2},{4,5},{5,4},{6,7},{7,6},{8,9},{9,8},{10,11... | collective-permute-start | bytes 147464 | tf_op jit(solution)/shard_map/ppermute | solution.py:619
  105.5 1.8 %collective-permute-start.7 = (bf16[48,512]{1,0:T(8,128)(2,1)S(1)}, bf16[48,512]{1,0:T(8,128)(2,1)S(1)}, u32[]{:S(2)}, u32[]{:S(2)}) collective-permute-start(bf16[48,512]{1,0:T(8,128)(2,1)S(1)} %copy-done.11), channel_id=1, source_target_pairs={{0,3},{1,2},{2,5},{3,4},{4,7},{5,6},{6,9},{7,8},{8,11},{9,10},{10,... | collective-permute-start | bytes 147464 | tf_op jit(solution)/shard_map/ppermute | solution.py:620
  107.3 19.5 %all-to-all-done.2 = bf16[64,8,1536]{2,1,0:T(8,128)(2,1)S(1)} async-done(((bf16[64,8,1536]{2,1,0:T(8,128)(2,1)}), bf16[64,8,1536]{2,1,0:T(8,128)(2,1)S(1)}, u32[]{:S(2)}, u32[]{:S(2)}) %all-to-all-start.2) | async-done | bytes 1572896 | tf_op jit(solution)/shard_map/all_to_all | solution.py:593
  126.8 0.2 reduce_sum.12
  127.0 1.1 broadcast_in_dim.28
  128.1 4.8 %all-to-all-start.3 = ((bf16[64,8,1024]{2,1,0:T(8,128)(2,1)}), bf16[64,8,1024]{2,1,0:T(8,128)(2,1)S(1)}, u32[]{:S(2)}, u32[]{:S(2)}) async-start(bf16[64,8,1024]{2,1,0:T(8,128)(2,1)} %broadcast_in_dim.28), calls=%async_computation.3 | async-start | bytes 2097152 | tf_op jit(solution)/shard_map/all_to_all | solution.py:598
  132.9 2.7 %collective-permute-start.8 = (bf16[8,512]{1,0:T(8,128)(2,1)S(1)}, bf16[8,512]{1,0:T(8,128)(2,1)S(1)}, u32[]{:S(2)}, u32[]{:S(2)}) collective-permute-start(bf16[8,512]{1,0:T(8,128)(2,1)S(1)} %get-tuple-element.53), channel_id=1, source_target_pairs={{0,1},{1,0},{2,3},{3,2},{4,5},{5,4},{6,7},{7,6},{8,9},{9,8},{10,11... | collective-permute-start | bytes 24584 | tf_op jit(solution)/shard_map/ppermute | solution.py:605
  135.6 0.3 collective-permute-start.9
  135.9 0.0 collective-permute-done.6
  135.9 0.6 collective-permute-start.10
  136.5 0.0 collective-permute-done.7
  136.6 0.0 collective-permute-done.5
  136.7 0.1 pad_maximum_fusion
  136.7 0.6 slice.39
  137.3 1.6 %pad_maximum_fusion.1 = bf16[12,2,48,512]{3,2,1,0:T(8,128)(2,1)} fusion(bf16[12,2,45,512]{3,2,1,0:T(8,128)(2,1)S(1)} %slice.39, bf16[12,2,3,512]{3,2,1,0:T(4,128)(2,1)S(1)} %reshape.128), kind=kLoop, calls=%fused_computation.6 | loop fusion | flops 2359296 | bytes 2359296 | tf_op jit(solution)/shard_map/concatenate | solution.py:628
  139.0 6.0 %collective-permute-done.8 = bf16[8,512]{1,0:T(8,128)(2,1)S(1)} collective-permute-done((bf16[8,512]{1,0:T(8,128)(2,1)S(1)}, bf16[8,512]{1,0:T(8,128)(2,1)S(1)}, u32[]{:S(2)}, u32[]{:S(2)}) %collective-permute-start.8) | collective-permute-done | bytes 8224 | tf_op jit(solution)/shard_map/ppermute | solution.py:605
  145.0 0.6 convert.2
  145.7 3.7 %all-to-all-done.3 = bf16[64,8,1024]{2,1,0:T(8,128)(2,1)S(1)} async-done(((bf16[64,8,1024]{2,1,0:T(8,128)(2,1)}), bf16[64,8,1024]{2,1,0:T(8,128)(2,1)S(1)}, u32[]{:S(2)}, u32[]{:S(2)}) %all-to-all-start.3) | async-done | bytes 1048608 | tf_op jit(solution)/shard_map/all_to_all | solution.py:598
  149.4 3.6 %collective-permute-start.11 = (bf16[512,1024]{1,0:T(8,128)(2,1)S(1)}, bf16[512,1024]{1,0:T(8,128)(2,1)S(1)}, u32[]{:S(2)}, u32[]{:S(2)}) collective-permute-start(bf16[512,1024]{1,0:T(8,128)(2,1)S(1)} %bitcast.27), channel_id=1, source_target_pairs={{0,4},{4,0},{1,5},{5,1},{2,6},{6,2},{3,7},{7,3},{8,12},{12,8},{9,1... | collective-permute-start | bytes 3145736 | tf_op jit(solution)/shard_map/ppermute | solution.py:631
  153.0 0.1 slice.32
  153.1 0.1 maximum_convert_fusion.1
  153.2 0.4 maximum_convert_fusion
  153.6 1.7 %collective-permute-done.11 = bf16[512,1024]{1,0:T(8,128)(2,1)S(1)} collective-permute-done((bf16[512,1024]{1,0:T(8,128)(2,1)S(1)}, bf16[512,1024]{1,0:T(8,128)(2,1)S(1)}, u32[]{:S(2)}, u32[]{:S(2)}) %collective-permute-start.11) | collective-permute-done | bytes 1048608 | tf_op jit(solution)/shard_map/ppermute | solution.py:631
  155.3 0.0 copy-start.2
  155.3 0.2 convert_dynamic-update-slice_fusion
  155.5 0.8 copy-done.2
  156.3 1.7 %copy-done = f32[512,1536]{1,0:T(8,128)} copy-done((f32[512,1536]{1,0:T(8,128)}, f32[512,1536]{1,0:T(8,128)S(1)}, u32[]{:S(2)}) %copy-start) | copy-done | bytes 3145752
  (38 shorter events, 0.3 us)
Async XLA Ops:
  3.9 13.1 %collective-permute-start = (bf16[704,128]{1,0:T(8,128)(2,1)}, bf16[704,128]{1,0:T(8,128)(2,1)S(1)}, u32[]{:S(2)}, u32[]{:S(2)}) collective-permute-start(bf16[704,128]{1,0:T(8,128)(2,1)} %get-tuple-element.26), channel_id=1, source_target_pairs={{0,1},{1,0},{2,3},{3,2},{4,5},{5,4},{6,7},{7,6},{8,9},{9,8},{10,11... | collective-permute-start | bytes 540680 | tf_op jit(solution)/shard_map/ppermute | solution.py:479
  7.5 22.0 %collective-permute-start.1 = (bf16[6,2,48,512]{3,2,1,0:T(8,128)(2,1)}, bf16[6,2,48,512]{3,2,1,0:T(8,128)(2,1)S(1)}, u32[]{:S(2)}, u32[]{:S(2)}) collective-permute-start(bf16[6,2,48,512]{3,2,1,0:T(8,128)(2,1)} %get-tuple-element.27), channel_id=1, source_target_pairs={{0,126},{2,0},{4,2},{6,4},{8,6},{10,8},{12,10},{14,12},{16,14},{18... | collective-permute-start | bytes 1769480 | tf_op jit(solution)/shard_map/ppermute | solution.py:480
  8.6 20.8 %collective-permute-start.2 = (bf16[48,512]{1,0:T(8,128)(2,1)}, bf16[48,512]{1,0:T(8,128)(2,1)S(1)}, u32[]{:S(2)}, u32[]{:S(2)}) collective-permute-start(bf16[48,512]{1,0:T(8,128)(2,1)} %get-tuple-element.28), channel_id=1, source_target_pairs={{0,127},{1,126},{2,1},{3,0},{4,3},{5,2},{6,5},{7,4},{8,7},{9,6},{1... | collective-permute-start | bytes 147464 | tf_op jit(solution)/shard_map/ppermute | solution.py:481
  9.2 18.1 %all-to-all-start.1 = ((bf16[16,32,512]{2,1,0:T(8,128)(2,1)}), bf16[16,32,512]{2,1,0:T(8,128)(2,1)S(1)}, u32[]{:S(2)}, u32[]{:S(2)}) async-start(bf16[16,32,512]{2,1,0:T(8,128)(2,1)} %get-tuple-element.30), calls=%async_computation.1 | async-start | bytes 1048576 | tf_op jit(solution)/shard_map/all_to_all | solution.py:486
  17.0 0.7 copy-start.10
  24.5 14.0 %copy-start.7 = (s32[64]{0:T(128)S(1)}, s32[64]{0:T(128)}, u32[]{:S(2)}) copy-start(s32[64]{0:T(128)} %param.18) | copy-start | bytes 772
  27.3 12.3 %copy-start.4 = (bf16[16,32,512]{2,1,0:T(8,128)(2,1)}, bf16[16,32,512]{2,1,0:T(8,128)(2,1)S(1)}, u32[]{:S(2)}) copy-start(bf16[16,32,512]{2,1,0:T(8,128)(2,1)S(1)} %all-to-all-done.1) | copy-start | bytes 1572868
  27.3 15.7 %collective-permute-start.3 = (bf16[512,512]{1,0:T(8,128)(2,1)S(1)}, bf16[512,512]{1,0:T(8,128)(2,1)S(1)}, u32[]{:S(2)}, u32[]{:S(2)}) collective-permute-start(bf16[512,512]{1,0:T(8,128)(2,1)S(1)} %bitcast.32), channel_id=1, source_target_pairs={{0,4},{4,0},{1,5},{5,1},{2,6},{6,2},{3,7},{7,3},{8,12},{12,8},{9,1... | collective-permute-start | bytes 1572872 | tf_op jit(solution)/shard_map/ppermute | solution.py:488
  29.5 10.2 %copy-start.13 = (bf16[48,512]{1,0:T(8,128)(2,1)}, bf16[48,512]{1,0:T(8,128)(2,1)S(1)}, u32[]{:S(2)}) copy-start(bf16[48,512]{1,0:T(8,128)(2,1)S(1)} %collective-permute-done.2.corner_ref) | copy-start | bytes 147460
  29.5 10.2 %copy-start.8 = (bf16[6,2,48,512]{3,2,1,0:T(8,128)(2,1)}, bf16[6,2,48,512]{3,2,1,0:T(8,128)(2,1)S(1)}, u32[]{:S(2)}) copy-start(bf16[6,2,48,512]{3,2,1,0:T(8,128)(2,1)S(1)} %collective-permute-done.1.ahead_ref) | copy-start | bytes 1769476
  29.5 10.9 %copy-start.5 = (s32[12,2,48]{2,1,0:T(2,128)S(1)}, s32[12,2,48]{2,1,0:T(2,128)}, u32[]{:S(2)}) copy-start(s32[12,2,48]{2,1,0:T(2,128)} %param.24) | copy-start | bytes 13828
  29.5 27.6 %all-to-all-start = ((bf16[64,8,1152]{2,1,0:T(8,128)(2,1)}), bf16[64,8,1152]{2,1,0:T(8,128)(2,1)S(1)}, u32[]{:S(2)}, u32[]{:S(2)}) async-start(bf16[64,8,1152]{2,1,0:T(8,128)(2,1)} %bitcast.30), calls=%async_computation | async-start | bytes 2359296 | tf_op jit(solution)/shard_map/all_to_all | solution.py:503
  38.5 3.1 %copy-start.6 = (f32[64,2]{0,1:T(2,128)S(1)}, f32[64,2]{0,1:T(2,128)}, u32[]{:S(2)}) copy-start(f32[64,2]{0,1:T(2,128)} %param.20) | copy-start | bytes 1540
  43.0 0.8 copy-start.9
  57.1 1.0 copy-start.1
  89.2 4.7 %collective-permute-start.4 = (bf16[512,1536]{1,0:T(8,128)(2,1)}, bf16[512,1536]{1,0:T(8,128)(2,1)S(1)}, u32[]{:S(2)}, u32[]{:S(2)}) collective-permute-start(bf16[512,1536]{1,0:T(8,128)(2,1)} %get-tuple-element.37), channel_id=1, source_target_pairs={{0,4},{4,0},{1,5},{5,1},{2,6},{6,2},{3,7},{7,3},{8,12},{12,8},{9,1... | collective-permute-start | bytes 4718600 | tf_op jit(solution)/shard_map/ppermute | solution.py:591
  96.8 6.3 %copy-start.12 = (bf16[48,512]{1,0:T(8,128)(2,1)S(1)}, bf16[48,512]{1,0:T(8,128)(2,1)}, u32[]{:S(2)}) copy-start(bf16[48,512]{1,0:T(8,128)(2,1)} %get-tuple-element.39) | copy-start | bytes 147460
  96.8 8.7 %copy-start.11 = (bf16[48,512]{1,0:T(8,128)(2,1)S(1)}, bf16[48,512]{1,0:T(8,128)(2,1)}, u32[]{:S(2)}) copy-start(bf16[48,512]{1,0:T(8,128)(2,1)} %get-tuple-element.40) | copy-start | bytes 147460
  96.8 30.0 %all-to-all-start.2 = ((bf16[64,8,1536]{2,1,0:T(8,128)(2,1)}), bf16[64,8,1536]{2,1,0:T(8,128)(2,1)S(1)}, u32[]{:S(2)}, u32[]{:S(2)}) async-start(bf16[64,8,1536]{2,1,0:T(8,128)(2,1)} %fusion), calls=%async_computation.2 | async-start | bytes 3145728 | tf_op jit(solution)/shard_map/all_to_all | solution.py:593
  102.0 34.6 %collective-permute-start.5 = (bf16[576,512]{1,0:T(8,128)(2,1)}, bf16[576,512]{1,0:T(8,128)(2,1)S(1)}, u32[]{:S(2)}, u32[]{:S(2)}) collective-permute-start(bf16[576,512]{1,0:T(8,128)(2,1)} %get-tuple-element.38), channel_id=1, source_target_pairs={{0,2},{2,4},{4,6},{6,8},{8,10},{10,12},{12,14},{14,16},{16,18},{18... | collective-permute-start | bytes 1769480 | tf_op jit(solution)/shard_map/ppermute | solution.py:618
  103.1 32.9 %collective-permute-start.6 = (bf16[48,512]{1,0:T(8,128)(2,1)S(1)}, bf16[48,512]{1,0:T(8,128)(2,1)S(1)}, u32[]{:S(2)}, u32[]{:S(2)}) collective-permute-start(bf16[48,512]{1,0:T(8,128)(2,1)S(1)} %copy-done.12), channel_id=1, source_target_pairs={{0,1},{1,0},{2,3},{3,2},{4,5},{5,4},{6,7},{7,6},{8,9},{9,8},{10,11... | collective-permute-start | bytes 147464 | tf_op jit(solution)/shard_map/ppermute | solution.py:619
  105.5 31.1 %collective-permute-start.7 = (bf16[48,512]{1,0:T(8,128)(2,1)S(1)}, bf16[48,512]{1,0:T(8,128)(2,1)S(1)}, u32[]{:S(2)}, u32[]{:S(2)}) collective-permute-start(bf16[48,512]{1,0:T(8,128)(2,1)S(1)} %copy-done.11), channel_id=1, source_target_pairs={{0,3},{1,2},{2,5},{3,4},{4,7},{5,6},{6,9},{7,8},{8,11},{9,10},{10,... | collective-permute-start | bytes 147464 | tf_op jit(solution)/shard_map/ppermute | solution.py:620
  128.1 8.6 %copy-start.3 = (bf16[576,512]{1,0:T(8,128)(2,1)S(1)}, bf16[576,512]{1,0:T(8,128)(2,1)}, u32[]{:S(2)}) copy-start(bf16[576,512]{1,0:T(8,128)(2,1)} %get-tuple-element.44) | copy-start | bytes 1769476
  128.1 21.3 %all-to-all-start.3 = ((bf16[64,8,1024]{2,1,0:T(8,128)(2,1)}), bf16[64,8,1024]{2,1,0:T(8,128)(2,1)S(1)}, u32[]{:S(2)}, u32[]{:S(2)}) async-start(bf16[64,8,1024]{2,1,0:T(8,128)(2,1)} %broadcast_in_dim.28), calls=%async_computation.3 | async-start | bytes 2097152 | tf_op jit(solution)/shard_map/all_to_all | solution.py:598
  132.9 12.1 %collective-permute-start.8 = (bf16[8,512]{1,0:T(8,128)(2,1)S(1)}, bf16[8,512]{1,0:T(8,128)(2,1)S(1)}, u32[]{:S(2)}, u32[]{:S(2)}) collective-permute-start(bf16[8,512]{1,0:T(8,128)(2,1)S(1)} %get-tuple-element.53), channel_id=1, source_target_pairs={{0,1},{1,0},{2,3},{3,2},{4,5},{5,4},{6,7},{7,6},{8,9},{9,8},{10,11... | collective-permute-start | bytes 24584 | tf_op jit(solution)/shard_map/ppermute | solution.py:605
  135.6 9.3 %collective-permute-start.9 = (bf16[8,512]{1,0:T(8,128)(2,1)S(1)}, bf16[8,512]{1,0:T(8,128)(2,1)S(1)}, u32[]{:S(2)}, u32[]{:S(2)}) collective-permute-start(bf16[8,512]{1,0:T(8,128)(2,1)S(1)} %get-tuple-element.53), channel_id=1, source_target_pairs={{0,2},{1,3},{2,0},{3,1},{4,6},{5,7},{6,4},{7,5},{8,10},{9,11},{10,... | collective-permute-start | bytes 24584 | tf_op jit(solution)/shard_map/ppermute | solution.py:605
  135.9 9.1 %collective-permute-start.10 = (bf16[8,512]{1,0:T(8,128)(2,1)S(1)}, bf16[8,512]{1,0:T(8,128)(2,1)S(1)}, u32[]{:S(2)}, u32[]{:S(2)}) collective-permute-start(bf16[8,512]{1,0:T(8,128)(2,1)S(1)} %get-tuple-element.53), channel_id=1, source_target_pairs={{0,3},{1,2},{2,1},{3,0},{4,7},{5,6},{6,5},{7,4},{8,11},{9,10},{10,... | collective-permute-start | bytes 24584 | tf_op jit(solution)/shard_map/ppermute | solution.py:605
  149.4 5.9 %collective-permute-start.11 = (bf16[512,1024]{1,0:T(8,128)(2,1)S(1)}, bf16[512,1024]{1,0:T(8,128)(2,1)S(1)}, u32[]{:S(2)}, u32[]{:S(2)}) collective-permute-start(bf16[512,1024]{1,0:T(8,128)(2,1)S(1)} %bitcast.27), channel_id=1, source_target_pairs={{0,4},{4,0},{1,5},{5,1},{2,6},{6,2},{3,7},{7,3},{8,12},{12,8},{9,1... | collective-permute-start | bytes 3145736 | tf_op jit(solution)/shard_map/ppermute | solution.py:631
  155.3 1.0 copy-start.2
  156.3 1.7 %copy-start = (f32[512,1536]{1,0:T(8,128)}, f32[512,1536]{1,0:T(8,128)S(1)}, u32[]{:S(2)}) copy-start(f32[512,1536]{1,0:T(8,128)S(1)} %convert_dynamic-update-slice_fusion) | copy-start | bytes 9437188

commit v4 on v3

--- a/solution.py
+++ b/solution.py
@@ -226,22 +226,14 @@
     wqkv_far,
     gb_far,
     ga_far,
-    wproj_far,
-    tokt_far,
-    top_far,
-    bot_far,
-    side_top_ref,
-    side_bot_ref,
+    tok_far,
+    att_far,
     gown_far,
     goth_far,
     lw_ref,
     wqkv_ref,
     gb_ref,
     ga_ref,
-    wproj_ref,
-    tokt_ref,
-    top_ref,
-    bot_ref,
     g_ref,
     a_s,
     at_s,
@@ -258,8 +250,8 @@
     sem_in,
     sem_out,
 ):
-    far = [lw_far, wqkv_far, gb_far, ga_far, wproj_far, tokt_far]
-    near = [lw_ref, wqkv_ref, gb_ref, ga_ref, wproj_ref, tokt_ref]
+    far = [lw_far, wqkv_far, gb_far, ga_far]
+    near = [lw_ref, wqkv_ref, gb_ref, ga_ref]
     moves = [pltpu.make_async_copy(x, y, sem_in.at[i]) for i, (x, y) in enumerate(zip(far, near))]
     for move in moves:
         move.start()
@@ -295,6 +287,9 @@
         for w in range(WINDOWS):
             t_s[w * WTOK + level * 72 : w * WTOK + level * 72 + 72, :] = tok[w * 72 : w * 72 + 72]
 
+    bo_s[...] = t_s[...].astype(BF)
+    send(bo_s, tok_far)
+
     def norm_step(w, carry):
         rows = pl.ds(pl.multiple_of(w * WTOK, WTOK), WTOK)
         x = t_s[rows, :]
@@ -306,7 +301,7 @@
         norm_s[rows, :] = (unit * gain).astype(BF)
         return carry
 
-    lax.fori_loop(0, WINDOWS, norm_step, 0)
+    lax.fori_loop(0, WINDOWS, norm_step, 0, unroll=True)
     moves[1].wait()
     for n in range(3):
         qkv_s[:, n * D : n * D + D] = dot(norm_s[...], wqkv_ref[:, n * D : n * D + D]).astype(BF)
@@ -353,17 +348,9 @@
             gp_s[rows, 2 * D + at : 2 * D + at + 256] = dot(prob, grads).astype(BF)
         return carry
 
-    lax.fori_loop(0, WINDOWS, window_step, 0)
-
-    branch = dot(att_s[...], wproj_ref[...]).astype(BF).astype(F32)
-    bo_s[...] = (t_s[...] + branch).astype(BF)
-    top_ref[...] = dot(tokt_ref[:PATCHES], bo_s[...]).astype(BF)
-    bot_ref[...] = dot(tokt_ref[PATCHES:TOKENS], bo_s[...]).astype(BF)
-    send(top_ref, top_far)
-    send(bot_ref, bot_far)
-    sides = dot(tokt_ref[TOKENS:], bo_s[...]).astype(BF)
-    side_top_ref[...] = sides[:STRIP]
-    side_bot_ref[...] = sides[STRIP : 2 * STRIP]
+    lax.fori_loop(0, WINDOWS, window_step, 0, unroll=4)
+
+    send(att_s, att_far)
 
     total = dot(norm_s[...], gp_s[...], TN)
     for part in range(2):
@@ -405,6 +392,35 @@
         g_ref[i, :, 1024:1536] = dot(pick, gs_s[...]).astype(BF)
         send(g_ref.at[i, :, 1024:], target.at[:, 1024:])
     for move in sent:
+        move.wait()
+
+
+def out_kernel(tok_ref, att_ref, wproj_ref, tokt_ref, top_ref, bot_ref, side_top_ref, side_bot_ref):
+    branch = dot(att_ref[...], wproj_ref[...]).astype(BF).astype(F32)
+    total = (tok_ref[...].astype(F32) + branch).astype(BF)
+    top_ref[...] = dot(tokt_ref[:PATCHES], total).astype(BF)
+    bot_ref[...] = dot(tokt_ref[PATCHES:TOKENS], total).astype(BF)
+    sides = dot(tokt_ref[TOKENS:], total).astype(BF)
+    side_top_ref[...] = sides[:STRIP]
+    side_bot_ref[...] = sides[STRIP : 2 * STRIP]
+
+
+def add_kernel(left_ref, right_ref, out_ref):
+    out_ref[...] = (left_ref[...].astype(F32) + right_ref[...].astype(F32)).astype(BF)
+
+
+def join_kernel(mine_ref, other_ref, qkv_far, proj_far, qkv_s, proj_s, sems):
+    core = lax.axis_index("core")
+    moves = []
+    for i, ref in enumerate((mine_ref, other_ref)):
+        for near, far, lanes in ((qkv_s, qkv_far, slice(0, 768)), (proj_s, proj_far, slice(768, 1024))):
+            width = near.shape[2]
+            near[i] = ref[:, lanes].astype(F32)
+            at = pl.multiple_of((core ^ i) * width, 256)
+            move = pltpu.make_async_copy(near.at[i], far.at[:, pl.ds(at, width)], sems.at[len(moves)])
+            move.start()
+            moves.append(move)
+    for move in moves:
         move.wait()
 
 
@@ -477,6 +493,7 @@
         jnp.asarray(strip_place(), BF),
     )
     halo = lax.ppermute(border, "lon", swap_lon)
+    halo, ahead, corner = lax.optimization_barrier((halo, ahead, corner))
     ahead = lax.ppermute(ahead, rows_ring, [(i, (i - 1) % ring) for i in range(ring)])
     corner = lax.ppermute(
         corner,
@@ -499,11 +516,11 @@
         far=(3,),
         us=6,
     )(pixels, jnp.asarray(edge, BF), halo, jnp.asarray(main, BF))
-    packed, ahead, corner = lax.optimization_barrier((packed, ahead, corner))
     recv = lax.all_to_all(
         packed.reshape(bands * 2, 8, LANES), rows_ring, split_axis=0, concat_axis=0, tiled=True
     ).reshape(bands, 2, 8, LANES)
 
+    var_order, ahead, corner = lax.optimization_barrier((var_order, ahead, corner))
     device = var_order // 2
     base = jnp.where(device % 2 == core, 0, 512) + (device // 2) * 32 + (var_order % 2) * 16
     index = base[None, :, None] + (
@@ -532,13 +549,11 @@
     )
 
     pmain, prest = patch_place()
-    top, bot, side_top, side_bot, gown, goth = vmem_call(
+    tokens, attended, gown, goth = vmem_call(
         block_kernel,
         [
-            shape(PATCHES, D),
-            shape(PATCHES, D),
-            shape(STRIP, D),
-            shape(STRIP, D),
+            shape(TOKENS, D),
+            shape(TOKENS, D),
             shape(512, 1536),
             shape(512, 1536),
         ],
@@ -547,10 +562,6 @@
             pltpu.VMEM((D, 3 * D), BF),
             pltpu.VMEM((TOKENS, D), BF),
             pltpu.VMEM((TOKENS, D), BF),
-            pltpu.VMEM((D, D), BF),
-            pltpu.VMEM((TOKENS + 128, TOKENS), BF),
-            pltpu.VMEM((PATCHES, D), BF),
-            pltpu.VMEM((PATCHES, D), BF),
             pltpu.VMEM((2, 512, 1536), BF),
             pltpu.VMEM((PATCHES, 1024), BF),
             pltpu.VMEM((1024, PATCHES), BF),
@@ -564,13 +575,13 @@
             pltpu.VMEM((TOKENS, D), BF),
             pltpu.VMEM((LEVELS, PATCHES, D), F32),
             pltpu.VMEM((1024, D), BF),
-            pltpu.SemaphoreType.DMA((6,)),
+            pltpu.SemaphoreType.DMA((4,)),
             pltpu.SemaphoreType.DMA((6,)),
         ],
-        count=14,
-        far=range(8, 14),
-        far_out=(0, 1, 4, 5),
-        us=38,
+        count=12,
+        far=range(8, 12),
+        far_out=(0, 1, 2, 3),
+        us=28,
     )(
         recv,
         index[None, :],
@@ -584,12 +595,10 @@
         w_qkv,
         grad_branch,
         grad_attended,
-        w_proj,
-        jnp.asarray(tok.T, BF),
     )
 
     from_core = lax.ppermute(goth, "core", swap_core)
-    chip_sum = (gown.astype(F32) + from_core.astype(F32)).astype(BF)
+    chip_sum = vmem_call(add_kernel, shape(512, 1536), count=2, mib=7, us=2)(gown, from_core)
     terms = lax.all_to_all(
         chip_sum.reshape(group_size, 8, 1536), group, split_axis=0, concat_axis=0, tiled=True
     )
@@ -615,6 +624,12 @@
     )
     grad_embed = grad_embed.reshape(2, 16, D).astype(F32)
 
+    top, bot, side_top, side_bot = vmem_call(
+        out_kernel,
+        [shape(PATCHES, D), shape(PATCHES, D), shape(STRIP, D), shape(STRIP, D)],
+        count=4,
+        us=5,
+    )(tokens, attended, w_proj, jnp.asarray(tok.T, BF))
     from_before = lax.ppermute(bot, rows_ring, [(i, (i + 1) % ring) for i in range(ring)])
     west = lax.ppermute(side_top, "lon", swap_lon)
     south_west = lax.ppermute(
@@ -629,12 +644,19 @@
 
     mine, block_out, grad_embed = lax.optimization_barrier((mine, block_out, grad_embed))
     other = lax.ppermute(mine, "core", swap_core)
-    grads = []
-    for lanes, width in ((slice(0, 768), 768), (slice(768, 1024), 256)):
-        own = jnp.concatenate([mine[:, lanes]] * 2, axis=1).astype(F32)
-        rest = other[:, lanes].astype(F32)
-        grads.append(lax.dynamic_update_slice(own, rest, (0, (1 - core) * width)))
-    grad_qkv, grad_proj = grads
+    grad_qkv, grad_proj = vmem_call(
+        join_kernel,
+        [shape(512, 1536, dtype=F32), shape(512, 512, dtype=F32)],
+        [
+            pltpu.VMEM((2, 512, 768), F32),
+            pltpu.VMEM((2, 512, 256), F32),
+            pltpu.SemaphoreType.DMA((4,)),
+        ],
+        count=2,
+        far_out=(0, 1),
+        mib=10,
+        us=2,
+    )(mine, other)
     return (block_out, grad_embed, grad_qkv, grad_proj)
 
 

time: 159 us -> 152 us (0.956)
  waiting for transfers between devices: 41.8 us -> 35.5 us
  Pallas kernels: 49.6 us -> 53.9 us
  other arithmetic: 6.34 us -> 2.74 us
  local copies, waits for them, and re-layouts: 11.2 us -> 9.45 us
    all_to_all x1, waiting for transfers between devices: 19.5 us -> 13.7 us  [per_device(): lax.all_to_all(chip_sum.reshape(group_size, 8, 1536), group, split_axis=0...]
    pallas_call x1 -> x4, Pallas kernels: 31 us -> 35.4 us  [the longest x1 25.9 us: per_device(): vmem_call(block_kernel, [shape(TOKENS, D), shape(TOKENS, D), shape(512, 1...]
    reshape x1 -> x0, other arithmetic: 2.93 us -> none  [per_device(): chip_sum.reshape(group_size, 8, 1536)]
    all_to_all x1, waiting for transfers between devices: 2.84 us -> 0.01 us  [per_device(): lax.all_to_all(copies, 'chip', split_axis=0, concat_axis=0, tiled=True)]
    all_to_all x1, starting transfers between devices: 5.2 us -> 7.31 us  [per_device(): lax.all_to_all(chip_sum.reshape(group_size, 8, 1536), group, split_axis=0...]
    unnamed x29 -> x25, local copies, waits for them, and re-layouts: 4.35 us -> 2.67 us
  transfers between devices with their start and end apart: 16 -> 16, of which waited for: 7 -> 6; matrix products, arithmetic and copies ran while one was open for 6% -> 6% of each run, Pallas kernels for 10% -> 14%
where the time goes in v4:
time: 152 us; the launch traced here: 151 us
  Pallas kernels  53.9 us (35%)
  starting transfers between devices  48.4 us (32%)
  waiting for transfers between devices  35.5 us (23%)
  local copies, waits for them, and re-layouts  9.45 us (6%)
  other arithmetic  2.74 us (2%)
    pallas_call x1, Pallas kernels, per_device(): vmem_call(block_kernel, [shape(TOKENS, D), shape(TOKENS, D), shape(512, 1...  25.9 us
    all_to_all x1, waiting for transfers between devices, per_device(): lax.all_to_all(chip_sum.reshape(group_size, 8, 1536), group, split_axis=0...  13.7 us
    all_to_all x1, starting transfers between devices, per_device(): lax.all_to_all(packed.reshape(bands * 2, 8, LANES), rows_ring, split_axis...  8.73 us
    pallas_call x1, Pallas kernels, per_device(): vmem_call(prepare_kernel, [shape(1024, 1024), shape(TOKENS, D), shape(TOK...  8.43 us
    all_to_all x1, starting transfers between devices, per_device(): lax.all_to_all(copies, 'chip', split_axis=0, concat_axis=0, tiled=True)  7.77 us
    all_to_all x1, starting transfers between devices, per_device(): lax.all_to_all(chip_sum.reshape(group_size, 8, 1536), group, split_axis=0...  7.31 us
    pallas_call x1, Pallas kernels, per_device(): vmem_call(pack_kernel, shape(bands, 2, 8, LANES), [pltpu.VMEM((2 * bands...  6.81 us
    ppermute x3, waiting for transfers between devices, per_device(): lax.ppermute(embed_part, ('lat', 'lon'), [(i * 2 + k, (i ^ dlat) * 2 + (k...  6.3 us
  transfers between devices with their start and end apart: 16, of which 6 were waited for; matrix products, arithmetic and copies ran while one was open for 6% of the time, Pallas kernels for 14%

profile of v4, /device:TPU:1, one launch (start us, length us, event | category | flops | bytes accessed | tf_op | source)
XLA Modules:
  0.0 151.1 jit_solution(13071865622193841009)
XLA Ops:
  0.6 0.0 copy-start.4
  0.6 3.3 %shard_map.192 = (bf16[704,128]{1,0:T(8,128)(2,1)}, bf16[6,2,48,512]{3,2,1,0:T(8,128)(2,1)}, bf16[48,512]{1,0:T(8,128)(2,1)}, bf16[16,32,512]{2,1,0:T(8,128)(2,1)}) custom-call(bf16[32,12,2,4,192]{4,3,2,1,0:T(4,128)(2,1)} %pix_ref.3, bf16[12,2,48,512]{3,2,1,0:T(8,128)(2,1)} %cot_ref.3, bf16[32,512]{1,0:T(8,128)(2,1)} %bitcast.39, ...), custom_call_target="tpu_custom_call" | custom-call | flops 3000000000 | tf_op jit(solution)/shard_map/pallas_call | solution.py:478
  3.9 3.7 %collective-permute-start = (bf16[704,128]{1,0:T(8,128)(2,1)}, bf16[704,128]{1,0:T(8,128)(2,1)S(1)}, u32[]{:S(2)}, u32[]{:S(2)}) collective-permute-start(bf16[704,128]{1,0:T(8,128)(2,1)} %get-tuple-element.33), channel_id=1, source_target_pairs={{0,1},{1,0},{2,3},{3,2},{4,5},{5,4},{6,7},{7,6},{8,9},{9,8},{10,11... | collective-permute-start | bytes 540680 | tf_op jit(solution)/shard_map/ppermute | solution.py:495
  7.6 7.8 %all-to-all-start.1 = ((bf16[16,32,512]{2,1,0:T(8,128)(2,1)}), bf16[16,32,512]{2,1,0:T(8,128)(2,1)S(1)}, u32[]{:S(2)}, u32[]{:S(2)}) async-start(bf16[16,32,512]{2,1,0:T(8,128)(2,1)} %get-tuple-element.40), calls=%async_computation.1 | async-start | bytes 1048576 | tf_op jit(solution)/shard_map/all_to_all | solution.py:503
  15.4 0.0 collective-permute-done.halo_ref
  15.4 1.5 %collective-permute-start.1 = (bf16[6,2,48,512]{3,2,1,0:T(8,128)(2,1)}, bf16[6,2,48,512]{3,2,1,0:T(8,128)(2,1)S(1)}, u32[]{:S(2)}, u32[]{:S(2)}) collective-permute-start(bf16[6,2,48,512]{3,2,1,0:T(8,128)(2,1)} %get-tuple-element.37), channel_id=1, source_target_pairs={{0,126},{2,0},{4,2},{6,4},{8,6},{10,8},{12,10},{14,12},{16,14},{18... | collective-permute-start | bytes 1769480 | tf_op jit(solution)/shard_map/ppermute | solution.py:497
  16.9 0.1 reshape.124
  17.1 1.1 broadcast_in_dim_reshape.6.mcol_ref
  18.1 0.1 tile.9
  18.2 0.1 copy.23
  18.3 0.7 tile.11.mrow_ref
  19.1 0.6 collective-permute-start.2
  19.6 0.0 copy-done.9
  19.6 6.8 %shard_map.193 = bf16[32,2,8,1152]{3,2,1,0:T(8,128)(2,1)} custom-call(bf16[32,12,2,4,192]{4,3,2,1,0:T(4,128)(2,1)} %pix_ref.3, bf16[128,128]{1,0:T(8,128)(2,1)} %constant.94.clone.edge_ref, bf16[704,128]{1,0:T(8,128)(2,1)} %copy-done.9, bf16[1152,1152]{1,0:T(8,128)(2,1)} %constant.95.clone.main_ref), custom_call_target="tpu_custom_call" | custom-call | flops 6000000000 | tf_op jit(solution)/shard_map/pallas_call | solution.py:507
  26.5 0.0 copy-start.6
  26.5 0.0 all-to-all-done.1
  26.5 0.0 copy-start.3
  26.5 8.7 %all-to-all-start = ((bf16[64,8,1152]{2,1,0:T(8,128)(2,1)}), bf16[64,8,1152]{2,1,0:T(8,128)(2,1)S(1)}, u32[]{:S(2)}, u32[]{:S(2)}) async-start(bf16[64,8,1152]{2,1,0:T(8,128)(2,1)} %bitcast.29), calls=%async_computation | async-start | bytes 2359296 | tf_op jit(solution)/shard_map/all_to_all | solution.py:519
  35.2 0.7 collective-permute-start.3
  35.9 0.0 collective-permute-done.2.corner_ref
  35.9 0.0 collective-permute-done.1.ahead_ref
  36.0 0.0 copy-done.6
  36.0 0.0 copy-start.7
  36.0 0.1 broadcast_add_fusion
  36.1 1.0 add.110.idx_ref
  37.1 0.7 add.101.idxr_ref
  37.8 0.6 gather_fusion
  38.4 0.0 collective-permute-done.3.woth_ref
  38.4 0.7 broadcast_in_dim.26
  39.1 0.1 copy-done.8
  39.2 8.4 %shard_map.194 = (bf16[1024,1024]{1,0:T(8,128)(2,1)}, bf16[1152,512]{1,0:T(8,128)(2,1)}, bf16[1152,512]{1,0:T(8,128)(2,1)}) custom-call(s32[1024,1]{1,0:T(8,128)} %add.110.idx_ref, f32[256,2]{1,0:T(8,128)} %bitcast.33, bf16[512,512]{1,0:T(8,128)(2,1)} %bitcast.31, bf16[512,512]{1,0:T(8,128)(2,1)} %copy-done.8, bf16[12,2,48,512]{3,2,1,0:T(8,128)(2,1)} %cot_ref.3, ...), custom_call_target="tpu_custom_call" | custom-call | flops 8000000000 | tf_op jit(solution)/shard_map/pallas_call | solution.py:536
  47.7 6.2 %all-to-all-done = bf16[64,8,1152]{2,1,0:T(8,128)(2,1)S(1)} async-done(((bf16[64,8,1152]{2,1,0:T(8,128)(2,1)}), bf16[64,8,1152]{2,1,0:T(8,128)(2,1)S(1)}, u32[]{:S(2)}, u32[]{:S(2)}) %all-to-all-start) | async-done | bytes 1179680 | tf_op jit(solution)/shard_map/all_to_all | solution.py:519
  53.9 1.0 copy-done.1
  54.9 25.9 %shard_map.195 = (bf16[1152,512]{1,0:T(8,128)(2,1)}, bf16[1152,512]{1,0:T(8,128)(2,1)}, bf16[512,1536]{1,0:T(8,128)(2,1)}, bf16[512,1536]{1,0:T(8,128)(2,1)}) custom-call(bf16[32,2,8,1152]{3,2,1,0:T(8,128)(2,1)} %bitcast.28, s32[1,1024]{1,0:T(1,128)} %add.101.idxr_ref, f32[256,2]{1,0:T(8,128)} %bitcast.34, f32[1,512]{1,0:T(1,128)} %bitcast.40, ...), custom_call_target="tpu_custom_call" | custom-call | flops 28000000000 | tf_op jit(solution)/shard_map/pallas_call | solution.py:552
  80.8 1.4 collective-permute-start.4
  82.2 3.2 %collective-permute-done.4.right_ref = bf16[512,1536]{1,0:T(8,128)(2,1)S(1)} collective-permute-done((bf16[512,1536]{1,0:T(8,128)(2,1)}, bf16[512,1536]{1,0:T(8,128)(2,1)S(1)}, u32[]{:S(2)}, u32[]{:S(2)}) %collective-permute-start.4) | collective-permute-done | bytes 1572896 | tf_op jit(solution)/shard_map/ppermute | solution.py:600
  85.5 1.4 copy-done
  86.9 1.5 shard_map.196
  88.4 7.3 %all-to-all-start.2 = ((bf16[64,8,1536]{2,1,0:T(8,128)(2,1)}), bf16[64,8,1536]{2,1,0:T(8,128)(2,1)S(1)}, u32[]{:S(2)}, u32[]{:S(2)}) async-start(bf16[64,8,1536]{2,1,0:T(8,128)(2,1)} %bitcast.7), calls=%async_computation.2 | async-start | bytes 3145728 | tf_op jit(solution)/shard_map/all_to_all | solution.py:602
  95.7 5.9 %shard_map.197 = (bf16[576,512]{1,0:T(8,128)(2,1)}, bf16[576,512]{1,0:T(8,128)(2,1)}, bf16[48,512]{1,0:T(8,128)(2,1)}, bf16[48,512]{1,0:T(8,128)(2,1)}) custom-call(bf16[1152,512]{1,0:T(8,128)(2,1)} %get-tuple-element.48.tok_ref, bf16[1152,512]{1,0:T(8,128)(2,1)} %get-tuple-element.49.att_ref, bf16[512,512]{1,0:T(8,128)(2,1)} %wproj_ref.3, ...), custom_call_target="tpu_custom_call" | custom-call | flops 5000000000 | tf_op jit(solution)/shard_map/pallas_call | solution.py:627
  101.6 0.8 collective-permute-start.5
  102.3 2.4 %collective-permute-start.6 = (bf16[48,512]{1,0:T(8,128)(2,1)}, bf16[48,512]{1,0:T(8,128)(2,1)S(1)}, u32[]{:S(2)}, u32[]{:S(2)}) collective-permute-start(bf16[48,512]{1,0:T(8,128)(2,1)} %get-tuple-element.51), channel_id=1, source_target_pairs={{0,1},{1,0},{2,3},{3,2},{4,5},{5,4},{6,7},{7,6},{8,9},{9,8},{10,11... | collective-permute-start | bytes 147464 | tf_op jit(solution)/shard_map/ppermute | solution.py:634
  104.7 1.8 %collective-permute-start.7 = (bf16[48,512]{1,0:T(8,128)(2,1)}, bf16[48,512]{1,0:T(8,128)(2,1)S(1)}, u32[]{:S(2)}, u32[]{:S(2)}) collective-permute-start(bf16[48,512]{1,0:T(8,128)(2,1)} %get-tuple-element.52), channel_id=1, source_target_pairs={{0,3},{1,2},{2,5},{3,4},{4,7},{5,6},{6,9},{7,8},{8,11},{9,10},{10,... | collective-permute-start | bytes 147464 | tf_op jit(solution)/shard_map/ppermute | solution.py:635
  106.5 13.7 %all-to-all-done.2 = bf16[64,8,1536]{2,1,0:T(8,128)(2,1)S(1)} async-done(((bf16[64,8,1536]{2,1,0:T(8,128)(2,1)}), bf16[64,8,1536]{2,1,0:T(8,128)(2,1)S(1)}, u32[]{:S(2)}, u32[]{:S(2)}) %all-to-all-start.2) | async-done | bytes 1572896 | tf_op jit(solution)/shard_map/all_to_all | solution.py:602
  120.2 0.2 reduce_sum.12
  120.5 1.1 broadcast_in_dim.28
  121.6 4.8 %all-to-all-start.3 = ((bf16[64,8,1024]{2,1,0:T(8,128)(2,1)}), bf16[64,8,1024]{2,1,0:T(8,128)(2,1)S(1)}, u32[]{:S(2)}, u32[]{:S(2)}) async-start(bf16[64,8,1024]{2,1,0:T(8,128)(2,1)} %broadcast_in_dim.28), calls=%async_computation.3 | async-start | bytes 2097152 | tf_op jit(solution)/shard_map/all_to_all | solution.py:607
  126.4 2.5 %collective-permute-start.8 = (bf16[8,512]{1,0:T(8,128)(2,1)S(1)}, bf16[8,512]{1,0:T(8,128)(2,1)S(1)}, u32[]{:S(2)}, u32[]{:S(2)}) collective-permute-start(bf16[8,512]{1,0:T(8,128)(2,1)S(1)} %get-tuple-element.67), channel_id=1, source_target_pairs={{0,1},{1,0},{2,3},{3,2},{4,5},{5,4},{6,7},{7,6},{8,9},{9,8},{10,11... | collective-permute-start | bytes 24584 | tf_op jit(solution)/shard_map/ppermute | solution.py:614
  128.8 0.3 collective-permute-start.9
  129.1 0.0 collective-permute-done.6
  129.1 0.6 collective-permute-start.10
  129.8 0.0 collective-permute-done.7
  129.8 0.0 collective-permute-done.5
  129.9 0.1 pad_maximum_fusion
  129.9 0.6 slice.23
  130.5 1.6 %pad_maximum_fusion.1 = bf16[12,2,48,512]{3,2,1,0:T(8,128)(2,1)} fusion(bf16[12,2,45,512]{3,2,1,0:T(8,128)(2,1)S(1)} %slice.23, bf16[12,2,3,512]{3,2,1,0:T(4,128)(2,1)S(1)} %reshape.128), kind=kLoop, calls=%fused_computation.2 | loop fusion | flops 2359296 | bytes 2359296 | tf_op jit(solution)/shard_map/concatenate | solution.py:643
  132.2 6.3 %collective-permute-done.8 = bf16[8,512]{1,0:T(8,128)(2,1)S(1)} collective-permute-done((bf16[8,512]{1,0:T(8,128)(2,1)S(1)}, bf16[8,512]{1,0:T(8,128)(2,1)S(1)}, u32[]{:S(2)}, u32[]{:S(2)}) %collective-permute-start.8) | collective-permute-done | bytes 8224 | tf_op jit(solution)/shard_map/ppermute | solution.py:614
  138.5 0.0 collective-permute-done.9
  138.5 0.0 collective-permute-done.10
  138.5 0.6 convert.2
  139.1 3.7 %all-to-all-done.3 = bf16[64,8,1024]{2,1,0:T(8,128)(2,1)S(1)} async-done(((bf16[64,8,1024]{2,1,0:T(8,128)(2,1)}), bf16[64,8,1024]{2,1,0:T(8,128)(2,1)S(1)}, u32[]{:S(2)}, u32[]{:S(2)}) %all-to-all-start.3) | async-done | bytes 1048608 | tf_op jit(solution)/shard_map/all_to_all | solution.py:607
  142.9 3.6 %collective-permute-start.11 = (bf16[512,1024]{1,0:T(8,128)(2,1)S(1)}, bf16[512,1024]{1,0:T(8,128)(2,1)S(1)}, u32[]{:S(2)}, u32[]{:S(2)}) collective-permute-start(bf16[512,1024]{1,0:T(8,128)(2,1)S(1)} %bitcast.25), channel_id=1, source_target_pairs={{0,4},{4,0},{1,5},{5,1},{2,6},{6,2},{3,7},{7,3},{8,12},{12,8},{9,1... | collective-permute-start | bytes 3145736 | tf_op jit(solution)/shard_map/ppermute | solution.py:646
  146.5 2.3 %collective-permute-done.11.other_ref = bf16[512,1024]{1,0:T(8,128)(2,1)S(1)} collective-permute-done((bf16[512,1024]{1,0:T(8,128)(2,1)S(1)}, bf16[512,1024]{1,0:T(8,128)(2,1)S(1)}, u32[]{:S(2)}, u32[]{:S(2)}) %collective-permute-start.11) | collective-permute-done | bytes 1048608 | tf_op jit(solution)/shard_map/ppermute | solution.py:646
  148.8 2.1 %shard_map.198 = (f32[512,1536]{1,0:T(8,128)}, f32[512,512]{1,0:T(8,128)}) custom-call(bf16[512,1024]{1,0:T(8,128)(2,1)S(1)} %bitcast.26, bf16[512,1024]{1,0:T(8,128)(2,1)S(1)} %collective-permute-done.11.other_ref), custom_call_target="tpu_custom_call" | custom-call | flops 2000000000 | tf_op jit(solution)/shard_map/pallas_call | solution.py:647
  (30 shorter events, 0.2 us)
Async XLA Ops:
  0.6 16.3 %copy-start.4 = (s32[12,2,48]{2,1,0:T(2,128)S(1)}, s32[12,2,48]{2,1,0:T(2,128)}, u32[]{:S(2)}) copy-start(s32[12,2,48]{2,1,0:T(2,128)} %param.24) | copy-start | bytes 13828
  3.9 14.3 %copy-start.5 = (f32[64,2]{0,1:T(2,128)S(1)}, f32[64,2]{0,1:T(2,128)}, u32[]{:S(2)}) copy-start(f32[64,2]{0,1:T(2,128)} %param.20) | copy-start | bytes 1540
  3.9 15.1 %copy-start.10 = (bf16[48,512]{1,0:T(8,128)(2,1)S(1)}, bf16[48,512]{1,0:T(8,128)(2,1)}, u32[]{:S(2)}) copy-start(bf16[48,512]{1,0:T(8,128)(2,1)} %get-tuple-element.38) | copy-start | bytes 147460
  3.9 11.4 %collective-permute-start = (bf16[704,128]{1,0:T(8,128)(2,1)}, bf16[704,128]{1,0:T(8,128)(2,1)S(1)}, u32[]{:S(2)}, u32[]{:S(2)}) collective-permute-start(bf16[704,128]{1,0:T(8,128)(2,1)} %get-tuple-element.33), channel_id=1, source_target_pairs={{0,1},{1,0},{2,3},{3,2},{4,5},{5,4},{6,7},{7,6},{8,9},{9,8},{10,11... | collective-permute-start | bytes 540680 | tf_op jit(solution)/shard_map/ppermute | solution.py:495
  7.6 18.9 %all-to-all-start.1 = ((bf16[16,32,512]{2,1,0:T(8,128)(2,1)}), bf16[16,32,512]{2,1,0:T(8,128)(2,1)S(1)}, u32[]{:S(2)}, u32[]{:S(2)}) async-start(bf16[16,32,512]{2,1,0:T(8,128)(2,1)} %get-tuple-element.40), calls=%async_computation.1 | async-start | bytes 1048576 | tf_op jit(solution)/shard_map/all_to_all | solution.py:503
  15.4 4.3 %copy-start.9 = (bf16[704,128]{1,0:T(8,128)(2,1)}, bf16[704,128]{1,0:T(8,128)(2,1)S(1)}, u32[]{:S(2)}) copy-start(bf16[704,128]{1,0:T(8,128)(2,1)S(1)} %collective-permute-done.halo_ref) | copy-start | bytes 540676
  15.4 20.6 %collective-permute-start.1 = (bf16[6,2,48,512]{3,2,1,0:T(8,128)(2,1)}, bf16[6,2,48,512]{3,2,1,0:T(8,128)(2,1)S(1)}, u32[]{:S(2)}, u32[]{:S(2)}) collective-permute-start(bf16[6,2,48,512]{3,2,1,0:T(8,128)(2,1)} %get-tuple-element.37), channel_id=1, source_target_pairs={{0,126},{2,0},{4,2},{6,4},{8,6},{10,8},{12,10},{14,12},{16,14},{18... | collective-permute-start | bytes 1769480 | tf_op jit(solution)/shard_map/ppermute | solution.py:497
  19.1 16.9 %collective-permute-start.2 = (bf16[48,512]{1,0:T(8,128)(2,1)S(1)}, bf16[48,512]{1,0:T(8,128)(2,1)S(1)}, u32[]{:S(2)}, u32[]{:S(2)}) collective-permute-start(bf16[48,512]{1,0:T(8,128)(2,1)S(1)} %copy-done.10), channel_id=1, source_target_pairs={{0,127},{1,126},{2,1},{3,0},{4,3},{5,2},{6,5},{7,4},{8,7},{9,6},{1... | collective-permute-start | bytes 147464 | tf_op jit(solution)/shard_map/ppermute | solution.py:498
  26.5 9.5 %copy-start.6 = (s32[64]{0:T(128)S(1)}, s32[64]{0:T(128)}, u32[]{:S(2)}) copy-start(s32[64]{0:T(128)} %param.18) | copy-start | bytes 772
  26.5 10.6 %copy-start.3 = (bf16[16,32,512]{2,1,0:T(8,128)(2,1)}, bf16[16,32,512]{2,1,0:T(8,128)(2,1)S(1)}, u32[]{:S(2)}) copy-start(bf16[16,32,512]{2,1,0:T(8,128)(2,1)S(1)} %all-to-all-done.1) | copy-start | bytes 1572868
  26.5 27.4 %all-to-all-start = ((bf16[64,8,1152]{2,1,0:T(8,128)(2,1)}), bf16[64,8,1152]{2,1,0:T(8,128)(2,1)S(1)}, u32[]{:S(2)}, u32[]{:S(2)}) async-start(bf16[64,8,1152]{2,1,0:T(8,128)(2,1)} %bitcast.29), calls=%async_computation | async-start | bytes 2359296 | tf_op jit(solution)/shard_map/all_to_all | solution.py:519
  35.2 3.2 %collective-permute-start.3 = (bf16[512,512]{1,0:T(8,128)(2,1)S(1)}, bf16[512,512]{1,0:T(8,128)(2,1)S(1)}, u32[]{:S(2)}, u32[]{:S(2)}) collective-permute-start(bf16[512,512]{1,0:T(8,128)(2,1)S(1)} %bitcast.30), channel_id=1, source_target_pairs={{0,4},{4,0},{1,5},{5,1},{2,6},{6,2},{3,7},{7,3},{8,12},{12,8},{9,1... | collective-permute-start | bytes 1572872 | tf_op jit(solution)/shard_map/ppermute | solution.py:505
  35.9 3.2 %copy-start.11 = (bf16[48,512]{1,0:T(8,128)(2,1)}, bf16[48,512]{1,0:T(8,128)(2,1)S(1)}, u32[]{:S(2)}) copy-start(bf16[48,512]{1,0:T(8,128)(2,1)S(1)} %collective-permute-done.2.corner_ref) | copy-start | bytes 147460
  36.0 3.2 %copy-start.7 = (bf16[6,2,48,512]{3,2,1,0:T(8,128)(2,1)}, bf16[6,2,48,512]{3,2,1,0:T(8,128)(2,1)S(1)}, u32[]{:S(2)}) copy-start(bf16[6,2,48,512]{3,2,1,0:T(8,128)(2,1)S(1)} %collective-permute-done.1.ahead_ref) | copy-start | bytes 1769476
  38.4 0.9 copy-start.8
  53.9 1.0 copy-start.1
  80.8 4.7 %collective-permute-start.4 = (bf16[512,1536]{1,0:T(8,128)(2,1)}, bf16[512,1536]{1,0:T(8,128)(2,1)S(1)}, u32[]{:S(2)}, u32[]{:S(2)}) collective-permute-start(bf16[512,1536]{1,0:T(8,128)(2,1)} %get-tuple-element.47), channel_id=1, source_target_pairs={{0,4},{4,0},{1,5},{5,1},{2,6},{6,2},{3,7},{7,3},{8,12},{12,8},{9,1... | collective-permute-start | bytes 4718600 | tf_op jit(solution)/shard_map/ppermute | solution.py:600
  85.5 1.4 copy-start
  88.4 31.8 %all-to-all-start.2 = ((bf16[64,8,1536]{2,1,0:T(8,128)(2,1)}), bf16[64,8,1536]{2,1,0:T(8,128)(2,1)S(1)}, u32[]{:S(2)}, u32[]{:S(2)}) async-start(bf16[64,8,1536]{2,1,0:T(8,128)(2,1)} %bitcast.7), calls=%async_computation.2 | async-start | bytes 3145728 | tf_op jit(solution)/shard_map/all_to_all | solution.py:602
  101.6 28.2 %collective-permute-start.5 = (bf16[576,512]{1,0:T(8,128)(2,1)}, bf16[576,512]{1,0:T(8,128)(2,1)S(1)}, u32[]{:S(2)}, u32[]{:S(2)}) collective-permute-start(bf16[576,512]{1,0:T(8,128)(2,1)} %get-tuple-element.50), channel_id=1, source_target_pairs={{0,2},{2,4},{4,6},{6,8},{8,10},{10,12},{12,14},{14,16},{16,18},{18... | collective-permute-start | bytes 1769480 | tf_op jit(solution)/shard_map/ppermute | solution.py:633
  102.3 26.8 %collective-permute-start.6 = (bf16[48,512]{1,0:T(8,128)(2,1)}, bf16[48,512]{1,0:T(8,128)(2,1)S(1)}, u32[]{:S(2)}, u32[]{:S(2)}) collective-permute-start(bf16[48,512]{1,0:T(8,128)(2,1)} %get-tuple-element.51), channel_id=1, source_target_pairs={{0,1},{1,0},{2,3},{3,2},{4,5},{5,4},{6,7},{7,6},{8,9},{9,8},{10,11... | collective-permute-start | bytes 147464 | tf_op jit(solution)/shard_map/ppermute | solution.py:634
  104.7 25.0 %collective-permute-start.7 = (bf16[48,512]{1,0:T(8,128)(2,1)}, bf16[48,512]{1,0:T(8,128)(2,1)S(1)}, u32[]{:S(2)}, u32[]{:S(2)}) collective-permute-start(bf16[48,512]{1,0:T(8,128)(2,1)} %get-tuple-element.52), channel_id=1, source_target_pairs={{0,3},{1,2},{2,5},{3,4},{4,7},{5,6},{6,9},{7,8},{8,11},{9,10},{10,... | collective-permute-start | bytes 147464 | tf_op jit(solution)/shard_map/ppermute | solution.py:635
  121.6 8.3 %copy-start.2 = (bf16[576,512]{1,0:T(8,128)(2,1)S(1)}, bf16[576,512]{1,0:T(8,128)(2,1)}, u32[]{:S(2)}) copy-start(bf16[576,512]{1,0:T(8,128)(2,1)} %get-tuple-element.56) | copy-start | bytes 1769476
  121.6 21.3 %all-to-all-start.3 = ((bf16[64,8,1024]{2,1,0:T(8,128)(2,1)}), bf16[64,8,1024]{2,1,0:T(8,128)(2,1)S(1)}, u32[]{:S(2)}, u32[]{:S(2)}) async-start(bf16[64,8,1024]{2,1,0:T(8,128)(2,1)} %broadcast_in_dim.28), calls=%async_computation.3 | async-start | bytes 2097152 | tf_op jit(solution)/shard_map/all_to_all | solution.py:607
  126.4 12.1 %collective-permute-start.8 = (bf16[8,512]{1,0:T(8,128)(2,1)S(1)}, bf16[8,512]{1,0:T(8,128)(2,1)S(1)}, u32[]{:S(2)}, u32[]{:S(2)}) collective-permute-start(bf16[8,512]{1,0:T(8,128)(2,1)S(1)} %get-tuple-element.67), channel_id=1, source_target_pairs={{0,1},{1,0},{2,3},{3,2},{4,5},{5,4},{6,7},{7,6},{8,9},{9,8},{10,11... | collective-permute-start | bytes 24584 | tf_op jit(solution)/shard_map/ppermute | solution.py:614
  128.8 9.6 %collective-permute-start.9 = (bf16[8,512]{1,0:T(8,128)(2,1)S(1)}, bf16[8,512]{1,0:T(8,128)(2,1)S(1)}, u32[]{:S(2)}, u32[]{:S(2)}) collective-permute-start(bf16[8,512]{1,0:T(8,128)(2,1)S(1)} %get-tuple-element.67), channel_id=1, source_target_pairs={{0,2},{1,3},{2,0},{3,1},{4,6},{5,7},{6,4},{7,5},{8,10},{9,11},{10,... | collective-permute-start | bytes 24584 | tf_op jit(solution)/shard_map/ppermute | solution.py:614
  129.1 9.3 %collective-permute-start.10 = (bf16[8,512]{1,0:T(8,128)(2,1)S(1)}, bf16[8,512]{1,0:T(8,128)(2,1)S(1)}, u32[]{:S(2)}, u32[]{:S(2)}) collective-permute-start(bf16[8,512]{1,0:T(8,128)(2,1)S(1)} %get-tuple-element.67), channel_id=1, source_target_pairs={{0,3},{1,2},{2,1},{3,0},{4,7},{5,6},{6,5},{7,4},{8,11},{9,10},{10,... | collective-permute-start | bytes 24584 | tf_op jit(solution)/shard_map/ppermute | solution.py:614
  142.9 5.9 %collective-permute-start.11 = (bf16[512,1024]{1,0:T(8,128)(2,1)S(1)}, bf16[512,1024]{1,0:T(8,128)(2,1)S(1)}, u32[]{:S(2)}, u32[]{:S(2)}) collective-permute-start(bf16[512,1024]{1,0:T(8,128)(2,1)S(1)} %bitcast.25), channel_id=1, source_target_pairs={{0,4},{4,0},{1,5},{5,1},{2,6},{6,2},{3,7},{7,3},{8,12},{12,8},{9,1... | collective-permute-start | bytes 3145736 | tf_op jit(solution)/shard_map/ppermute | solution.py:646

commit v5 on v4

--- a/solution.py
+++ b/solution.py
@@ -136,44 +136,35 @@
     copies_ref[...] = jnp.broadcast_to(weight_ref[...][None], copies_ref.shape)
 
 
-def store_half(out_ref, half, lat, lanes, block):
-    bands = out_ref.shape[0]
-    if half == 1:
-        out_ref[:, lat, :, lanes] = block
-        return
-
-    @pl.when(lat == 0)
-    def _():
-        out_ref[: bands - 1, 1, :, lanes] = block[1:]
-        out_ref[bands - 1 :, 1, :, lanes] = block[:1]
-
-    @pl.when(lat == 1)
-    def _():
-        out_ref[:, 0, :, lanes] = block
-
-
-def pack_kernel(pix_ref, edge_ref, halo_ref, main_ref, out_ref, rows_s, main_s, sem):
-    move = pltpu.make_async_copy(main_ref, main_s, sem)
+def pack_kernel(pix_ref, edge_ref, halo_ref, main_ref, out_ref, rows_s, main_s, out_s, sems):
+    move = pltpu.make_async_copy(main_ref, main_s, sems.at[0])
     move.start()
     lat = lax.axis_index("lat")
     bands = out_ref.shape[0]
     size = bands * 8
+    moves = []
     for half in range(2):
         for i in range(HALF // 2):
             pair = [half_rows(pix_ref, half, 2 * i + k, 4 * COLS) for k in range(2)]
-            rows_s[half * size : half * size + size, 384 * i : 384 * i + 384] = jnp.concatenate(
-                pair, axis=1
-            ).astype(BF)
-    move.wait()
-    for n in range(3):
-        lanes = slice(384 * n, 384 * n + 384)
-        block = dot(rows_s[...], main_s[:, lanes])
-        if n == 2:
-            halo = dot(halo_ref[: 2 * size, :], edge_ref[...])
-            block = jnp.concatenate([block[:, :256], block[:, 256:] + halo], axis=1)
-        for half in range(2):
-            part = block[half * size : half * size + size].reshape(bands, 8, 384).astype(BF)
-            store_half(out_ref, half, lat, lanes, part)
+            rows_s[half, :, 384 * i : 384 * i + 384] = jnp.concatenate(pair, axis=1).astype(BF)
+        if half == 0:
+            move.wait()
+        for n in range(3):
+            lanes = slice(384 * n, 384 * n + 384)
+            block = dot(rows_s[half], main_s[:, lanes])
+            if n == 2:
+                halo = dot(halo_ref[half * size : half * size + size, :], edge_ref[...])
+                block = jnp.concatenate([block[:, :256], block[:, 256:] + halo], axis=1)
+            block = block.reshape(bands, 8, 384)
+            if half == 0:
+                later = jnp.concatenate([block[1:], block[:1]], axis=0)
+                block = jnp.where(lat == 0, later, block)
+            out_s[half, :, :, lanes] = block.astype(BF)
+        target = lat if half == 1 else 1 - lat
+        moves.append(pltpu.make_async_copy(out_s.at[half], out_ref.at[:, target], sems.at[1 + half]))
+        moves[half].start()
+    for move in moves:
+        move.wait()
 
 
 def prepare_kernel(
@@ -409,21 +400,27 @@
     out_ref[...] = (left_ref[...].astype(F32) + right_ref[...].astype(F32)).astype(BF)
 
 
-def join_kernel(mine_ref, other_ref, qkv_far, proj_far, qkv_s, proj_s, sems):
-    core = lax.axis_index("core")
+def join_half(part, ref, qkv_far, proj_far, qkv_s, proj_s, sems):
     moves = []
-    for i, ref in enumerate((mine_ref, other_ref)):
-        for near, far, lanes in ((qkv_s, qkv_far, slice(0, 768)), (proj_s, proj_far, slice(768, 1024))):
-            width = near.shape[2]
-            near[i] = ref[:, lanes].astype(F32)
-            at = pl.multiple_of((core ^ i) * width, 256)
-            move = pltpu.make_async_copy(near.at[i], far.at[:, pl.ds(at, width)], sems.at[len(moves)])
-            move.start()
-            moves.append(move)
+    for near, far, first in ((qkv_s, qkv_far, 0), (proj_s, proj_far, 768)):
+        width = near.shape[1]
+        near[...] = ref[:, first : first + width].astype(F32)
+        at = pl.multiple_of((lax.axis_index("core") ^ part) * width, 256)
+        move = pltpu.make_async_copy(near, far.at[:, pl.ds(at, width)], sems.at[len(moves)])
+        move.start()
+        moves.append(move)
     for move in moves:
         move.wait()
 
 
+def own_kernel(mine_ref, *rest):
+    join_half(0, mine_ref, *rest)
+
+
+def other_kernel(other_ref, qkv_in, proj_in, *rest):
+    join_half(1, other_ref, *rest)
+
+
 def shape(*dims, dtype=BF):
     return jax.ShapeDtypeStruct(dims, dtype)
 
@@ -432,7 +429,7 @@
     return pl.CostEstimate(flops=int(us * 1e9), bytes_accessed=0, transcendentals=0)
 
 
-def vmem_call(kernel, outs, scratch=(), count=0, far=(), far_out=(), mib=58, us=1):
+def vmem_call(kernel, outs, scratch=(), count=0, far=(), far_out=(), mib=58, us=1, aliases=None):
     def spec(is_far):
         return pl.BlockSpec(memory_space=pl.ANY if is_far else pltpu.VMEM)
 
@@ -443,6 +440,7 @@
         in_specs=[spec(i in far) for i in range(count)],
         out_specs=[spec(i in far_out) for i in range(len(outs))] if many else spec(False),
         scratch_shapes=list(scratch),
+        input_output_aliases=aliases or {},
         compiler_params=pltpu.CompilerParams(vmem_limit_bytes=mib * 1024 * 1024),
         cost_estimate=cost(us),
     )
@@ -504,16 +502,18 @@
     own_weight = own_weight.reshape(512, D)
     oth_weight = lax.ppermute(own_weight, "core", swap_core)
 
-    packed = vmem_call(
+    (packed,) = vmem_call(
         pack_kernel,
-        shape(bands, 2, 8, LANES),
+        [shape(bands, 2, 8, LANES)],
         [
-            pltpu.VMEM((2 * bands * 8, LANES), BF),
+            pltpu.VMEM((2, bands * 8, LANES), BF),
             pltpu.VMEM((LANES, LANES), BF),
-            pltpu.SemaphoreType.DMA,
+            pltpu.VMEM((2, bands, 8, LANES), BF),
+            pltpu.SemaphoreType.DMA((3,)),
         ],
         count=4,
         far=(3,),
+        far_out=(0,),
         us=6,
     )(pixels, jnp.asarray(edge, BF), halo, jnp.asarray(main, BF))
     recv = lax.all_to_all(
@@ -644,19 +644,16 @@
 
     mine, block_out, grad_embed = lax.optimization_barrier((mine, block_out, grad_embed))
     other = lax.ppermute(mine, "core", swap_core)
+    full = [shape(512, 1536, dtype=F32), shape(512, 512, dtype=F32)]
+    room = [
+        pltpu.VMEM((512, 768), F32),
+        pltpu.VMEM((512, 256), F32),
+        pltpu.SemaphoreType.DMA((2,)),
+    ]
+    own = vmem_call(own_kernel, full, room, count=1, far_out=(0, 1), mib=10, us=2)(mine)
     grad_qkv, grad_proj = vmem_call(
-        join_kernel,
-        [shape(512, 1536, dtype=F32), shape(512, 512, dtype=F32)],
-        [
-            pltpu.VMEM((2, 512, 768), F32),
-            pltpu.VMEM((2, 512, 256), F32),
-            pltpu.SemaphoreType.DMA((4,)),
-        ],
-        count=2,
-        far_out=(0, 1),
-        mib=10,
-        us=2,
-    )(mine, other)
+        other_kernel, full, room, 3, (1, 2), (0, 1), mib=10, us=2, aliases={1: 0, 2: 1}
+    )(other, *own)
     return (block_out, grad_embed, grad_qkv, grad_proj)
 
 

time: 152 us -> 151 us (level)
    pallas_call x2 -> x3, Pallas kernels: 8.95 us -> 9.03 us  [the longest x1 6.17 us: per_device(): vmem_call(pack_kernel, [shape(bands, 2, 8, LANES)], [pltpu.VMEM((2, bands...]
  transfers between devices with their start and end apart: 16 -> 16, of which waited for: 6 -> 6; matrix products, arithmetic and copies ran while one was open for 6% -> 6% of each run, Pallas kernels for 14% -> 15%
where the time goes in v5:
time: 151 us; the launch traced here: 150 us
  Pallas kernels  54 us (36%)
  starting transfers between devices  49 us (32%)
  waiting for transfers between devices  34 us (23%)
  local copies, waits for them, and re-layouts  9.45 us (6%)
  other arithmetic  2.74 us (2%)
    pallas_call x1, Pallas kernels, per_device(): vmem_call(block_kernel, [shape(TOKENS, D), shape(TOKENS, D), shape(512, 1...  25.9 us
    all_to_all x1, waiting for transfers between devices, per_device(): lax.all_to_all(chip_sum.reshape(group_size, 8, 1536), group, split_axis=0...  13.7 us
    all_to_all x1, starting transfers between devices, per_device(): lax.all_to_all(packed.reshape(bands * 2, 8, LANES), rows_ring, split_axis...  9.37 us
    pallas_call x1, Pallas kernels, per_device(): vmem_call(prepare_kernel, [shape(1024, 1024), shape(TOKENS, D), shape(TOK...  8.43 us
    all_to_all x1, starting transfers between devices, per_device(): lax.all_to_all(copies, 'chip', split_axis=0, concat_axis=0, tiled=True)  7.77 us
    all_to_all x1, starting transfers between devices, per_device(): lax.all_to_all(chip_sum.reshape(group_size, 8, 1536), group, split_axis=0...  7.31 us
    ppermute x3, waiting for transfers between devices, per_device(): lax.ppermute(embed_part, ('lat', 'lon'), [(i * 2 + k, (i ^ dlat) * 2 + (k...  6.3 us
    all_to_all x1, waiting for transfers between devices, per_device(): lax.all_to_all(packed.reshape(bands * 2, 8, LANES), rows_ring, split_axis...  6.19 us
  transfers between devices with their start and end apart: 16, of which 6 were waited for; matrix products, arithmetic and copies ran while one was open for 6% of the time, Pallas kernels for 15%

profile of v5, /device:TPU:1, one launch (start us, length us, event | category | flops | bytes accessed | tf_op | source)
XLA Modules:
  0.0 150.4 jit_solution(14335333625261334165)
XLA Ops:
  0.6 0.0 copy-start.4
  0.6 3.3 %shard_map.192 = (bf16[704,128]{1,0:T(8,128)(2,1)}, bf16[6,2,48,512]{3,2,1,0:T(8,128)(2,1)}, bf16[48,512]{1,0:T(8,128)(2,1)}, bf16[16,32,512]{2,1,0:T(8,128)(2,1)}) custom-call(bf16[32,12,2,4,192]{4,3,2,1,0:T(4,128)(2,1)} %pix_ref.3, bf16[12,2,48,512]{3,2,1,0:T(8,128)(2,1)} %cot_ref.3, bf16[32,512]{1,0:T(8,128)(2,1)} %bitcast.39, ...), custom_call_target="tpu_custom_call" | custom-call | flops 3000000000 | tf_op jit(solution)/shard_map/pallas_call | solution.py:476
  3.9 3.7 %collective-permute-start = (bf16[704,128]{1,0:T(8,128)(2,1)}, bf16[704,128]{1,0:T(8,128)(2,1)S(1)}, u32[]{:S(2)}, u32[]{:S(2)}) collective-permute-start(bf16[704,128]{1,0:T(8,128)(2,1)} %get-tuple-element.35), channel_id=1, source_target_pairs={{0,1},{1,0},{2,3},{3,2},{4,5},{5,4},{6,7},{7,6},{8,9},{9,8},{10,11... | collective-permute-start | bytes 540680 | tf_op jit(solution)/shard_map/ppermute | solution.py:493
  7.6 7.8 %all-to-all-start.1 = ((bf16[16,32,512]{2,1,0:T(8,128)(2,1)}), bf16[16,32,512]{2,1,0:T(8,128)(2,1)S(1)}, u32[]{:S(2)}, u32[]{:S(2)}) async-start(bf16[16,32,512]{2,1,0:T(8,128)(2,1)} %get-tuple-element.42), calls=%async_computation.1 | async-start | bytes 1048576 | tf_op jit(solution)/shard_map/all_to_all | solution.py:501
  15.4 0.0 collective-permute-done.halo_ref
  15.4 1.5 %collective-permute-start.1 = (bf16[6,2,48,512]{3,2,1,0:T(8,128)(2,1)}, bf16[6,2,48,512]{3,2,1,0:T(8,128)(2,1)S(1)}, u32[]{:S(2)}, u32[]{:S(2)}) collective-permute-start(bf16[6,2,48,512]{3,2,1,0:T(8,128)(2,1)} %get-tuple-element.39), channel_id=1, source_target_pairs={{0,126},{2,0},{4,2},{6,4},{8,6},{10,8},{12,10},{14,12},{16,14},{18... | collective-permute-start | bytes 1769480 | tf_op jit(solution)/shard_map/ppermute | solution.py:495
  16.9 0.1 reshape.124
  17.1 1.1 broadcast_in_dim_reshape.6.mcol_ref
  18.1 0.1 tile.9
  18.2 0.1 copy.25
  18.3 0.7 tile.11.mrow_ref
  19.1 0.6 collective-permute-start.2
  19.6 6.2 %shard_map.193 = bf16[32,2,8,1152]{3,2,1,0:T(8,128)(2,1)} custom-call(bf16[32,12,2,4,192]{4,3,2,1,0:T(4,128)(2,1)} %pix_ref.3, bf16[128,128]{1,0:T(8,128)(2,1)} %constant.94.clone.edge_ref, bf16[704,128]{1,0:T(8,128)(2,1)} %copy-done.9, bf16[1152,1152]{1,0:T(8,128)(2,1)} %constant.95.clone.main_ref), custom_call_target="tpu_custom_call" | custom-call | flops 6000000000 | tf_op jit(solution)/shard_map/pallas_call | solution.py:505
  25.8 0.0 copy-start.6
  25.8 0.0 all-to-all-done.1
  25.9 9.4 %all-to-all-start = ((bf16[64,8,1152]{2,1,0:T(8,128)(2,1)}), bf16[64,8,1152]{2,1,0:T(8,128)(2,1)S(1)}, u32[]{:S(2)}, u32[]{:S(2)}) async-start(bf16[64,8,1152]{2,1,0:T(8,128)(2,1)} %bitcast.29), calls=%async_computation | async-start | bytes 2359296 | tf_op jit(solution)/shard_map/all_to_all | solution.py:519
  35.2 0.7 collective-permute-start.3
  35.9 0.0 collective-permute-done.2.corner_ref
  35.9 0.0 collective-permute-done.1.ahead_ref
  36.0 0.0 copy-done.6
  36.0 0.0 copy-start.7
  36.0 0.1 broadcast_add_fusion
  36.1 1.0 add.110.idx_ref
  37.1 0.7 add.101.idxr_ref
  37.8 0.6 gather_fusion
  38.4 0.0 collective-permute-done.3.woth_ref
  38.4 0.7 broadcast_in_dim.26
  39.1 0.1 copy-done.8
  39.2 8.4 %shard_map.194 = (bf16[1024,1024]{1,0:T(8,128)(2,1)}, bf16[1152,512]{1,0:T(8,128)(2,1)}, bf16[1152,512]{1,0:T(8,128)(2,1)}) custom-call(s32[1024,1]{1,0:T(8,128)} %add.110.idx_ref, f32[256,2]{1,0:T(8,128)} %bitcast.33, bf16[512,512]{1,0:T(8,128)(2,1)} %bitcast.31, bf16[512,512]{1,0:T(8,128)(2,1)} %copy-done.8, bf16[12,2,48,512]{3,2,1,0:T(8,128)(2,1)} %cot_ref.3, ...), custom_call_target="tpu_custom_call" | custom-call | flops 8000000000 | tf_op jit(solution)/shard_map/pallas_call | solution.py:536
  47.7 6.2 %all-to-all-done = bf16[64,8,1152]{2,1,0:T(8,128)(2,1)S(1)} async-done(((bf16[64,8,1152]{2,1,0:T(8,128)(2,1)}), bf16[64,8,1152]{2,1,0:T(8,128)(2,1)S(1)}, u32[]{:S(2)}, u32[]{:S(2)}) %all-to-all-start) | async-done | bytes 1179680 | tf_op jit(solution)/shard_map/all_to_all | solution.py:519
  53.9 1.0 copy-done.1
  54.9 25.9 %shard_map.195 = (bf16[1152,512]{1,0:T(8,128)(2,1)}, bf16[1152,512]{1,0:T(8,128)(2,1)}, bf16[512,1536]{1,0:T(8,128)(2,1)}, bf16[512,1536]{1,0:T(8,128)(2,1)}) custom-call(bf16[32,2,8,1152]{3,2,1,0:T(8,128)(2,1)} %bitcast.28, s32[1,1024]{1,0:T(1,128)} %add.101.idxr_ref, f32[256,2]{1,0:T(8,128)} %bitcast.34, f32[1,512]{1,0:T(1,128)} %bitcast.40, ...), custom_call_target="tpu_custom_call" | custom-call | flops 28000000000 | tf_op jit(solution)/shard_map/pallas_call | solution.py:552
  80.8 1.4 collective-permute-start.4
  82.3 3.2 %collective-permute-done.4.right_ref = bf16[512,1536]{1,0:T(8,128)(2,1)S(1)} collective-permute-done((bf16[512,1536]{1,0:T(8,128)(2,1)}, bf16[512,1536]{1,0:T(8,128)(2,1)S(1)}, u32[]{:S(2)}, u32[]{:S(2)}) %collective-permute-start.4) | collective-permute-done | bytes 1572896 | tf_op jit(solution)/shard_map/ppermute | solution.py:600
  85.5 1.4 copy-done
  86.9 1.5 shard_map.196
  88.4 7.3 %all-to-all-start.2 = ((bf16[64,8,1536]{2,1,0:T(8,128)(2,1)}), bf16[64,8,1536]{2,1,0:T(8,128)(2,1)S(1)}, u32[]{:S(2)}, u32[]{:S(2)}) async-start(bf16[64,8,1536]{2,1,0:T(8,128)(2,1)} %bitcast.7), calls=%async_computation.2 | async-start | bytes 3145728 | tf_op jit(solution)/shard_map/all_to_all | solution.py:602
  95.7 5.9 %shard_map.197 = (bf16[576,512]{1,0:T(8,128)(2,1)}, bf16[576,512]{1,0:T(8,128)(2,1)}, bf16[48,512]{1,0:T(8,128)(2,1)}, bf16[48,512]{1,0:T(8,128)(2,1)}) custom-call(bf16[1152,512]{1,0:T(8,128)(2,1)} %get-tuple-element.50.tok_ref, bf16[1152,512]{1,0:T(8,128)(2,1)} %get-tuple-element.51.att_ref, bf16[512,512]{1,0:T(8,128)(2,1)} %wproj_ref.3, ...), custom_call_target="tpu_custom_call" | custom-call | flops 5000000000 | tf_op jit(solution)/shard_map/pallas_call | solution.py:627
  101.6 0.8 collective-permute-start.5
  102.4 2.4 %collective-permute-start.6 = (bf16[48,512]{1,0:T(8,128)(2,1)}, bf16[48,512]{1,0:T(8,128)(2,1)S(1)}, u32[]{:S(2)}, u32[]{:S(2)}) collective-permute-start(bf16[48,512]{1,0:T(8,128)(2,1)} %get-tuple-element.53), channel_id=1, source_target_pairs={{0,1},{1,0},{2,3},{3,2},{4,5},{5,4},{6,7},{7,6},{8,9},{9,8},{10,11... | collective-permute-start | bytes 147464 | tf_op jit(solution)/shard_map/ppermute | solution.py:634
  104.8 1.8 %collective-permute-start.7 = (bf16[48,512]{1,0:T(8,128)(2,1)}, bf16[48,512]{1,0:T(8,128)(2,1)S(1)}, u32[]{:S(2)}, u32[]{:S(2)}) collective-permute-start(bf16[48,512]{1,0:T(8,128)(2,1)} %get-tuple-element.54), channel_id=1, source_target_pairs={{0,3},{1,2},{2,5},{3,4},{4,7},{5,6},{6,9},{7,8},{8,11},{9,10},{10,... | collective-permute-start | bytes 147464 | tf_op jit(solution)/shard_map/ppermute | solution.py:635
  106.5 13.7 %all-to-all-done.2 = bf16[64,8,1536]{2,1,0:T(8,128)(2,1)S(1)} async-done(((bf16[64,8,1536]{2,1,0:T(8,128)(2,1)}), bf16[64,8,1536]{2,1,0:T(8,128)(2,1)S(1)}, u32[]{:S(2)}, u32[]{:S(2)}) %all-to-all-start.2) | async-done | bytes 1572896 | tf_op jit(solution)/shard_map/all_to_all | solution.py:602
  120.2 0.2 reduce_sum.12
  120.5 1.1 broadcast_in_dim.28
  121.6 4.8 %all-to-all-start.3 = ((bf16[64,8,1024]{2,1,0:T(8,128)(2,1)}), bf16[64,8,1024]{2,1,0:T(8,128)(2,1)S(1)}, u32[]{:S(2)}, u32[]{:S(2)}) async-start(bf16[64,8,1024]{2,1,0:T(8,128)(2,1)} %broadcast_in_dim.28), calls=%async_computation.3 | async-start | bytes 2097152 | tf_op jit(solution)/shard_map/all_to_all | solution.py:607
  126.4 2.5 %collective-permute-start.8 = (bf16[8,512]{1,0:T(8,128)(2,1)S(1)}, bf16[8,512]{1,0:T(8,128)(2,1)S(1)}, u32[]{:S(2)}, u32[]{:S(2)}) collective-permute-start(bf16[8,512]{1,0:T(8,128)(2,1)S(1)} %get-tuple-element.71), channel_id=1, source_target_pairs={{0,1},{1,0},{2,3},{3,2},{4,5},{5,4},{6,7},{7,6},{8,9},{9,8},{10,11... | collective-permute-start | bytes 24584 | tf_op jit(solution)/shard_map/ppermute | solution.py:614
  128.9 0.3 collective-permute-start.9
  129.2 0.0 collective-permute-done.6
  129.2 0.6 collective-permute-start.10
  129.8 0.0 collective-permute-done.7
  129.8 0.0 collective-permute-done.5
  129.9 0.0 copy-done.2
  129.9 0.1 pad_maximum_fusion
  130.0 0.6 slice.23
  130.5 1.6 %pad_maximum_fusion.1 = bf16[12,2,48,512]{3,2,1,0:T(8,128)(2,1)} fusion(bf16[12,2,45,512]{3,2,1,0:T(8,128)(2,1)S(1)} %slice.23, bf16[12,2,3,512]{3,2,1,0:T(4,128)(2,1)S(1)} %reshape.128), kind=kLoop, calls=%fused_computation.2 | loop fusion | flops 2359296 | bytes 2359296 | tf_op jit(solution)/shard_map/concatenate | solution.py:643
  132.2 6.3 %collective-permute-done.8 = bf16[8,512]{1,0:T(8,128)(2,1)S(1)} collective-permute-done((bf16[8,512]{1,0:T(8,128)(2,1)S(1)}, bf16[8,512]{1,0:T(8,128)(2,1)S(1)}, u32[]{:S(2)}, u32[]{:S(2)}) %collective-permute-start.8) | collective-permute-done | bytes 8224 | tf_op jit(solution)/shard_map/ppermute | solution.py:614
  138.5 0.0 collective-permute-done.9
  138.5 0.0 collective-permute-done.10
  138.5 0.6 convert.2
  139.2 3.7 %all-to-all-done.3 = bf16[64,8,1024]{2,1,0:T(8,128)(2,1)S(1)} async-done(((bf16[64,8,1024]{2,1,0:T(8,128)(2,1)}), bf16[64,8,1024]{2,1,0:T(8,128)(2,1)S(1)}, u32[]{:S(2)}, u32[]{:S(2)}) %all-to-all-start.3) | async-done | bytes 1048608 | tf_op jit(solution)/shard_map/all_to_all | solution.py:607
  142.9 3.6 %collective-permute-start.11 = (bf16[512,1024]{1,0:T(8,128)(2,1)S(1)}, bf16[512,1024]{1,0:T(8,128)(2,1)S(1)}, u32[]{:S(2)}, u32[]{:S(2)}) collective-permute-start(bf16[512,1024]{1,0:T(8,128)(2,1)S(1)} %bitcast.25), channel_id=1, source_target_pairs={{0,4},{4,0},{1,5},{5,1},{2,6},{6,2},{3,7},{7,3},{8,12},{12,8},{9,1... | collective-permute-start | bytes 3145736 | tf_op jit(solution)/shard_map/ppermute | solution.py:646
  146.5 1.4 shard_map.198
  147.9 0.8 collective-permute-done.11.other_ref
  148.8 1.4 shard_map.199
  (31 shorter events, 0.2 us)
Async XLA Ops:
  0.6 16.3 %copy-start.4 = (s32[12,2,48]{2,1,0:T(2,128)S(1)}, s32[12,2,48]{2,1,0:T(2,128)}, u32[]{:S(2)}) copy-start(s32[12,2,48]{2,1,0:T(2,128)} %param.24) | copy-start | bytes 13828
  3.9 14.3 %copy-start.5 = (f32[64,2]{0,1:T(2,128)S(1)}, f32[64,2]{0,1:T(2,128)}, u32[]{:S(2)}) copy-start(f32[64,2]{0,1:T(2,128)} %param.20) | copy-start | bytes 1540
  3.9 15.1 %copy-start.10 = (bf16[48,512]{1,0:T(8,128)(2,1)S(1)}, bf16[48,512]{1,0:T(8,128)(2,1)}, u32[]{:S(2)}) copy-start(bf16[48,512]{1,0:T(8,128)(2,1)} %get-tuple-element.40) | copy-start | bytes 147460
  3.9 11.4 %collective-permute-start = (bf16[704,128]{1,0:T(8,128)(2,1)}, bf16[704,128]{1,0:T(8,128)(2,1)S(1)}, u32[]{:S(2)}, u32[]{:S(2)}) collective-permute-start(bf16[704,128]{1,0:T(8,128)(2,1)} %get-tuple-element.35), channel_id=1, source_target_pairs={{0,1},{1,0},{2,3},{3,2},{4,5},{5,4},{6,7},{7,6},{8,9},{9,8},{10,11... | collective-permute-start | bytes 540680 | tf_op jit(solution)/shard_map/ppermute | solution.py:493
  7.6 18.3 %all-to-all-start.1 = ((bf16[16,32,512]{2,1,0:T(8,128)(2,1)}), bf16[16,32,512]{2,1,0:T(8,128)(2,1)S(1)}, u32[]{:S(2)}, u32[]{:S(2)}) async-start(bf16[16,32,512]{2,1,0:T(8,128)(2,1)} %get-tuple-element.42), calls=%async_computation.1 | async-start | bytes 1048576 | tf_op jit(solution)/shard_map/all_to_all | solution.py:501
  15.4 4.3 %copy-start.9 = (bf16[704,128]{1,0:T(8,128)(2,1)}, bf16[704,128]{1,0:T(8,128)(2,1)S(1)}, u32[]{:S(2)}) copy-start(bf16[704,128]{1,0:T(8,128)(2,1)S(1)} %collective-permute-done.halo_ref) | copy-start | bytes 540676
  15.4 20.6 %collective-permute-start.1 = (bf16[6,2,48,512]{3,2,1,0:T(8,128)(2,1)}, bf16[6,2,48,512]{3,2,1,0:T(8,128)(2,1)S(1)}, u32[]{:S(2)}, u32[]{:S(2)}) collective-permute-start(bf16[6,2,48,512]{3,2,1,0:T(8,128)(2,1)} %get-tuple-element.39), channel_id=1, source_target_pairs={{0,126},{2,0},{4,2},{6,4},{8,6},{10,8},{12,10},{14,12},{16,14},{18... | collective-permute-start | bytes 1769480 | tf_op jit(solution)/shard_map/ppermute | solution.py:495
  19.1 16.9 %collective-permute-start.2 = (bf16[48,512]{1,0:T(8,128)(2,1)S(1)}, bf16[48,512]{1,0:T(8,128)(2,1)S(1)}, u32[]{:S(2)}, u32[]{:S(2)}) collective-permute-start(bf16[48,512]{1,0:T(8,128)(2,1)S(1)} %copy-done.10), channel_id=1, source_target_pairs={{0,127},{1,126},{2,1},{3,0},{4,3},{5,2},{6,5},{7,4},{8,7},{9,6},{1... | collective-permute-start | bytes 147464 | tf_op jit(solution)/shard_map/ppermute | solution.py:496
  25.8 10.1 %copy-start.6 = (s32[64]{0:T(128)S(1)}, s32[64]{0:T(128)}, u32[]{:S(2)}) copy-start(s32[64]{0:T(128)} %param.18) | copy-start | bytes 772
  25.8 11.2 %copy-start.3 = (bf16[16,32,512]{2,1,0:T(8,128)(2,1)}, bf16[16,32,512]{2,1,0:T(8,128)(2,1)S(1)}, u32[]{:S(2)}) copy-start(bf16[16,32,512]{2,1,0:T(8,128)(2,1)S(1)} %all-to-all-done.1) | copy-start | bytes 1572868
  25.9 28.0 %all-to-all-start = ((bf16[64,8,1152]{2,1,0:T(8,128)(2,1)}), bf16[64,8,1152]{2,1,0:T(8,128)(2,1)S(1)}, u32[]{:S(2)}, u32[]{:S(2)}) async-start(bf16[64,8,1152]{2,1,0:T(8,128)(2,1)} %bitcast.29), calls=%async_computation | async-start | bytes 2359296 | tf_op jit(solution)/shard_map/all_to_all | solution.py:519
  35.2 3.2 %collective-permute-start.3 = (bf16[512,512]{1,0:T(8,128)(2,1)S(1)}, bf16[512,512]{1,0:T(8,128)(2,1)S(1)}, u32[]{:S(2)}, u32[]{:S(2)}) collective-permute-start(bf16[512,512]{1,0:T(8,128)(2,1)S(1)} %bitcast.30), channel_id=1, source_target_pairs={{0,4},{4,0},{1,5},{5,1},{2,6},{6,2},{3,7},{7,3},{8,12},{12,8},{9,1... | collective-permute-start | bytes 1572872 | tf_op jit(solution)/shard_map/ppermute | solution.py:503
  35.9 3.2 %copy-start.11 = (bf16[48,512]{1,0:T(8,128)(2,1)}, bf16[48,512]{1,0:T(8,128)(2,1)S(1)}, u32[]{:S(2)}) copy-start(bf16[48,512]{1,0:T(8,128)(2,1)S(1)} %collective-permute-done.2.corner_ref) | copy-start | bytes 147460
  36.0 3.2 %copy-start.7 = (bf16[6,2,48,512]{3,2,1,0:T(8,128)(2,1)}, bf16[6,2,48,512]{3,2,1,0:T(8,128)(2,1)S(1)}, u32[]{:S(2)}) copy-start(bf16[6,2,48,512]{3,2,1,0:T(8,128)(2,1)S(1)} %collective-permute-done.1.ahead_ref) | copy-start | bytes 1769476
  38.4 0.8 copy-start.8
  53.9 1.0 copy-start.1
  80.8 4.7 %collective-permute-start.4 = (bf16[512,1536]{1,0:T(8,128)(2,1)}, bf16[512,1536]{1,0:T(8,128)(2,1)S(1)}, u32[]{:S(2)}, u32[]{:S(2)}) collective-permute-start(bf16[512,1536]{1,0:T(8,128)(2,1)} %get-tuple-element.49), channel_id=1, source_target_pairs={{0,4},{4,0},{1,5},{5,1},{2,6},{6,2},{3,7},{7,3},{8,12},{12,8},{9,1... | collective-permute-start | bytes 4718600 | tf_op jit(solution)/shard_map/ppermute | solution.py:600
  85.5 1.4 copy-start
  88.4 31.8 %all-to-all-start.2 = ((bf16[64,8,1536]{2,1,0:T(8,128)(2,1)}), bf16[64,8,1536]{2,1,0:T(8,128)(2,1)S(1)}, u32[]{:S(2)}, u32[]{:S(2)}) async-start(bf16[64,8,1536]{2,1,0:T(8,128)(2,1)} %bitcast.7), calls=%async_computation.2 | async-start | bytes 3145728 | tf_op jit(solution)/shard_map/all_to_all | solution.py:602
  101.6 28.2 %collective-permute-start.5 = (bf16[576,512]{1,0:T(8,128)(2,1)}, bf16[576,512]{1,0:T(8,128)(2,1)S(1)}, u32[]{:S(2)}, u32[]{:S(2)}) collective-permute-start(bf16[576,512]{1,0:T(8,128)(2,1)} %get-tuple-element.52), channel_id=1, source_target_pairs={{0,2},{2,4},{4,6},{6,8},{8,10},{10,12},{12,14},{14,16},{16,18},{18... | collective-permute-start | bytes 1769480 | tf_op jit(solution)/shard_map/ppermute | solution.py:633
  102.4 26.8 %collective-permute-start.6 = (bf16[48,512]{1,0:T(8,128)(2,1)}, bf16[48,512]{1,0:T(8,128)(2,1)S(1)}, u32[]{:S(2)}, u32[]{:S(2)}) collective-permute-start(bf16[48,512]{1,0:T(8,128)(2,1)} %get-tuple-element.53), channel_id=1, source_target_pairs={{0,1},{1,0},{2,3},{3,2},{4,5},{5,4},{6,7},{7,6},{8,9},{9,8},{10,11... | collective-permute-start | bytes 147464 | tf_op jit(solution)/shard_map/ppermute | solution.py:634
  104.8 25.0 %collective-permute-start.7 = (bf16[48,512]{1,0:T(8,128)(2,1)}, bf16[48,512]{1,0:T(8,128)(2,1)S(1)}, u32[]{:S(2)}, u32[]{:S(2)}) collective-permute-start(bf16[48,512]{1,0:T(8,128)(2,1)} %get-tuple-element.54), channel_id=1, source_target_pairs={{0,3},{1,2},{2,5},{3,4},{4,7},{5,6},{6,9},{7,8},{8,11},{9,10},{10,... | collective-permute-start | bytes 147464 | tf_op jit(solution)/shard_map/ppermute | solution.py:635
  121.6 8.3 %copy-start.2 = (bf16[576,512]{1,0:T(8,128)(2,1)S(1)}, bf16[576,512]{1,0:T(8,128)(2,1)}, u32[]{:S(2)}) copy-start(bf16[576,512]{1,0:T(8,128)(2,1)} %get-tuple-element.58) | copy-start | bytes 1769476
  121.6 21.3 %all-to-all-start.3 = ((bf16[64,8,1024]{2,1,0:T(8,128)(2,1)}), bf16[64,8,1024]{2,1,0:T(8,128)(2,1)S(1)}, u32[]{:S(2)}, u32[]{:S(2)}) async-start(bf16[64,8,1024]{2,1,0:T(8,128)(2,1)} %broadcast_in_dim.28), calls=%async_computation.3 | async-start | bytes 2097152 | tf_op jit(solution)/shard_map/all_to_all | solution.py:607
  126.4 12.1 %collective-permute-start.8 = (bf16[8,512]{1,0:T(8,128)(2,1)S(1)}, bf16[8,512]{1,0:T(8,128)(2,1)S(1)}, u32[]{:S(2)}, u32[]{:S(2)}) collective-permute-start(bf16[8,512]{1,0:T(8,128)(2,1)S(1)} %get-tuple-element.71), channel_id=1, source_target_pairs={{0,1},{1,0},{2,3},{3,2},{4,5},{5,4},{6,7},{7,6},{8,9},{9,8},{10,11... | collective-permute-start | bytes 24584 | tf_op jit(solution)/shard_map/ppermute | solution.py:614
  128.9 9.6 %collective-permute-start.9 = (bf16[8,512]{1,0:T(8,128)(2,1)S(1)}, bf16[8,512]{1,0:T(8,128)(2,1)S(1)}, u32[]{:S(2)}, u32[]{:S(2)}) collective-permute-start(bf16[8,512]{1,0:T(8,128)(2,1)S(1)} %get-tuple-element.71), channel_id=1, source_target_pairs={{0,2},{1,3},{2,0},{3,1},{4,6},{5,7},{6,4},{7,5},{8,10},{9,11},{10,... | collective-permute-start | bytes 24584 | tf_op jit(solution)/shard_map/ppermute | solution.py:614
  129.2 9.3 %collective-permute-start.10 = (bf16[8,512]{1,0:T(8,128)(2,1)S(1)}, bf16[8,512]{1,0:T(8,128)(2,1)S(1)}, u32[]{:S(2)}, u32[]{:S(2)}) collective-permute-start(bf16[8,512]{1,0:T(8,128)(2,1)S(1)} %get-tuple-element.71), channel_id=1, source_target_pairs={{0,3},{1,2},{2,1},{3,0},{4,7},{5,6},{6,5},{7,4},{8,11},{9,10},{10,... | collective-permute-start | bytes 24584 | tf_op jit(solution)/shard_map/ppermute | solution.py:614
  142.9 5.9 %collective-permute-start.11 = (bf16[512,1024]{1,0:T(8,128)(2,1)S(1)}, bf16[512,1024]{1,0:T(8,128)(2,1)S(1)}, u32[]{:S(2)}, u32[]{:S(2)}) collective-permute-start(bf16[512,1024]{1,0:T(8,128)(2,1)S(1)} %bitcast.25), channel_id=1, source_target_pairs={{0,4},{4,0},{1,5},{5,1},{2,6},{6,2},{3,7},{7,3},{8,12},{12,8},{9,1... | collective-permute-start | bytes 3145736 | tf_op jit(solution)/shard_map/ppermute | solution.py:646

commit v6 on v5

--- a/solution.py
+++ b/solution.py
@@ -397,7 +397,7 @@
 
 
 def add_kernel(left_ref, right_ref, out_ref):
-    out_ref[...] = (left_ref[...].astype(F32) + right_ref[...].astype(F32)).astype(BF)
+    out_ref[...] = (left_ref[...] + right_ref[...].astype(F32)).astype(BF)
 
 
 def join_half(part, ref, qkv_far, proj_far, qkv_s, proj_s, sems):
@@ -598,7 +598,8 @@
     )
 
     from_core = lax.ppermute(goth, "core", swap_core)
-    chip_sum = vmem_call(add_kernel, shape(512, 1536), count=2, mib=7, us=2)(gown, from_core)
+    wide = gown.astype(F32)
+    chip_sum = vmem_call(add_kernel, shape(512, 1536), count=2, mib=12, us=2)(wide, from_core)
     terms = lax.all_to_all(
         chip_sum.reshape(group_size, 8, 1536), group, split_axis=0, concat_axis=0, tiled=True
     )

time: 151 us -> 150 us (level)
  waiting for transfers between devices: 34 us -> 32.2 us
  other arithmetic: 2.74 us -> 4.53 us
    ppermute x1, waiting for transfers between devices: 3.25 us -> 1.44 us  [per_device(): from_core = lax.ppermute(goth, 'core', swap_core)]
    convert_element_type x0 -> x1, other arithmetic: none -> 1.8 us  [per_device(): wide = gown.astype(F32)]
  transfers between devices with their start and end apart: 16 -> 16, of which waited for: 6 -> 6; matrix products, arithmetic and copies ran while one was open for 6% -> 8% of each run, Pallas kernels for 15% -> 15%
where the time goes in v6:
time: 150 us; the launch traced here: 149 us
  Pallas kernels  53.9 us (36%)
  starting transfers between devices  49 us (33%)
  waiting for transfers between devices  32.2 us (21%)
  local copies, waits for them, and re-layouts  8.04 us (5%)
  other arithmetic  4.53 us (3%)
    pallas_call x1, Pallas kernels, per_device(): vmem_call(block_kernel, [shape(TOKENS, D), shape(TOKENS, D), shape(512, 1...  25.9 us
    all_to_all x1, waiting for transfers between devices, per_device(): lax.all_to_all(chip_sum.reshape(group_size, 8, 1536), group, split_axis=0...  13.7 us
    all_to_all x1, starting transfers between devices, per_device(): lax.all_to_all(packed.reshape(bands * 2, 8, LANES), rows_ring, split_axis...  9.37 us
    pallas_call x1, Pallas kernels, per_device(): vmem_call(prepare_kernel, [shape(1024, 1024), shape(TOKENS, D), shape(TOK...  8.43 us
    all_to_all x1, starting transfers between devices, per_device(): lax.all_to_all(copies, 'chip', split_axis=0, concat_axis=0, tiled=True)  7.77 us
    all_to_all x1, starting transfers between devices, per_device(): lax.all_to_all(chip_sum.reshape(group_size, 8, 1536), group, split_axis=0...  7.31 us
    ppermute x3, waiting for transfers between devices, per_device(): lax.ppermute(embed_part, ('lat', 'lon'), [(i * 2 + k, (i ^ dlat) * 2 + (k...  6.3 us
    all_to_all x1, waiting for transfers between devices, per_device(): lax.all_to_all(packed.reshape(bands * 2, 8, LANES), rows_ring, split_axis...  6.19 us
  transfers between devices with their start and end apart: 16, of which 6 were waited for; matrix products, arithmetic and copies ran while one was open for 8% of the time, Pallas kernels for 15%

profile of v6, /device:TPU:1, one launch (start us, length us, event | category | flops | bytes accessed | tf_op | source)
XLA Modules:
  0.0 148.9 jit_solution(5616151420024180608)
XLA Ops:
  0.6 3.3 %shard_map.192 = (bf16[704,128]{1,0:T(8,128)(2,1)}, bf16[6,2,48,512]{3,2,1,0:T(8,128)(2,1)}, bf16[48,512]{1,0:T(8,128)(2,1)}, bf16[16,32,512]{2,1,0:T(8,128)(2,1)}) custom-call(bf16[32,12,2,4,192]{4,3,2,1,0:T(4,128)(2,1)} %pix_ref.3, bf16[12,2,48,512]{3,2,1,0:T(8,128)(2,1)} %cot_ref.3, bf16[32,512]{1,0:T(8,128)(2,1)} %bitcast.39, ...), custom_call_target="tpu_custom_call" | custom-call | flops 3000000000 | tf_op jit(solution)/shard_map/pallas_call | solution.py:476
  3.9 3.7 %collective-permute-start = (bf16[704,128]{1,0:T(8,128)(2,1)}, bf16[704,128]{1,0:T(8,128)(2,1)S(1)}, u32[]{:S(2)}, u32[]{:S(2)}) collective-permute-start(bf16[704,128]{1,0:T(8,128)(2,1)} %get-tuple-element.35), channel_id=1, source_target_pairs={{0,1},{1,0},{2,3},{3,2},{4,5},{5,4},{6,7},{7,6},{8,9},{9,8},{10,11... | collective-permute-start | bytes 540680 | tf_op jit(solution)/shard_map/ppermute | solution.py:493
  7.6 7.8 %all-to-all-start.1 = ((bf16[16,32,512]{2,1,0:T(8,128)(2,1)}), bf16[16,32,512]{2,1,0:T(8,128)(2,1)S(1)}, u32[]{:S(2)}, u32[]{:S(2)}) async-start(bf16[16,32,512]{2,1,0:T(8,128)(2,1)} %get-tuple-element.42), calls=%async_computation.1 | async-start | bytes 1048576 | tf_op jit(solution)/shard_map/all_to_all | solution.py:501
  15.4 0.0 collective-permute-done.halo_ref
  15.4 1.5 %collective-permute-start.1 = (bf16[6,2,48,512]{3,2,1,0:T(8,128)(2,1)}, bf16[6,2,48,512]{3,2,1,0:T(8,128)(2,1)S(1)}, u32[]{:S(2)}, u32[]{:S(2)}) collective-permute-start(bf16[6,2,48,512]{3,2,1,0:T(8,128)(2,1)} %get-tuple-element.39), channel_id=1, source_target_pairs={{0,126},{2,0},{4,2},{6,4},{8,6},{10,8},{12,10},{14,12},{16,14},{18... | collective-permute-start | bytes 1769480 | tf_op jit(solution)/shard_map/ppermute | solution.py:495
  16.9 0.1 reshape.124
  17.1 1.1 broadcast_in_dim_reshape.6.mcol_ref
  18.1 0.1 tile.9
  18.2 0.1 copy.25
  18.3 0.7 tile.11.mrow_ref
  19.1 0.6 collective-permute-start.2
  19.6 0.0 copy-done.8
  19.6 6.2 %shard_map.193 = bf16[32,2,8,1152]{3,2,1,0:T(8,128)(2,1)} custom-call(bf16[32,12,2,4,192]{4,3,2,1,0:T(4,128)(2,1)} %pix_ref.3, bf16[128,128]{1,0:T(8,128)(2,1)} %constant.94.clone.edge_ref, bf16[704,128]{1,0:T(8,128)(2,1)} %copy-done.8, bf16[1152,1152]{1,0:T(8,128)(2,1)} %constant.95.clone.main_ref), custom_call_target="tpu_custom_call" | custom-call | flops 6000000000 | tf_op jit(solution)/shard_map/pallas_call | solution.py:505
  25.8 0.0 copy-start.5
  25.8 0.0 all-to-all-done.1
  25.8 9.4 %all-to-all-start = ((bf16[64,8,1152]{2,1,0:T(8,128)(2,1)}), bf16[64,8,1152]{2,1,0:T(8,128)(2,1)S(1)}, u32[]{:S(2)}, u32[]{:S(2)}) async-start(bf16[64,8,1152]{2,1,0:T(8,128)(2,1)} %bitcast.29), calls=%async_computation | async-start | bytes 2359296 | tf_op jit(solution)/shard_map/all_to_all | solution.py:519
  35.2 0.7 collective-permute-start.3
  35.9 0.0 collective-permute-done.2.corner_ref
  35.9 0.0 collective-permute-done.1.ahead_ref
  36.0 0.0 copy-done.5
  36.0 0.0 copy-start.6
  36.0 0.1 broadcast_add_fusion
  36.1 1.0 add.110.idx_ref
  37.1 0.7 add.101.idxr_ref
  37.8 0.6 gather_fusion
  38.4 0.0 collective-permute-done.3.woth_ref
  38.4 0.7 broadcast_in_dim.26
  39.1 0.0 copy-done.10
  39.1 0.1 copy-done.7
  39.2 8.4 %shard_map.194 = (bf16[1024,1024]{1,0:T(8,128)(2,1)}, bf16[1152,512]{1,0:T(8,128)(2,1)}, bf16[1152,512]{1,0:T(8,128)(2,1)}) custom-call(s32[1024,1]{1,0:T(8,128)} %add.110.idx_ref, f32[256,2]{1,0:T(8,128)} %bitcast.33, bf16[512,512]{1,0:T(8,128)(2,1)} %bitcast.31, bf16[512,512]{1,0:T(8,128)(2,1)} %copy-done.7, bf16[12,2,48,512]{3,2,1,0:T(8,128)(2,1)} %cot_ref.3, ...), custom_call_target="tpu_custom_call" | custom-call | flops 8000000000 | tf_op jit(solution)/shard_map/pallas_call | solution.py:536
  47.7 6.2 %all-to-all-done = bf16[64,8,1152]{2,1,0:T(8,128)(2,1)S(1)} async-done(((bf16[64,8,1152]{2,1,0:T(8,128)(2,1)}), bf16[64,8,1152]{2,1,0:T(8,128)(2,1)S(1)}, u32[]{:S(2)}, u32[]{:S(2)}) %all-to-all-start) | async-done | bytes 1179680 | tf_op jit(solution)/shard_map/all_to_all | solution.py:519
  53.9 1.0 copy-done
  54.9 25.9 %shard_map.195 = (bf16[1152,512]{1,0:T(8,128)(2,1)}, bf16[1152,512]{1,0:T(8,128)(2,1)}, bf16[512,1536]{1,0:T(8,128)(2,1)}, bf16[512,1536]{1,0:T(8,128)(2,1)}) custom-call(bf16[32,2,8,1152]{3,2,1,0:T(8,128)(2,1)} %bitcast.28, s32[1,1024]{1,0:T(1,128)} %add.101.idxr_ref, f32[256,2]{1,0:T(8,128)} %bitcast.34, f32[1,512]{1,0:T(1,128)} %bitcast.40, ...), custom_call_target="tpu_custom_call" | custom-call | flops 28000000000 | tf_op jit(solution)/shard_map/pallas_call | solution.py:552
  80.8 1.4 collective-permute-start.4
  82.2 1.8 %convert_element_type.11.left_ref = f32[512,1536]{1,0:T(8,128)S(1)} convert(bf16[512,1536]{1,0:T(8,128)(2,1)} %get-tuple-element.48) | non-fusion elementwise | flops 786432 | bytes 4718592 | tf_op jit(solution)/shard_map/convert_element_type | solution.py:601
  84.0 1.4 collective-permute-done.4.right_ref
  85.5 1.4 shard_map.196
  86.9 7.3 %all-to-all-start.2 = ((bf16[64,8,1536]{2,1,0:T(8,128)(2,1)}), bf16[64,8,1536]{2,1,0:T(8,128)(2,1)S(1)}, u32[]{:S(2)}, u32[]{:S(2)}) async-start(bf16[64,8,1536]{2,1,0:T(8,128)(2,1)} %bitcast.7), calls=%async_computation.2 | async-start | bytes 3145728 | tf_op jit(solution)/shard_map/all_to_all | solution.py:603
  94.2 5.9 %shard_map.197 = (bf16[576,512]{1,0:T(8,128)(2,1)}, bf16[576,512]{1,0:T(8,128)(2,1)}, bf16[48,512]{1,0:T(8,128)(2,1)}, bf16[48,512]{1,0:T(8,128)(2,1)}) custom-call(bf16[1152,512]{1,0:T(8,128)(2,1)} %get-tuple-element.50.tok_ref, bf16[1152,512]{1,0:T(8,128)(2,1)} %get-tuple-element.51.att_ref, bf16[512,512]{1,0:T(8,128)(2,1)} %wproj_ref.3, ...), custom_call_target="tpu_custom_call" | custom-call | flops 5000000000 | tf_op jit(solution)/shard_map/pallas_call | solution.py:628
  100.1 0.7 collective-permute-start.5
  100.8 2.4 %collective-permute-start.6 = (bf16[48,512]{1,0:T(8,128)(2,1)}, bf16[48,512]{1,0:T(8,128)(2,1)S(1)}, u32[]{:S(2)}, u32[]{:S(2)}) collective-permute-start(bf16[48,512]{1,0:T(8,128)(2,1)} %get-tuple-element.53), channel_id=1, source_target_pairs={{0,1},{1,0},{2,3},{3,2},{4,5},{5,4},{6,7},{7,6},{8,9},{9,8},{10,11... | collective-permute-start | bytes 147464 | tf_op jit(solution)/shard_map/ppermute | solution.py:635
  103.2 1.8 %collective-permute-start.7 = (bf16[48,512]{1,0:T(8,128)(2,1)}, bf16[48,512]{1,0:T(8,128)(2,1)S(1)}, u32[]{:S(2)}, u32[]{:S(2)}) collective-permute-start(bf16[48,512]{1,0:T(8,128)(2,1)} %get-tuple-element.54), channel_id=1, source_target_pairs={{0,3},{1,2},{2,5},{3,4},{4,7},{5,6},{6,9},{7,8},{8,11},{9,10},{10,... | collective-permute-start | bytes 147464 | tf_op jit(solution)/shard_map/ppermute | solution.py:636
  105.0 13.7 %all-to-all-done.2 = bf16[64,8,1536]{2,1,0:T(8,128)(2,1)S(1)} async-done(((bf16[64,8,1536]{2,1,0:T(8,128)(2,1)}), bf16[64,8,1536]{2,1,0:T(8,128)(2,1)S(1)}, u32[]{:S(2)}, u32[]{:S(2)}) %all-to-all-start.2) | async-done | bytes 1572896 | tf_op jit(solution)/shard_map/all_to_all | solution.py:603
  118.7 0.2 reduce_sum.12
  119.0 1.1 broadcast_in_dim.28
  120.1 4.8 %all-to-all-start.3 = ((bf16[64,8,1024]{2,1,0:T(8,128)(2,1)}), bf16[64,8,1024]{2,1,0:T(8,128)(2,1)S(1)}, u32[]{:S(2)}, u32[]{:S(2)}) async-start(bf16[64,8,1024]{2,1,0:T(8,128)(2,1)} %broadcast_in_dim.28), calls=%async_computation.3 | async-start | bytes 2097152 | tf_op jit(solution)/shard_map/all_to_all | solution.py:608
  124.9 2.5 %collective-permute-start.8 = (bf16[8,512]{1,0:T(8,128)(2,1)S(1)}, bf16[8,512]{1,0:T(8,128)(2,1)S(1)}, u32[]{:S(2)}, u32[]{:S(2)}) collective-permute-start(bf16[8,512]{1,0:T(8,128)(2,1)S(1)} %get-tuple-element.71), channel_id=1, source_target_pairs={{0,1},{1,0},{2,3},{3,2},{4,5},{5,4},{6,7},{7,6},{8,9},{9,8},{10,11... | collective-permute-start | bytes 24584 | tf_op jit(solution)/shard_map/ppermute | solution.py:615
  127.3 0.3 collective-permute-start.9
  127.6 0.0 collective-permute-done.6
  127.6 0.6 collective-permute-start.10
  128.2 0.0 collective-permute-done.7
  128.2 0.0 collective-permute-done.5
  128.4 0.1 pad_maximum_fusion
  128.4 0.6 slice.23
  129.0 1.6 %pad_maximum_fusion.1 = bf16[12,2,48,512]{3,2,1,0:T(8,128)(2,1)} fusion(bf16[12,2,45,512]{3,2,1,0:T(8,128)(2,1)S(1)} %slice.23, bf16[12,2,3,512]{3,2,1,0:T(4,128)(2,1)S(1)} %reshape.128), kind=kLoop, calls=%fused_computation.2 | loop fusion | flops 2359296 | bytes 2359296 | tf_op jit(solution)/shard_map/concatenate | solution.py:644
  130.7 6.3 %collective-permute-done.8 = bf16[8,512]{1,0:T(8,128)(2,1)S(1)} collective-permute-done((bf16[8,512]{1,0:T(8,128)(2,1)S(1)}, bf16[8,512]{1,0:T(8,128)(2,1)S(1)}, u32[]{:S(2)}, u32[]{:S(2)}) %collective-permute-start.8) | collective-permute-done | bytes 8224 | tf_op jit(solution)/shard_map/ppermute | solution.py:615
  136.9 0.0 collective-permute-done.9
  137.0 0.0 collective-permute-done.10
  137.0 0.6 convert.2
  137.6 3.7 %all-to-all-done.3 = bf16[64,8,1024]{2,1,0:T(8,128)(2,1)S(1)} async-done(((bf16[64,8,1024]{2,1,0:T(8,128)(2,1)}), bf16[64,8,1024]{2,1,0:T(8,128)(2,1)S(1)}, u32[]{:S(2)}, u32[]{:S(2)}) %all-to-all-start.3) | async-done | bytes 1048608 | tf_op jit(solution)/shard_map/all_to_all | solution.py:608
  141.4 3.6 %collective-permute-start.11 = (bf16[512,1024]{1,0:T(8,128)(2,1)S(1)}, bf16[512,1024]{1,0:T(8,128)(2,1)S(1)}, u32[]{:S(2)}, u32[]{:S(2)}) collective-permute-start(bf16[512,1024]{1,0:T(8,128)(2,1)S(1)} %bitcast.25), channel_id=1, source_target_pairs={{0,4},{4,0},{1,5},{5,1},{2,6},{6,2},{3,7},{7,3},{8,12},{12,8},{9,1... | collective-permute-start | bytes 3145736 | tf_op jit(solution)/shard_map/ppermute | solution.py:647
  145.0 1.4 shard_map.198
  146.4 0.8 collective-permute-done.11.other_ref
  147.2 1.4 shard_map.199
  (30 shorter events, 0.2 us)
Async XLA Ops:
  0.6 16.3 %copy-start.3 = (s32[12,2,48]{2,1,0:T(2,128)S(1)}, s32[12,2,48]{2,1,0:T(2,128)}, u32[]{:S(2)}) copy-start(s32[12,2,48]{2,1,0:T(2,128)} %param.24) | copy-start | bytes 13828
  3.9 14.3 %copy-start.4 = (f32[64,2]{0,1:T(2,128)S(1)}, f32[64,2]{0,1:T(2,128)}, u32[]{:S(2)}) copy-start(f32[64,2]{0,1:T(2,128)} %param.20) | copy-start | bytes 1540
  3.9 15.1 %copy-start.9 = (bf16[48,512]{1,0:T(8,128)(2,1)S(1)}, bf16[48,512]{1,0:T(8,128)(2,1)}, u32[]{:S(2)}) copy-start(bf16[48,512]{1,0:T(8,128)(2,1)} %get-tuple-element.40) | copy-start | bytes 147460
  3.9 11.4 %collective-permute-start = (bf16[704,128]{1,0:T(8,128)(2,1)}, bf16[704,128]{1,0:T(8,128)(2,1)S(1)}, u32[]{:S(2)}, u32[]{:S(2)}) collective-permute-start(bf16[704,128]{1,0:T(8,128)(2,1)} %get-tuple-element.35), channel_id=1, source_target_pairs={{0,1},{1,0},{2,3},{3,2},{4,5},{5,4},{6,7},{7,6},{8,9},{9,8},{10,11... | collective-permute-start | bytes 540680 | tf_op jit(solution)/shard_map/ppermute | solution.py:493
  7.6 18.2 %all-to-all-start.1 = ((bf16[16,32,512]{2,1,0:T(8,128)(2,1)}), bf16[16,32,512]{2,1,0:T(8,128)(2,1)S(1)}, u32[]{:S(2)}, u32[]{:S(2)}) async-start(bf16[16,32,512]{2,1,0:T(8,128)(2,1)} %get-tuple-element.42), calls=%async_computation.1 | async-start | bytes 1048576 | tf_op jit(solution)/shard_map/all_to_all | solution.py:501
  15.4 4.3 %copy-start.8 = (bf16[704,128]{1,0:T(8,128)(2,1)}, bf16[704,128]{1,0:T(8,128)(2,1)S(1)}, u32[]{:S(2)}) copy-start(bf16[704,128]{1,0:T(8,128)(2,1)S(1)} %collective-permute-done.halo_ref) | copy-start | bytes 540676
  15.4 20.6 %collective-permute-start.1 = (bf16[6,2,48,512]{3,2,1,0:T(8,128)(2,1)}, bf16[6,2,48,512]{3,2,1,0:T(8,128)(2,1)S(1)}, u32[]{:S(2)}, u32[]{:S(2)}) collective-permute-start(bf16[6,2,48,512]{3,2,1,0:T(8,128)(2,1)} %get-tuple-element.39), channel_id=1, source_target_pairs={{0,126},{2,0},{4,2},{6,4},{8,6},{10,8},{12,10},{14,12},{16,14},{18... | collective-permute-start | bytes 1769480 | tf_op jit(solution)/shard_map/ppermute | solution.py:495
  19.1 16.9 %collective-permute-start.2 = (bf16[48,512]{1,0:T(8,128)(2,1)S(1)}, bf16[48,512]{1,0:T(8,128)(2,1)S(1)}, u32[]{:S(2)}, u32[]{:S(2)}) collective-permute-start(bf16[48,512]{1,0:T(8,128)(2,1)S(1)} %copy-done.9), channel_id=1, source_target_pairs={{0,127},{1,126},{2,1},{3,0},{4,3},{5,2},{6,5},{7,4},{8,7},{9,6},{1... | collective-permute-start | bytes 147464 | tf_op jit(solution)/shard_map/ppermute | solution.py:496
  25.8 10.1 %copy-start.5 = (s32[64]{0:T(128)S(1)}, s32[64]{0:T(128)}, u32[]{:S(2)}) copy-start(s32[64]{0:T(128)} %param.18) | copy-start | bytes 772
  25.8 11.2 %copy-start.2 = (bf16[16,32,512]{2,1,0:T(8,128)(2,1)}, bf16[16,32,512]{2,1,0:T(8,128)(2,1)S(1)}, u32[]{:S(2)}) copy-start(bf16[16,32,512]{2,1,0:T(8,128)(2,1)S(1)} %all-to-all-done.1) | copy-start | bytes 1572868
  25.8 28.0 %all-to-all-start = ((bf16[64,8,1152]{2,1,0:T(8,128)(2,1)}), bf16[64,8,1152]{2,1,0:T(8,128)(2,1)S(1)}, u32[]{:S(2)}, u32[]{:S(2)}) async-start(bf16[64,8,1152]{2,1,0:T(8,128)(2,1)} %bitcast.29), calls=%async_computation | async-start | bytes 2359296 | tf_op jit(solution)/shard_map/all_to_all | solution.py:519
  35.2 3.2 %collective-permute-start.3 = (bf16[512,512]{1,0:T(8,128)(2,1)S(1)}, bf16[512,512]{1,0:T(8,128)(2,1)S(1)}, u32[]{:S(2)}, u32[]{:S(2)}) collective-permute-start(bf16[512,512]{1,0:T(8,128)(2,1)S(1)} %bitcast.30), channel_id=1, source_target_pairs={{0,4},{4,0},{1,5},{5,1},{2,6},{6,2},{3,7},{7,3},{8,12},{12,8},{9,1... | collective-permute-start | bytes 1572872 | tf_op jit(solution)/shard_map/ppermute | solution.py:503
  35.9 3.2 %copy-start.10 = (bf16[48,512]{1,0:T(8,128)(2,1)}, bf16[48,512]{1,0:T(8,128)(2,1)S(1)}, u32[]{:S(2)}) copy-start(bf16[48,512]{1,0:T(8,128)(2,1)S(1)} %collective-permute-done.2.corner_ref) | copy-start | bytes 147460
  36.0 3.2 %copy-start.6 = (bf16[6,2,48,512]{3,2,1,0:T(8,128)(2,1)}, bf16[6,2,48,512]{3,2,1,0:T(8,128)(2,1)S(1)}, u32[]{:S(2)}) copy-start(bf16[6,2,48,512]{3,2,1,0:T(8,128)(2,1)S(1)} %collective-permute-done.1.ahead_ref) | copy-start | bytes 1769476
  38.4 0.9 copy-start.7
  53.9 1.0 copy-start
  80.8 4.7 %collective-permute-start.4 = (bf16[512,1536]{1,0:T(8,128)(2,1)}, bf16[512,1536]{1,0:T(8,128)(2,1)S(1)}, u32[]{:S(2)}, u32[]{:S(2)}) collective-permute-start(bf16[512,1536]{1,0:T(8,128)(2,1)} %get-tuple-element.49), channel_id=1, source_target_pairs={{0,4},{4,0},{1,5},{5,1},{2,6},{6,2},{3,7},{7,3},{8,12},{12,8},{9,1... | collective-permute-start | bytes 4718600 | tf_op jit(solution)/shard_map/ppermute | solution.py:600
  86.9 31.8 %all-to-all-start.2 = ((bf16[64,8,1536]{2,1,0:T(8,128)(2,1)}), bf16[64,8,1536]{2,1,0:T(8,128)(2,1)S(1)}, u32[]{:S(2)}, u32[]{:S(2)}) async-start(bf16[64,8,1536]{2,1,0:T(8,128)(2,1)} %bitcast.7), calls=%async_computation.2 | async-start | bytes 3145728 | tf_op jit(solution)/shard_map/all_to_all | solution.py:603
  100.1 28.2 %collective-permute-start.5 = (bf16[576,512]{1,0:T(8,128)(2,1)}, bf16[576,512]{1,0:T(8,128)(2,1)S(1)}, u32[]{:S(2)}, u32[]{:S(2)}) collective-permute-start(bf16[576,512]{1,0:T(8,128)(2,1)} %get-tuple-element.52), channel_id=1, source_target_pairs={{0,2},{2,4},{4,6},{6,8},{8,10},{10,12},{12,14},{14,16},{16,18},{18... | collective-permute-start | bytes 1769480 | tf_op jit(solution)/shard_map/ppermute | solution.py:634
  100.8 26.8 %collective-permute-start.6 = (bf16[48,512]{1,0:T(8,128)(2,1)}, bf16[48,512]{1,0:T(8,128)(2,1)S(1)}, u32[]{:S(2)}, u32[]{:S(2)}) collective-permute-start(bf16[48,512]{1,0:T(8,128)(2,1)} %get-tuple-element.53), channel_id=1, source_target_pairs={{0,1},{1,0},{2,3},{3,2},{4,5},{5,4},{6,7},{7,6},{8,9},{9,8},{10,11... | collective-permute-start | bytes 147464 | tf_op jit(solution)/shard_map/ppermute | solution.py:635
  103.2 25.0 %collective-permute-start.7 = (bf16[48,512]{1,0:T(8,128)(2,1)}, bf16[48,512]{1,0:T(8,128)(2,1)S(1)}, u32[]{:S(2)}, u32[]{:S(2)}) collective-permute-start(bf16[48,512]{1,0:T(8,128)(2,1)} %get-tuple-element.54), channel_id=1, source_target_pairs={{0,3},{1,2},{2,5},{3,4},{4,7},{5,6},{6,9},{7,8},{8,11},{9,10},{10,... | collective-permute-start | bytes 147464 | tf_op jit(solution)/shard_map/ppermute | solution.py:636
  120.0 8.3 %copy-start.1 = (bf16[576,512]{1,0:T(8,128)(2,1)S(1)}, bf16[576,512]{1,0:T(8,128)(2,1)}, u32[]{:S(2)}) copy-start(bf16[576,512]{1,0:T(8,128)(2,1)} %get-tuple-element.58) | copy-start | bytes 1769476
  120.1 21.3 %all-to-all-start.3 = ((bf16[64,8,1024]{2,1,0:T(8,128)(2,1)}), bf16[64,8,1024]{2,1,0:T(8,128)(2,1)S(1)}, u32[]{:S(2)}, u32[]{:S(2)}) async-start(bf16[64,8,1024]{2,1,0:T(8,128)(2,1)} %broadcast_in_dim.28), calls=%async_computation.3 | async-start | bytes 2097152 | tf_op jit(solution)/shard_map/all_to_all | solution.py:608
  124.9 12.1 %collective-permute-start.8 = (bf16[8,512]{1,0:T(8,128)(2,1)S(1)}, bf16[8,512]{1,0:T(8,128)(2,1)S(1)}, u32[]{:S(2)}, u32[]{:S(2)}) collective-permute-start(bf16[8,512]{1,0:T(8,128)(2,1)S(1)} %get-tuple-element.71), channel_id=1, source_target_pairs={{0,1},{1,0},{2,3},{3,2},{4,5},{5,4},{6,7},{7,6},{8,9},{9,8},{10,11... | collective-permute-start | bytes 24584 | tf_op jit(solution)/shard_map/ppermute | solution.py:615
  127.3 9.6 %collective-permute-start.9 = (bf16[8,512]{1,0:T(8,128)(2,1)S(1)}, bf16[8,512]{1,0:T(8,128)(2,1)S(1)}, u32[]{:S(2)}, u32[]{:S(2)}) collective-permute-start(bf16[8,512]{1,0:T(8,128)(2,1)S(1)} %get-tuple-element.71), channel_id=1, source_target_pairs={{0,2},{1,3},{2,0},{3,1},{4,6},{5,7},{6,4},{7,5},{8,10},{9,11},{10,... | collective-permute-start | bytes 24584 | tf_op jit(solution)/shard_map/ppermute | solution.py:615
  127.6 9.3 %collective-permute-start.10 = (bf16[8,512]{1,0:T(8,128)(2,1)S(1)}, bf16[8,512]{1,0:T(8,128)(2,1)S(1)}, u32[]{:S(2)}, u32[]{:S(2)}) collective-permute-start(bf16[8,512]{1,0:T(8,128)(2,1)S(1)} %get-tuple-element.71), channel_id=1, source_target_pairs={{0,3},{1,2},{2,1},{3,0},{4,7},{5,6},{6,5},{7,4},{8,11},{9,10},{10,... | collective-permute-start | bytes 24584 | tf_op jit(solution)/shard_map/ppermute | solution.py:615
  141.4 5.9 %collective-permute-start.11 = (bf16[512,1024]{1,0:T(8,128)(2,1)S(1)}, bf16[512,1024]{1,0:T(8,128)(2,1)S(1)}, u32[]{:S(2)}, u32[]{:S(2)}) collective-permute-start(bf16[512,1024]{1,0:T(8,128)(2,1)S(1)} %bitcast.25), channel_id=1, source_target_pairs={{0,4},{4,0},{1,5},{5,1},{2,6},{6,2},{3,7},{7,3},{8,12},{12,8},{9,1... | collective-permute-start | bytes 3145736 | tf_op jit(solution)/shard_map/ppermute | solution.py:647
